TPU v7x, 32 devices: a whole 2x2x4 slice. The times are simulated.
32 devices in a mesh: seq: 8 (over y, x, core), tp: 4 (over z).
Axes of the slice: x: 2, y: 2, z: 4, core: 2. Of those that a mesh axis runs over, the one named last changes fastest.
Arguments:
- tokens: float32 [8192, 1536], P(('seq', 'tp')), may hold values from -6 to 6
- inner_proj: bfloat16 [2, 1536, 2, 3072], P(None, 'seq', None, 'tp'), may hold values from -0.15625 to 0.15625
- step_proj: bfloat16 [2, 1536, 48], P(None, 'seq', 'tp'), may hold values from -0.15625 to 0.15625
- state_proj: bfloat16 [2, 1536, 256], P(None, ('seq', 'tp')), may hold values from -0.15625 to 0.15625
- inner_conv: float32 [2, 4, 3072], P(None, None, 'tp'), may hold values from -0.5 to 0.5
- state_conv: bfloat16 [2, 4, 256], P(None, None, ('seq', 'tp')), may hold values from -0.5 to 0.5
- decay_log: float32 [2, 48], P(None, 'tp'), may hold values from -1 to 1.5
- step_bias: float32 [2, 48], P(None, 'tp'), may hold values from -9 to -2
- skip_gain: float32 [2, 48], P(None, 'tp'), may hold values from 0.5 to 1.5
- gate_gain: float32 [2, 3072], P(None, 'tp'), may hold values from 0.5 to 1.5
- outer_proj: bfloat16 [2, 3072, 1536], P(None, 'tp', 'seq'), may hold values from -0.109375 to 0.109375
- norm_gains: bfloat16 [2, 2, 1536], P(None, None, ('seq', 'tp')), may hold values from 0.5 to 1.5
- router: bfloat16 [2, 1536, 16], P(None, ('seq', 'tp')), may hold values from -0.078125 to 0.078125
- expert_up: bfloat16 [2, 16, 1536, 1024], P(None, 'tp', 'seq'), may hold values from -0.15625 to 0.15625
- expert_down: bfloat16 [2, 16, 512, 1536], P(None, 'tp', 'seq'), may hold values from -0.75 to 0.75
- shared_up: bfloat16 [2, 1536, 2048], P(None, ('seq', 'tp')), may hold values from -0.15625 to 0.15625
- shared_down: bfloat16 [2, 1024, 1536], P(None, ('seq', 'tp')), may hold values from -0.25 to 0.25
- routes: int32 [2, 8192, 6], P(None, ('seq', 'tp')), may hold values from 0 to 15, all different within a row; in each aligned block of 256 rows (0 to 255, 256 to 511, ..., all dimensions but the last counted through in order) at most 120 rows name the same one
- packed_lengths: int32 [4], replicated, may hold values from 1 to 4096, 8192 in all
- cotangent: float32 [8192, 1536], P(('seq', 'tp')), may hold values from -6 to 6
Outputs:
- layer_output: float32 [8192, 1536], P(('seq', 'tp'))
- tokens_grad: float32 [8192, 1536], P(('seq', 'tp'))
- inner_proj_grad: float32 [2, 1536, 2, 3072], P(None, 'seq', None, 'tp')
- step_proj_grad: float32 [2, 1536, 48], P(None, 'seq', 'tp')
- state_proj_grad: float32 [2, 1536, 256], P(None, ('seq', 'tp'))
- inner_conv_grad: float32 [2, 4, 3072], P(None, None, 'tp')
- state_conv_grad: float32 [2, 4, 256], P(None, None, ('seq', 'tp'))
- decay_log_grad: float32 [2, 48], P(None, 'tp')
- step_bias_grad: float32 [2, 48], P(None, 'tp')
- skip_gain_grad: float32 [2, 48], P(None, 'tp')
- gate_gain_grad: float32 [2, 3072], P(None, 'tp')
- outer_proj_grad: float32 [2, 3072, 1536], P(None, 'tp', 'seq')
- norm_gains_grad: float32 [2, 2, 1536], P(None, None, ('seq', 'tp'))
- router_grad: float32 [2, 1536, 16], P(None, ('seq', 'tp'))
- expert_up_grad: float32 [2, 16, 1536, 1024], P(None, 'tp', 'seq')
- expert_down_grad: float32 [2, 16, 512, 1536], P(None, 'tp', 'seq')
- shared_up_grad: float32 [2, 1536, 2048], P(None, ('seq', 'tp'))
- shared_down_grad: float32 [2, 1024, 1536], P(None, ('seq', 'tp'))
Inputs may be any that keep to these rules, and one draw needn't show every extreme that they name: `routes`: each row names 6 different experts. Within the 256 rows of one device, no expert is named by more than 120 rows, and in some device's rows one expert is named by exactly 120. `packed_lengths`: the lengths sum to 8192; the longest is exactly 4096.
All inputs are finite; a program needn't handle non-finite values.
Results may differ from a plain program's by a relative error of at most 0.02175.
Values may be sent and summed in bfloat16 or wider, within the bound.
No kernel may reach another device: no remote copies, remote signals or barrier semaphores. Data moves between devices by JAX's collectives and lax.ppermute only.
A program may use at most 512 MiB of HBM per device.

v0:
```python
from functools import partial

import jax
import jax.numpy as jnp
from jax import lax
from jax.sharding import PartitionSpec as P

D = 1536
HEAD_DIM = 64
STATE = 128
INNER = 3072
CONV_WIDTH = 4
TOP = 6
EXP_DEV = 4
LAYERS = 2
BLOCK_LEN = 256


epsilon = 1e-05
highest = lax.Precision.HIGHEST


def from_behind(value, axis, steps):
    count = lax.axis_size(axis)
    initial, last = (max(0, -steps), min(count, count - steps))
    return lax.ppermute(value, axis, [(source, source + steps) for source in range(initial, last)])


def carried_in(shard, axis, combine, identity):
    peers, position = (lax.axis_size(axis), lax.axis_index(axis))
    everything = jax.tree.map(
        lambda part, kind: lax.all_gather(part.astype(kind), axis),
        shard,
        (jnp.bfloat16, jnp.bfloat16),
    )
    start = jax.tree.map(
        lambda part, zero: jnp.broadcast_to(jnp.asarray(zero, part.dtype), part.shape),
        shard,
        identity,
    )

    def carried_turn(k, before):
        reached = k < position
        new = combine(
            before, jax.tree.map(lambda part, own: part[k].astype(own.dtype), everything, shard)
        )
        return jax.tree.map(lambda a, b: jnp.where(reached, a, b), new, before)

    return lax.fori_loop(0, peers, carried_turn, start)


def prefix(shard, axis, combine, identity):
    peers, position = (lax.axis_size(axis), lax.axis_index(axis))
    everything = jax.tree.map(
        lambda part, kind: lax.all_gather(part.astype(kind), axis),
        shard,
        jax.tree.map(lambda a: jnp.bfloat16 if a.dtype == jnp.float32 else a.dtype, shard),
    )
    start = jax.tree.map(
        lambda part, zero: jnp.broadcast_to(jnp.asarray(zero, part.dtype), part.shape),
        shard,
        identity,
    )

    def prefix_turn(k, before):
        at = peers - 1 - k
        reached = at > position
        new = combine(
            before, jax.tree.map(lambda part, own: part[at].astype(own.dtype), everything, shard)
        )
        return jax.tree.map(lambda a, b: jnp.where(reached, a, b), new, before)

    return lax.fori_loop(0, peers, prefix_turn, start)


def rms_norm(values, weight):
    return values * lax.rsqrt(jnp.mean(values * values, axis=-1, keepdims=True) + epsilon) * weight


def swiglu(hidden):
    half_width = hidden.shape[-1] // 2
    return jax.nn.silu(hidden[..., :half_width]) * hidden[..., half_width:]


def boundaries(packed_lengths, first_row, row_count, margin):
    seq_ends = jnp.cumsum(packed_lengths, dtype=jnp.int32)
    seq_starts = seq_ends - packed_lengths
    positions = first_row + jnp.arange(-margin, row_count, dtype=jnp.int32)
    return jnp.any(positions[:, None] == seq_starts[None, :], axis=1).astype(jnp.float32)


def conv_masks(starts_here, row_count, margin):
    stay_mask = 1.0 - starts_here
    running = jnp.ones((row_count,), jnp.float32)
    lag_list = [running]
    for offset in range(1, margin + 1):
        running = running * stay_mask[margin - offset + 1 : margin - offset + 1 + row_count]
        lag_list.append(running)
    return jnp.stack(lag_list, 0)


def causal_conv(padded, conv_taps, lag_masks):
    row_count = lag_masks.shape[1]
    margin = padded.shape[0] - row_count
    summed = conv_taps[0] * padded[margin:]
    for offset in range(1, conv_taps.shape[0]):
        summed = (
            summed
            + conv_taps[offset]
            * padded[margin - offset : margin - offset + row_count]
            * lag_masks[offset][:, None]
        )
    return summed


def to_blocks(values, blocks):
    return values.reshape((blocks, values.shape[0] // blocks) + values.shape[1:])


def block_step(carry_state, block_data):
    inputs, key_rows, queries, log_rates, step_sizes, resets = block_data
    log_sums = jnp.cumsum(log_rates, axis=0)
    segment = jnp.cumsum(resets)
    order_ids = jnp.arange(log_rates.shape[0])
    same_run = (segment[:, None] == segment[None, :]) & (order_ids[None, :] <= order_ids[:, None])
    log_gap = log_sums[:, None, :] - log_sums[None, :, :]
    decay_table = jnp.where(
        same_run[:, :, None], jnp.exp(jnp.where(same_run[:, :, None], log_gap, 0.0)), 0.0
    )
    scores = jnp.dot(queries, key_rows.T, precision=highest)
    weights = decay_table * scores[:, :, None] * step_sizes[None, :, :]
    within = jnp.einsum("tsh,shp->thp", weights, inputs, precision=highest)
    entry_decay = jnp.exp(log_sums) * (segment == 0)[:, None]
    carried = (
        jnp.einsum("tn,hpn->thp", queries, carry_state, precision=highest) * entry_decay[:, :, None]
    )
    tail_decay = (
        jnp.exp(log_sums[-1][None, :] - log_sums) * (segment == segment[-1])[:, None] * step_sizes
    )
    through = jnp.exp(log_sums[-1]) * (segment[-1] == 0)
    new_state = through[:, None, None] * carry_state + jnp.einsum(
        "sh,shp,sn->hpn", tail_decay, inputs, key_rows, precision=highest
    )
    return (new_state, within + carried)


def block_scan(heads_in, key_rows, queries, log_rates, step_sizes, resets):
    blocks = heads_in.shape[0] // BLOCK_LEN
    start_state = jnp.zeros((heads_in.shape[1], HEAD_DIM, STATE), jnp.float32)
    final_state, outputs = lax.scan(
        jax.checkpoint(block_step),
        start_state,
        (
            to_blocks(heads_in, blocks),
            to_blocks(key_rows, blocks),
            to_blocks(queries, blocks),
            to_blocks(log_rates, blocks),
            to_blocks(step_sizes, blocks),
            to_blocks(resets, blocks),
        ),
    )
    return (final_state, outputs.reshape(heads_in.shape))


def mixer_inputs(
    conv_in, bc_proj, edge_x, edge_bc, step_raw, x_taps, bc_taps, decay_log, step_bias, lag_masks
):
    conv_out = jax.nn.silu(causal_conv(jnp.concatenate([edge_x, conv_in], 0), x_taps, lag_masks))
    bc_out = jax.nn.silu(causal_conv(jnp.concatenate([edge_bc, bc_proj], 0), bc_taps, lag_masks))
    step_sizes = jax.nn.softplus(step_raw + step_bias)
    log_rates = -jnp.exp(decay_log) * step_sizes
    heads_in = conv_out.reshape(conv_in.shape[0], -1, HEAD_DIM)
    return (heads_in, bc_out[:, :STATE], bc_out[:, STATE:], log_rates, step_sizes)


def mixer_core(
    conv_in,
    bc_proj,
    edge_rows,
    step_raw,
    x_taps,
    bc_taps,
    decay_log,
    step_bias,
    skip_gain,
    resets,
    lag_masks,
):
    local_inner = conv_in.shape[1]
    heads_in, key_rows, queries, log_rates, step_sizes = mixer_inputs(
        conv_in,
        bc_proj,
        edge_rows[:, :local_inner],
        edge_rows[:, local_inner:],
        step_raw,
        x_taps,
        bc_taps,
        decay_log,
        step_bias,
        lag_masks,
    )
    local_state, outputs = block_scan(heads_in, key_rows, queries, log_rates, step_sizes, resets)
    scanned = outputs + skip_gain[None, :, None] * heads_in
    log_sums = jnp.cumsum(log_rates, axis=0)
    alive = (jnp.cumsum(resets) == 0).astype(jnp.float32)
    entry_decay = jnp.exp(log_sums) * alive[:, None]
    through = jnp.exp(log_sums[-1]) * alive[-1]
    return (scanned, through, local_state, queries, entry_decay)


def readout(queries, entry_decay, state_in):
    return jnp.einsum("tn,hpn->thp", queries, state_in, precision=highest) * entry_decay[:, :, None]


def chain_join(earlier, later):
    return (earlier[0] * later[0], later[0][:, None, None] * earlier[1] + later[1])


def slot_tables(expert_ids, capacity, experts):
    flat_ids = expert_ids.reshape(-1)
    onehot = (flat_ids[:, None] == jnp.arange(experts, dtype=jnp.int32)[None, :]).astype(jnp.int32)
    before = jnp.cumsum(onehot, axis=0, dtype=jnp.int32) - onehot
    position = jnp.sum(before * onehot, axis=1)
    slot_ids = flat_ids * capacity + position
    owners = (
        jnp.full((experts * capacity,), flat_ids.shape[0], jnp.int32)
        .at[slot_ids]
        .set(jnp.arange(flat_ids.shape[0], dtype=jnp.int32))
    )
    return (slot_ids, owners)


def owned_weights(inner_proj, step_proj, outer_proj, expert_up, expert_down, layer_index):
    return (
        lax.all_gather(inner_proj[layer_index], "seq", axis=0, tiled=True),
        lax.all_gather(step_proj[layer_index], "seq", axis=0, tiled=True),
        lax.all_gather(outer_proj[layer_index], "seq", axis=1, tiled=True),
        lax.all_gather(expert_up[layer_index], "seq", axis=1, tiled=True),
        lax.all_gather(expert_down[layer_index], "seq", axis=1, tiled=True),
    )


def common_weights(state_proj, state_conv, norm_gains, router, shared_up, shared_down, layer_index):
    return (
        lax.all_gather(state_proj[layer_index], ("seq", "tp"), axis=0, tiled=True),
        lax.all_gather(state_conv[layer_index], ("seq", "tp"), axis=1, tiled=True),
        lax.all_gather(norm_gains[layer_index], ("seq", "tp"), axis=1, tiled=True),
        lax.all_gather(router[layer_index], ("seq", "tp"), axis=0, tiled=True),
        lax.all_gather(shared_up[layer_index], ("seq", "tp"), axis=0, tiled=True),
        lax.all_gather(shared_down[layer_index], ("seq", "tp"), axis=0, tiled=True),
    )


def row_gather(values):
    return lax.all_gather(values, "tp", axis=0, tiled=True)


def row_sums(term, own_rows):
    return lax.psum_scatter(
        term(jnp.int32(0), own_rows * lax.axis_size("tp")), "tp", scatter_dimension=0, tiled=True
    )


def tensor_total(values):
    return lax.psum(values, "tp")


def to_owners(buffer):
    return lax.all_to_all(buffer, "tp", split_axis=0, concat_axis=0, tiled=True)


def from_owners(buffer):
    return lax.all_to_all(buffer, "tp", split_axis=0, concat_axis=0, tiled=True)


def gate_product(mix_val, gate_val):
    return mix_val * jax.nn.silu(gate_val)


def local(
    tokens,
    inner_proj,
    step_proj,
    state_proj,
    inner_conv,
    state_conv,
    decay_log,
    step_bias,
    skip_gain,
    gate_gain,
    outer_proj,
    norm_gains,
    router,
    expert_up,
    expert_down,
    shared_up,
    shared_down,
    routes,
    packed_lengths,
    cotangent,
):
    tensor_size = lax.axis_size("tp")
    own_rows = tokens.shape[0]
    local_rows = own_rows * tensor_size
    margin = CONV_WIDTH - 1
    starts_here = boundaries(packed_lengths, lax.axis_index("seq") * local_rows, local_rows, margin)
    resets = starts_here[margin:]
    lag_masks = conv_masks(starts_here, local_rows, margin)
    experts = EXP_DEV * tensor_size
    capacity = own_rows * TOP * 5 // (4 * experts)
    local_inner = gate_gain.shape[1]
    core = partial(mixer_core, resets=resets, lag_masks=lag_masks)
    residual = tokens
    saved = []
    for layer_index in range(LAYERS):
        owned = owned_weights(
            inner_proj, step_proj, outer_proj, expert_up, expert_down, layer_index
        )
        common = common_weights(
            state_proj, state_conv, norm_gains, router, shared_up, shared_down, layer_index
        )
        zx_weight, dt_weight, out_weight, up_weight, down_weight = owned
        bc_weight, bc_taps, gain_pair, router_weight, shared_in, shared_back = common
        gain_first = gain_pair[0].astype(jnp.float32)
        normed = row_gather(rms_norm(residual, gain_first).astype(jnp.bfloat16))
        zx_proj = jnp.dot(
            normed, zx_weight.reshape(D, 2 * local_inner), preferred_element_type=jnp.float32
        )
        step_raw = jnp.dot(normed, dt_weight, preferred_element_type=jnp.float32)
        bc_proj = jnp.dot(normed, bc_weight, preferred_element_type=jnp.float32)
        gate_in = zx_proj[:, :local_inner]
        conv_in = zx_proj[:, local_inner:]
        edge_rows = from_behind(
            jnp.concatenate([conv_in[local_rows - margin :], bc_proj[local_rows - margin :]], 1),
            "seq",
            1,
        )
        core_args = (
            conv_in,
            bc_proj,
            edge_rows,
            step_raw,
            inner_conv[layer_index],
            bc_taps.astype(jnp.float32),
            decay_log[layer_index],
            step_bias[layer_index],
            skip_gain[layer_index],
        )
        core_out, core_back = jax.vjp(core, *core_args)
        scanned, through, local_state, queries, entry_decay = core_out
        prior = carried_in(
            (through, local_state),
            "seq",
            chain_join,
            (jnp.ones_like(through), jnp.zeros_like(local_state)),
        )
        state_in = prior[1]
        mixed_flat = (scanned + readout(queries, entry_decay, state_in)).reshape(
            local_rows, local_inner
        )
        gated_out = gate_product(mixed_flat, gate_in)
        inverse = lax.rsqrt(tensor_total(jnp.sum(gated_out * gated_out, axis=1)) / INNER + epsilon)
        normed_gate = (gated_out * inverse[:, None] * gate_gain[layer_index]).astype(jnp.bfloat16)

        def out_term(start, row_count):
            return jnp.dot(normed_gate, out_weight, preferred_element_type=jnp.float32)

        residual_mid = residual + row_sums(out_term, own_rows)
        gain_second = gain_pair[1].astype(jnp.float32)
        moe_in = rms_norm(residual_mid, gain_second).astype(jnp.bfloat16)
        logits = jnp.dot(moe_in, router_weight, preferred_element_type=jnp.float32)
        expert_ids = routes[layer_index]
        gate_weights = jax.nn.softmax(jnp.take_along_axis(logits, expert_ids, axis=1), axis=1)
        slot_ids, owners = slot_tables(expert_ids, capacity, experts)
        padded = jnp.concatenate([moe_in, jnp.zeros((1, D), jnp.bfloat16)], 0)
        arrived = to_owners(padded[owners // TOP].reshape(tensor_size, EXP_DEV, capacity, D))
        hidden = jnp.einsum(
            "secd,edf->secf", arrived, up_weight, preferred_element_type=jnp.float32
        )
        activated = swiglu(hidden).astype(jnp.bfloat16)
        produced = jnp.einsum(
            "secf,efd->secd", activated, down_weight, preferred_element_type=jnp.float32
        ).astype(jnp.bfloat16)
        returned = from_owners(produced).reshape(experts * capacity, D)
        picked = returned[slot_ids].astype(jnp.float32).reshape(own_rows, TOP, D)
        routed = jnp.sum(gate_weights[:, :, None] * picked, axis=1)
        shared_hidden = jnp.dot(moe_in, shared_in, preferred_element_type=jnp.float32)
        shared_act = swiglu(shared_hidden).astype(jnp.bfloat16)
        shared_out = jnp.dot(shared_act, shared_back, preferred_element_type=jnp.float32)
        saved.append(
            {
                "owned": owned,
                "common": common,
                "residual": residual,
                "residual_mid": residual_mid,
                "normed": normed,
                "gate_in": gate_in,
                "core_back": core_back,
                "scanned": scanned,
                "through": through,
                "queries": queries,
                "entry_decay": entry_decay,
                "state_in": state_in,
                "mixed_flat": mixed_flat,
                "gated_out": gated_out,
                "inverse": inverse,
                "normed_gate": normed_gate,
                "moe_in": moe_in,
                "expert_ids": expert_ids,
                "gate_weights": gate_weights,
                "slot_ids": slot_ids,
                "owners": owners,
                "arrived": arrived,
                "hidden": hidden,
                "activated": activated,
                "picked": picked,
                "shared_hidden": shared_hidden,
                "shared_act": shared_act,
            }
        )
        residual = residual_mid + routed + shared_out
    grad_residual = cotangent
    owned_list = [None] * LAYERS
    common_list = [None] * LAYERS
    taps_list = [None] * LAYERS
    decay_list = [None] * LAYERS
    bias_list = [None] * LAYERS
    skip_list = [None] * LAYERS
    gain_list = [None] * LAYERS
    for layer_index in reversed(range(LAYERS)):
        kept_layer = saved[layer_index]
        owned = owned_weights(
            inner_proj, step_proj, outer_proj, expert_up, expert_down, layer_index
        )
        common = common_weights(
            state_proj, state_conv, norm_gains, router, shared_up, shared_down, layer_index
        )
        zx_weight, dt_weight, out_weight, up_weight, down_weight = owned
        bc_weight, bc_taps, gain_pair, router_weight, shared_in, shared_back = common
        moe_in = kept_layer["moe_in"]
        gate_weights = kept_layer["gate_weights"]
        slot_ids = kept_layer["slot_ids"]
        d_shared = grad_residual.astype(jnp.bfloat16)
        shared_back_grad = jnp.einsum(
            "rf,rd->fd", kept_layer["shared_act"], d_shared, preferred_element_type=jnp.float32
        )
        d_shared_act = jnp.einsum(
            "rd,fd->rf", d_shared, shared_back, preferred_element_type=jnp.float32
        )
        d_shared_hidden = jax.vjp(swiglu, kept_layer["shared_hidden"])[1](d_shared_act)[0].astype(
            jnp.bfloat16
        )
        shared_in_grad = jnp.einsum(
            "rd,rf->df", moe_in, d_shared_hidden, preferred_element_type=jnp.float32
        )
        d_moe_in = jnp.einsum(
            "rf,df->rd", d_shared_hidden, shared_in, preferred_element_type=jnp.float32
        )
        d_picked = (
            (gate_weights[:, :, None] * grad_residual[:, None, :])
            .astype(jnp.bfloat16)
            .reshape(own_rows * TOP, D)
        )
        d_gates = jnp.sum(kept_layer["picked"] * grad_residual[:, None, :], axis=2)
        d_padded = jnp.concatenate([d_picked, jnp.zeros((1, D), jnp.bfloat16)], 0)
        d_produced = to_owners(
            d_padded[kept_layer["owners"]].reshape(tensor_size, EXP_DEV, capacity, D)
        )
        down_grad = jnp.einsum(
            "secf,secd->efd",
            kept_layer["activated"],
            d_produced,
            preferred_element_type=jnp.float32,
        )
        d_activated = jnp.einsum(
            "secd,efd->secf", d_produced, down_weight, preferred_element_type=jnp.float32
        )
        d_hidden = jax.vjp(swiglu, kept_layer["hidden"])[1](d_activated)[0].astype(jnp.bfloat16)
        up_grad = jnp.einsum(
            "secd,secf->edf", kept_layer["arrived"], d_hidden, preferred_element_type=jnp.float32
        )
        d_arrived = jnp.einsum(
            "secf,edf->secd", d_hidden, up_weight, preferred_element_type=jnp.float32
        ).astype(jnp.bfloat16)
        d_returned = from_owners(d_arrived).reshape(experts * capacity, D)
        d_moe_in = d_moe_in + jnp.sum(
            d_returned[slot_ids].astype(jnp.float32).reshape(own_rows, TOP, D), axis=1
        )
        d_chosen = gate_weights * (d_gates - jnp.sum(gate_weights * d_gates, axis=1, keepdims=True))
        onehot = (
            kept_layer["expert_ids"][:, :, None]
            == jnp.arange(experts, dtype=jnp.int32)[None, None, :]
        ).astype(jnp.float32)
        d_logits = jnp.sum(d_chosen[:, :, None] * onehot, axis=1)
        moe_wide = moe_in.astype(jnp.float32)
        router_grad_layer = jnp.einsum("rd,re->de", moe_wide, d_logits, precision=highest)
        d_moe_in = d_moe_in + jnp.einsum(
            "re,de->rd", d_logits, router_weight.astype(jnp.float32), precision=highest
        )
        gain_second = gain_pair[1].astype(jnp.float32)
        d_mid, gain_second_grad = jax.vjp(rms_norm, kept_layer["residual_mid"], gain_second)[1](
            d_moe_in
        )
        grad_mid = grad_residual + d_mid
        d_mixer = row_gather(grad_mid.astype(jnp.bfloat16))
        normed_gate = kept_layer["normed_gate"]
        gated_out = kept_layer["gated_out"]
        inverse = kept_layer["inverse"]
        out_grad = jnp.einsum("tk,td->kd", normed_gate, d_mixer, preferred_element_type=jnp.float32)
        d_normed_gate = jnp.einsum(
            "td,kd->tk", d_mixer, out_weight, preferred_element_type=jnp.float32
        )
        weighted = d_normed_gate * gate_gain[layer_index]
        gate_gain_grad_layer = jnp.sum(d_normed_gate * gated_out * inverse[:, None], axis=0)
        cross_sum = tensor_total(jnp.sum(weighted * gated_out, axis=1))
        inverse_cube = inverse * inverse * inverse
        d_gated = (
            weighted * inverse[:, None] - gated_out * (inverse_cube * cross_sum / INNER)[:, None]
        )
        d_mixed, d_gate_in = jax.vjp(gate_product, kept_layer["mixed_flat"], kept_layer["gate_in"])[
            1
        ](d_gated)
        d_mix_heads = d_mixed.reshape(kept_layer["scanned"].shape)
        state_in = kept_layer["state_in"]
        through = kept_layer["through"]
        d_queries, d_entry, local_term = jax.vjp(
            readout, kept_layer["queries"], kept_layer["entry_decay"], state_in
        )[1](d_mix_heads)
        after = prefix(
            (through, local_term),
            "seq",
            chain_join,
            (jnp.ones_like(through), jnp.zeros_like(local_term)),
        )
        state_grad = after[1]
        d_through = jnp.sum(state_grad * state_in, axis=(1, 2))
        core_grads = kept_layer["core_back"](
            (d_mix_heads, d_through, state_grad, d_queries, d_entry)
        )
        (
            d_conv_in,
            d_bc_proj,
            d_edge_rows,
            d_step_raw,
            taps_grad,
            bc_taps_grad,
            decay_grad,
            bias_grad,
            skip_grad,
        ) = core_grads
        back_rows = from_behind(d_edge_rows, "seq", -1)
        d_conv_in = d_conv_in.at[local_rows - margin :].add(back_rows[:, :local_inner])
        d_bc_proj = d_bc_proj.at[local_rows - margin :].add(back_rows[:, local_inner:])
        normed = kept_layer["normed"]
        d_zx = jnp.concatenate([d_gate_in, d_conv_in], 1).astype(jnp.bfloat16)
        d_step = d_step_raw.astype(jnp.bfloat16)
        zx_grad = jnp.einsum("td,tk->dk", normed, d_zx, preferred_element_type=jnp.float32).reshape(
            D, 2, local_inner
        )
        dt_grad = jnp.einsum("td,th->dh", normed, d_step, preferred_element_type=jnp.float32)
        bc_grad = jnp.einsum("td,tc->dc", normed.astype(jnp.float32), d_bc_proj, precision=highest)
        zx_flat = zx_weight.reshape(D, 2 * local_inner)
        bc_wide = bc_weight.astype(jnp.float32)

        def in_term(start, row_count):
            summed = jnp.einsum("tk,dk->td", d_zx, zx_flat, preferred_element_type=jnp.float32)
            summed = summed + jnp.einsum(
                "th,dh->td", d_step, dt_weight, preferred_element_type=jnp.float32
            )
            return summed + jnp.einsum("tc,dc->td", d_bc_proj, bc_wide, precision=highest)

        d_own_normed = row_sums(in_term, own_rows)
        gain_first = gain_pair[0].astype(jnp.float32)
        d_first, gain_first_grad = jax.vjp(rms_norm, kept_layer["residual"], gain_first)[1](
            d_own_normed
        )
        grad_residual = grad_mid + d_first
        owned_list[layer_index] = (
            lax.psum_scatter(
                zx_grad.astype(jnp.bfloat16), "seq", scatter_dimension=0, tiled=True
            ).astype(jnp.float32),
            lax.psum_scatter(
                dt_grad.astype(jnp.bfloat16), "seq", scatter_dimension=0, tiled=True
            ).astype(jnp.float32),
            lax.psum_scatter(
                out_grad.astype(jnp.bfloat16), "seq", scatter_dimension=1, tiled=True
            ).astype(jnp.float32),
            lax.psum_scatter(
                up_grad.astype(jnp.bfloat16), "seq", scatter_dimension=1, tiled=True
            ).astype(jnp.float32),
            lax.psum_scatter(
                down_grad.astype(jnp.bfloat16), "seq", scatter_dimension=1, tiled=True
            ).astype(jnp.float32),
        )
        common_list[layer_index] = (
            lax.psum_scatter(bc_grad, ("seq", "tp"), scatter_dimension=0, tiled=True),
            lax.psum_scatter(bc_taps_grad, ("seq", "tp"), scatter_dimension=1, tiled=True),
            lax.psum_scatter(
                jnp.stack([gain_first_grad, gain_second_grad], 0),
                ("seq", "tp"),
                scatter_dimension=1,
                tiled=True,
            ),
            lax.psum_scatter(router_grad_layer, ("seq", "tp"), scatter_dimension=0, tiled=True),
            lax.psum_scatter(shared_in_grad, ("seq", "tp"), scatter_dimension=0, tiled=True),
            lax.psum_scatter(shared_back_grad, ("seq", "tp"), scatter_dimension=0, tiled=True),
        )
        taps_list[layer_index] = taps_grad
        decay_list[layer_index] = decay_grad
        bias_list[layer_index] = bias_grad
        skip_list[layer_index] = skip_grad
        gain_list[layer_index] = gate_gain_grad_layer
    small_sums = lax.psum(
        (
            jnp.stack(taps_list, 0),
            jnp.stack(decay_list, 0),
            jnp.stack(bias_list, 0),
            jnp.stack(skip_list, 0),
            jnp.stack(gain_list, 0),
        ),
        "seq",
    )
    inner_proj_grad = jnp.stack([owned_list[index_layer][0] for index_layer in range(LAYERS)], 0)
    step_proj_grad = jnp.stack([owned_list[index_layer][1] for index_layer in range(LAYERS)], 0)
    outer_proj_grad = jnp.stack([owned_list[index_layer][2] for index_layer in range(LAYERS)], 0)
    expert_up_grad = jnp.stack([owned_list[index_layer][3] for index_layer in range(LAYERS)], 0)
    expert_down_grad = jnp.stack([owned_list[index_layer][4] for index_layer in range(LAYERS)], 0)
    state_proj_grad = jnp.stack([common_list[index_layer][0] for index_layer in range(LAYERS)], 0)
    state_conv_grad = jnp.stack([common_list[index_layer][1] for index_layer in range(LAYERS)], 0)
    norm_gains_grad = jnp.stack([common_list[index_layer][2] for index_layer in range(LAYERS)], 0)
    router_grad = jnp.stack([common_list[index_layer][3] for index_layer in range(LAYERS)], 0)
    shared_up_grad = jnp.stack([common_list[index_layer][4] for index_layer in range(LAYERS)], 0)
    shared_down_grad = jnp.stack([common_list[index_layer][5] for index_layer in range(LAYERS)], 0)
    return (
        residual,
        grad_residual,
        inner_proj_grad,
        step_proj_grad,
        state_proj_grad,
        small_sums[0],
        state_conv_grad,
        small_sums[1],
        small_sums[2],
        small_sums[3],
        small_sums[4],
        outer_proj_grad,
        norm_gains_grad,
        router_grad,
        expert_up_grad,
        expert_down_grad,
        shared_up_grad,
        shared_down_grad,
    )


def solution(mesh):
    in_specs = (
        P(("seq", "tp"), None),
        P(None, "seq", None, "tp"),
        P(None, "seq", "tp"),
        P(None, ("seq", "tp"), None),
        P(None, None, "tp"),
        P(None, None, ("seq", "tp")),
        P(None, "tp"),
        P(None, "tp"),
        P(None, "tp"),
        P(None, "tp"),
        P(None, "tp", "seq"),
        P(None, None, ("seq", "tp")),
        P(None, ("seq", "tp"), None),
        P(None, "tp", "seq", None),
        P(None, "tp", "seq", None),
        P(None, ("seq", "tp"), None),
        P(None, ("seq", "tp"), None),
        P(None, ("seq", "tp"), None),
        P(),
        P(("seq", "tp"), None),
    )
    out_specs = (
        P(("seq", "tp"), None),
        P(("seq", "tp"), None),
        P(None, "seq", None, "tp"),
        P(None, "seq", "tp"),
        P(None, ("seq", "tp"), None),
        P(None, None, "tp"),
        P(None, None, ("seq", "tp")),
        P(None, "tp"),
        P(None, "tp"),
        P(None, "tp"),
        P(None, "tp"),
        P(None, "tp", "seq"),
        P(None, None, ("seq", "tp")),
        P(None, ("seq", "tp"), None),
        P(None, "tp", "seq", None),
        P(None, "tp", "seq", None),
        P(None, ("seq", "tp"), None),
        P(None, ("seq", "tp"), None),
    )
    return jax.shard_map(local, mesh=mesh, in_specs=in_specs, out_specs=out_specs, check_vma=False)
```

profile of v0, /device:TPU:0, one launch (start us, length us, event | category | flops | bytes accessed | tf_op | source)
XLA Modules:
  0.0 5516.5 jit_solution(12129843216474111727)
XLA Ops:
  8.7 76.1 %all-gather = bf16[1,2,1536]{1,0,2:T(2,128)(2,1)S(1)} all-gather(bf16[1,2,48]{1,0,2:T(2,128)(2,1)S(1)} %copy.676), channel_id=2, replica_groups=mesh['seq'=8,'tp'=4] {'seq','tp'}, dimensions={2}, use_global_device_ids=true | all-gather | bytes 6336 | tf_op jit(solution)/shard_map/all_gather | solution.py:247
  84.9 25.7 fusion.336
  115.8 66.5 %all-gather.4 = bf16[1,4,256]{1,0,2:T(2,128)(2,1)S(1)} all-gather(bf16[1,4,8]{1,0,2:T(2,128)(2,1)S(1)} %copy.679), channel_id=6, replica_groups=mesh['seq'=8,'tp'=4] {'seq','tp'}, dimensions={2}, use_global_device_ids=true | all-gather | bytes 2112 | tf_op jit(solution)/shard_map/all_gather | solution.py:246
  203.8 71.9 %all-gather.3 = bf16[1,1536,256]{2,1,0:T(8,128)(2,1)S(1)} all-gather(bf16[1,48,256]{2,1,0:T(8,128)(2,1)S(1)} %get-tuple-element.2309), channel_id=5, replica_groups=mesh['seq'=8,'tp'=4] {'seq','tp'}, dimensions={1}, use_global_device_ids=true | all-gather | bytes 811008 | tf_op jit(solution)/shard_map/all_gather | solution.py:245
  317.6 139.8 %while.148 = (s32[]{:T(128)}, f32[12,64,128]{2,1,0:T(8,128)S(1)}, f32[4,256,12,64]{1,0,3,2:T(4,128)}, f32[4,12,64,128]{3,2,1,0:T(8,128)}, f32[4,256,12]{1,2,0:T(...) while((s32[]{:T(128)}, f32[12,64,128]{2,1,0:T(8,128)S(1)}, ...), condition=%wide.region_8.10_spmd.clone, body=%wide.region_3.9_spmd.clone.sunk | while | flops 1314272256 | bytes 10584823 | solution.py:150
  331.2 17.9 dynamic_update_slice.153
  366.1 17.9 dynamic_update_slice.153
  401.0 17.9 dynamic_update_slice.153
  436.0 17.9 dynamic_update_slice.153
  559.1 87.2 %reduce-scatter.37.cloned.1.call-done = f32[256,1536]{1,0:T(8,128)} async-done(((f32[1024,1536]{1,0:T(8,128)}), f32[256,1536]{1,0:T(8,128)}) %reduce-scatter.37.cloned.1.call-update) | async-done | bytes 1572880 | tf_op jit(solution)/shard_map/reduce_scatter | solution.py:259
  662.9 58.4 %all-gather.63.cloned.1.call-done = bf16[1,4,1536,1024]{3,2,1,0:T(8,128)(2,1)} async-done(((bf16[1,4,192,1024]{3,2,1,0:T(8,128)(2,1)}), bf16[1,4,1536,1024]{3,2,1,0:T(8,128)(2,1)}) %all-gather.63.cloned.1.call-update) | async-done | bytes 12582928 | tf_op jit(solution)/shard_map/all_gather | solution.py:238
  721.2 75.4 %all-to-all-done = bf16[4,4,120,1536]{3,2,1,0:T(8,128)(2,1)} async-done(((bf16[4,4,120,1536]{3,2,1,0:T(8,128)(2,1)}), bf16[4,4,120,1536]{3,2,1,0:T(8,128)(2,1)}, u32[]{:S(2)}, u32[]{:S(2)}) %all-to-all-start) | async-done | bytes 5898272 | tf_op jit(solution)/shard_map/all_to_all | solution.py:269
  829.7 210.5 %all-gather.7 = bf16[1,1536,16]{2,0,1:T(2,128)(2,1)S(1)} all-gather(bf16[1,48,16]{2,0,1:T(2,128)(2,1)S(1)} %copy.681), channel_id=9, replica_groups=mesh['seq'=8,'tp'=4] {'seq','tp'}, dimensions={1}, use_global_device_ids=true | all-gather | bytes 50688 | tf_op jit(solution)/shard_map/all_gather | solution.py:248
  1040.9 70.6 %all-gather.12 = bf16[1,2,1536]{1,0,2:T(2,128)(2,1)S(1)} all-gather(bf16[1,2,48]{1,0,2:T(2,128)(2,1)S(1)} %copy.682), channel_id=14, replica_groups=mesh['seq'=8,'tp'=4] {'seq','tp'}, dimensions={2}, use_global_device_ids=true | all-gather | bytes 6336 | tf_op jit(solution)/shard_map/all_gather | solution.py:247
  1111.5 25.7 fusion.334
  1196.8 67.9 %all-gather.16 = bf16[1,4,256]{1,0,2:T(2,128)(2,1)S(1)} all-gather(bf16[1,4,8]{1,0,2:T(2,128)(2,1)S(1)} %copy.685), channel_id=18, replica_groups=mesh['seq'=8,'tp'=4] {'seq','tp'}, dimensions={2}, use_global_device_ids=true | all-gather | bytes 2112 | tf_op jit(solution)/shard_map/all_gather | solution.py:246
  1279.8 71.6 %all-gather.15 = bf16[1,1536,256]{2,1,0:T(8,128)(2,1)S(1)} all-gather(bf16[1,48,256]{2,1,0:T(8,128)(2,1)S(1)} %copy-done.182), channel_id=17, replica_groups=mesh['seq'=8,'tp'=4] {'seq','tp'}, dimensions={1}, use_global_device_ids=true | all-gather | bytes 811008 | tf_op jit(solution)/shard_map/all_gather | solution.py:245
  1403.4 135.0 %while.150 = (s32[]{:T(128)}, f32[12,64,128]{2,1,0:T(8,128)S(1)}, f32[4,256,12,64]{1,0,3,2:T(4,128)}, f32[4,12,64,128]{3,2,1,0:T(8,128)}, f32[4,256,12]{1,2,0:T(...) while((s32[]{:T(128)}, f32[12,64,128]{2,1,0:T(8,128)S(1)}, ...), condition=%wide.region_32.35_spmd.clone, body=%wide.region_27.34_spmd.clone.sunk | while | flops 1314272256 | bytes 10592971 | solution.py:150
  1415.8 17.9 dynamic_update_slice.155
  1449.5 17.9 dynamic_update_slice.155
  1483.2 17.9 dynamic_update_slice.155
  1517.0 17.9 dynamic_update_slice.155
  1619.1 95.2 %reduce-scatter.39.cloned.1.call-done = f32[256,1536]{1,0:T(8,128)} async-done(((f32[1024,1536]{1,0:T(8,128)}), f32[256,1536]{1,0:T(8,128)}) %reduce-scatter.39.cloned.1.call-update) | async-done | bytes 1572880 | tf_op jit(solution)/shard_map/reduce_scatter | solution.py:259
  1731.3 194.4 %all-gather.19 = bf16[1,1536,16]{2,0,1:T(2,128)(2,1)S(1)} all-gather(bf16[1,48,16]{2,0,1:T(2,128)(2,1)S(1)} %copy.687), channel_id=21, replica_groups=mesh['seq'=8,'tp'=4] {'seq','tp'}, dimensions={1}, use_global_device_ids=true | all-gather | bytes 50688 | tf_op jit(solution)/shard_map/all_gather | solution.py:248
  1964.6 16.2 gather_fusion.4
  2000.3 140.3 %all-to-all-done.4 = bf16[4,4,120,1536]{3,2,1,0:T(8,128)(2,1)} async-done(((bf16[4,4,120,1536]{3,2,1,0:T(8,128)(2,1)}), bf16[4,4,120,1536]{3,2,1,0:T(8,128)(2,1)}, u32[]{:S(2)}, u32[]{:S(2)}) %all-to-all-start.4) | async-done | bytes 5898272 | tf_op jit(solution)/shard_map/all_to_all | solution.py:269
  2140.6 14.9 bitcast_multiply_fusion.11
  2188.3 111.3 %all-to-all-done.3 = bf16[4,4,120,1536]{3,2,1,0:T(8,128)(2,1)} async-done(((bf16[4,4,120,1536]{3,2,1,0:T(8,128)(2,1)}), bf16[4,4,120,1536]{3,2,1,0:T(8,128)(2,1)}, u32[]{:S(2)}, u32[]{:S(2)}) %all-to-all-start.3) | async-done | bytes 5898272 | tf_op jit(solution)/shard_map/all_to_all | solution.py:273
  2311.8 121.8 %all-gather.83.cloned.1.call-done = bf16[1,1024,1536]{2,1,0:T(8,128)(2,1)} async-done(((bf16[1,32,1536]{2,1,0:T(8,128)(2,1)}), bf16[1,1024,1536]{2,1,0:T(8,128)(2,1)}) %all-gather.83.cloned.1.call-update) | async-done | bytes 3145744 | tf_op jit(solution)/shard_map/all_gather | solution.py:250
  2512.8 77.9 %all-gather.53.cloned.1.call-done = bf16[1024,1536]{1,0:T(8,128)(2,1)} async-done(((bf16[256,1536]{1,0:T(8,128)(2,1)}), bf16[1024,1536]{1,0:T(8,128)(2,1)}) %all-gather.53.cloned.1.call-update) | async-done | bytes 3145744 | tf_op jit(solution)/shard_map/all_gather | solution.py:255
  2631.0 17.6 all-gather.85.cloned.1.call-done
  2668.6 237.0 %while.146 = (s32[]{:T(128)}, f32[12,64,128]{2,1,0:T(8,128)S(1)}, f32[4,256,12,64]{1,0,3,2:T(4,128)}, f32[4,256,128]{2,1,0:T(8,128)}, f32[4,256,128]{2,1,0:T(8,1...) while((s32[]{:T(128)}, f32[12,64,128]{2,1,0:T(8,128)S(1)}, ...), condition=%wide.region_71.74_spmd, body=%wide.region_57.73_spmd.sunk | while | flops 3038862336 | bytes 31277412 | solution.py:150
  2703.6 17.9 dynamic_update_slice.144
  2762.7 17.9 dynamic_update_slice.144
  2821.8 17.9 dynamic_update_slice.144
  2880.9 17.9 dynamic_update_slice.144
  2933.9 15.1 reduce-window.283
  2976.7 111.8 %reduce-scatter.41.cloned.1.call-done = f32[256,1536]{1,0:T(8,128)} async-done(((f32[1024,1536]{1,0:T(8,128)}), f32[256,1536]{1,0:T(8,128)}) %reduce-scatter.41.cloned.1.call-update) | async-done | bytes 1572880 | tf_op jit(solution)/shard_map/reduce_scatter | solution.py:259
  3117.1 16.2 gather_fusion.6
  3133.3 137.7 %all_to_all.40 = bf16[4,4,120,1536]{3,2,1,0:T(8,128)(2,1)} all-to-all(bf16[4,4,120,1536]{3,2,1,0:T(8,128)(2,1)} %bitcast.1136), channel_id=1, replica_groups=mesh['seq'=8,'tp'=4] {'tp'}, dimensions={0} | all-to-all | bytes 11796480 | tf_op jit(solution)/shard_map/all_to_all | solution.py:269
  3319.8 117.9 %all-to-all-done.7 = bf16[4,4,120,1536]{3,2,1,0:T(8,128)(2,1)} async-done(((bf16[4,4,120,1536]{3,2,1,0:T(8,128)(2,1)}), bf16[4,4,120,1536]{3,2,1,0:T(8,128)(2,1)}, u32[]{:S(2)}, u32[]{:S(2)}) %all-to-all-start.7) | async-done | bytes 5898272 | tf_op jit(solution)/shard_map/all_to_all | solution.py:273
  3478.4 62.5 %all-gather.55.cloned.1.call-done = bf16[1024,1536]{1,0:T(8,128)(2,1)} async-done(((bf16[256,1536]{1,0:T(8,128)(2,1)}), bf16[1024,1536]{1,0:T(8,128)(2,1)}) %all-gather.55.cloned.1.call-update) | async-done | bytes 3145744 | tf_op jit(solution)/shard_map/all_gather | solution.py:255
  3657.2 237.2 %while.147 = (s32[]{:T(128)}, f32[12,64,128]{2,1,0:T(8,128)S(1)}, f32[4,256,12,64]{1,0,3,2:T(4,128)}, f32[4,256,128]{2,1,0:T(8,128)}, f32[4,256,128]{2,1,0:T(8,1...) while((s32[]{:T(128)}, f32[12,64,128]{2,1,0:T(8,128)S(1)}, ...), condition=%wide.region_101.104_spmd, body=%wide.region_87.103_spmd.sunk | while | flops 3038862336 | bytes 31277412 | solution.py:150
  3691.9 17.9 dynamic_update_slice.149
  3751.1 17.9 dynamic_update_slice.149
  3810.2 17.9 dynamic_update_slice.149
  3869.4 17.9 dynamic_update_slice.149
  3898.2 14.9 reduce-window.285
  3987.9 14.6 bitcast_convert_fusion.4
  4095.3 80.0 %reduce-scatter.65.cloned.1.call-done = f32[32,1536]{1,0:T(8,128)} async-done(((f32[1024,1536]{1,0:T(8,128)}), f32[32,1536]{1,0:T(8,128)}) %reduce-scatter.65.cloned.1.call-update) | async-done | bytes 196624 | tf_op jit(solution)/shard_map/reduce_scatter | solution.py:606
  4177.0 158.7 %reduce-scatter.63.cloned.1.call-done = f32[48,2048]{1,0:T(8,128)} async-done(((f32[1536,2048]{1,0:T(8,128)}), f32[48,2048]{1,0:T(8,128)}) %reduce-scatter.63.cloned.1.call-update) | async-done | bytes 393232 | tf_op jit(solution)/shard_map/reduce_scatter | solution.py:605
  4335.8 162.0 %reduce-scatter.61.cloned.1.call-done = f32[48,2048]{1,0:T(8,128)} async-done(((f32[1536,2048]{1,0:T(8,128)}), f32[48,2048]{1,0:T(8,128)}) %reduce-scatter.61.cloned.1.call-update) | async-done | bytes 393232 | tf_op jit(solution)/shard_map/reduce_scatter | solution.py:605
  4499.9 62.2 %reduce-scatter.59.cloned.1.call-done = bf16[4,64,1536]{2,1,0:T(8,128)(2,1)} async-done(((bf16[4,512,1536]{2,1,0:T(8,128)(2,1)}), bf16[4,64,1536]{2,1,0:T(8,128)(2,1)}) %reduce-scatter.59.cloned.1.call-update) | async-done | bytes 786448 | tf_op jit(solution)/shard_map/reduce_scatter | solution.py:591
  4562.0 65.4 %reduce-scatter.57.cloned.1.call-done = bf16[4,64,1536]{2,1,0:T(8,128)(2,1)} async-done(((bf16[4,512,1536]{2,1,0:T(8,128)(2,1)}), bf16[4,64,1536]{2,1,0:T(8,128)(2,1)}) %reduce-scatter.57.cloned.1.call-update) | async-done | bytes 786448 | tf_op jit(solution)/shard_map/reduce_scatter | solution.py:591
  4631.0 39.4 all-reduce.62
  4670.6 24.2 all-reduce.63
  4710.8 46.1 reduce-scatter.49.cloned.1.call-done
  4759.0 100.0 %reduce-scatter.47.cloned.1.call-done = f32[48,256]{1,0:T(8,128)} async-done(((f32[1536,256]{1,0:T(8,128)}), f32[48,256]{1,0:T(8,128)}) %reduce-scatter.47.cloned.1.call-update) | async-done | bytes 49168 | tf_op jit(solution)/shard_map/reduce_scatter | solution.py:596
  4859.0 101.3 %reduce-scatter.45.cloned.1.call-done = f32[48,256]{1,0:T(8,128)} async-done(((f32[1536,256]{1,0:T(8,128)}), f32[48,256]{1,0:T(8,128)}) %reduce-scatter.45.cloned.1.call-update) | async-done | bytes 49168 | tf_op jit(solution)/shard_map/reduce_scatter | solution.py:596
  4961.8 93.3 %reduce-scatter.55.cloned.1.call-done = bf16[4,192,1024]{2,1,0:T(8,128)(2,1)} async-done(((bf16[4,1536,1024]{2,1,0:T(8,128)(2,1)}), bf16[4,192,1024]{2,1,0:T(8,128)(2,1)}) %reduce-scatter.55.cloned.1.call-update) | async-done | bytes 1572880 | tf_op jit(solution)/shard_map/reduce_scatter | solution.py:588
  5055.1 95.9 %reduce-scatter.53.cloned.1.call-done = bf16[4,192,1024]{2,1,0:T(8,128)(2,1)} async-done(((bf16[4,1536,1024]{2,1,0:T(8,128)(2,1)}), bf16[4,192,1024]{2,1,0:T(8,128)(2,1)}) %reduce-scatter.53.cloned.1.call-update) | async-done | bytes 1572880 | tf_op jit(solution)/shard_map/reduce_scatter | solution.py:588
  5156.0 137.0 %all-reduce.67.cloned.1.call-done = (bf16[1536,2,768]{2,1,0:T(2,128)(2,1)}, bf16[1536,2,768]{2,1,0:T(2,128)(2,1)}) async-done(((bf16[1536,2,768]{2,1,0:T(2,128)(2,1)}, bf16[1536,2,768]{2,1,0:T(2,128)(2,1)}), (bf16[1536,2,768]{2,1,0:T(2,128)(2,1)}, bf16[1536,2,768]{2,1,0:T(2,128)(2,1)})) %all-reduce.67.cloned.1.call-update) | async-done | bytes 9437200
  5298.9 107.4 %reduce-scatter.43.cloned.1.call-done = f32[256,1536]{1,0:T(8,128)} async-done(((f32[1024,1536]{1,0:T(8,128)}), f32[256,1536]{1,0:T(8,128)}) %reduce-scatter.43.cloned.1.call-update) | async-done | bytes 1572880 | tf_op jit(solution)/shard_map/reduce_scatter | solution.py:259
  5412.3 95.8 %reduce-scatter.73.cloned.1.call-done = f32[48,2]{1,0:T(8,128)} async-done(((f32[1536,2]{1,0:T(8,128)}), f32[48,2]{1,0:T(8,128)}) %reduce-scatter.73.cloned.1.call-update) | async-done | bytes 400
  (2080 shorter events, 1684.3 us)
Async XLA Ops:
  7.2 268.6 %all-gather.49.cloned.1.call-start = ((), (), s32[]{:S(2)}) async-start(), calls=%async_computation.30 | async-start | bytes 3932160 | tf_op jit(solution)/shard_map/all_gather | solution.py:255
  113.0 166.9 %all-gather.57.cloned.1.call-start = ((), (), s32[]{:S(2)}) async-start(), calls=%async_computation.50 | async-start | bytes 5308416 | tf_op jit(solution)/shard_map/all_gather | solution.py:235
  114.9 378.7 %all-gather.59.cloned.1.call-start = ((), (), s32[]{:S(2)}) async-start(), calls=%async_computation.51 | async-start | bytes 1769472 | tf_op jit(solution)/shard_map/all_gather | solution.py:32
  288.4 6.5 collective-permute-start
  458.2 70.7 %all-gather.61.cloned.1.call-start = ((), (), s32[]{:S(2)}) async-start(), calls=%async_computation.52 | async-start | bytes 2654208 | tf_op jit(solution)/shard_map/all_gather | solution.py:237
  460.4 185.9 %reduce-scatter.37.cloned.1.call-start = ((), (), s32[]{:S(2)}) async-start(), calls=%async_computation.31 | async-start | bytes 7864320 | tf_op jit(solution)/shard_map/reduce_scatter | solution.py:259
  536.8 184.4 %all-gather.63.cloned.1.call-start = ((), (), s32[]{:S(2)}) async-start(), calls=%async_computation.53 | async-start | bytes 14155776 | tf_op jit(solution)/shard_map/all_gather | solution.py:238
  540.9 272.5 %all-gather.65.cloned.1.call-start = ((), (), s32[]{:S(2)}) async-start(), calls=%async_computation.54 | async-start | bytes 7077888 | tf_op jit(solution)/shard_map/all_gather | solution.py:239
  544.2 606.9 %all-gather.67.cloned.1.call-start = ((), (), s32[]{:S(2)}) async-start(), calls=%async_computation.55 | async-start | bytes 6488064 | tf_op jit(solution)/shard_map/all_gather | solution.py:249
  648.4 542.6 %copy-start.21 = (f32[256,1536]{1,0:T(8,128)}, f32[256,1536]{1,0:T(8,128)S(1)}, u32[]{:S(2)}) copy-start(f32[256,1536]{1,0:T(8,128)S(1)} %get-tuple-element.2219) | copy-start | bytes 4718596
  648.6 502.5 %copy-start.53 = (bf16[256,1536]{1,0:T(8,128)(2,1)}, bf16[256,1536]{1,0:T(8,128)(2,1)S(1)}, u32[]{:S(2)}) copy-start(bf16[256,1536]{1,0:T(8,128)(2,1)S(1)} %multiply_convert_fusion.8) | copy-start | bytes 2359300
  656.5 140.2 %all-to-all-start = ((bf16[4,4,120,1536]{3,2,1,0:T(8,128)(2,1)}), bf16[4,4,120,1536]{3,2,1,0:T(8,128)(2,1)}, u32[]{:S(2)}, u32[]{:S(2)}) async-start(bf16[4,4,120,1536]{3,2,1,0:T(8,128)(2,1)} %bitcast.1135), calls=%async_computation.1 | async-start | bytes 11796480 | tf_op jit(solution)/shard_map/all_to_all | solution.py:269
  662.1 528.8 %all-gather.69.cloned.1.call-start = ((), (), s32[]{:S(2)}) async-start(), calls=%async_computation.56 | async-start | bytes 3244032 | tf_op jit(solution)/shard_map/all_gather | solution.py:250
  823.0 217.7 %copy-start.289 = (bf16[1,2,48]{2,1,0:T(2,128)(2,1)S(1)}, bf16[1,2,48]{2,1,0:T(2,128)(2,1)}, u32[]{:S(2)}) copy-start(bf16[1,2,48]{2,1,0:T(2,128)(2,1)} %get-tuple-element.2335) | copy-start | bytes 580
  823.0 334.4 %all-to-all-start.1 = ((bf16[4,4,120,1536]{3,2,1,0:T(8,128)(2,1)}), bf16[4,4,120,1536]{3,2,1,0:T(8,128)(2,1)}, u32[]{:S(2)}, u32[]{:S(2)}) async-start(bf16[4,4,120,1536]{3,2,1,0:T(8,128)(2,1)} %copy.559), calls=%async_computation.2 | async-start | bytes 11796480 | tf_op jit(solution)/shard_map/all_to_all | solution.py:273
  828.4 523.0 %all-gather.71.cloned.1.call-start = ((), (), s32[]{:S(2)}) async-start(), calls=%async_computation.57 | async-start | bytes 5308416 | tf_op jit(solution)/shard_map/all_gather | solution.py:235
  829.0 528.2 %all-gather.51.cloned.1.call-start = ((), (), s32[]{:S(2)}) async-start(), calls=%async_computation.32 | async-start | bytes 3932160 | tf_op jit(solution)/shard_map/all_gather | solution.py:255
  1196.7 366.1 %all-gather.73.cloned.1.call-start = ((), (), s32[]{:S(2)}) async-start(), calls=%async_computation.58 | async-start | bytes 1769472 | tf_op jit(solution)/shard_map/all_gather | solution.py:32
  1367.8 10.0 collective-permute-start.1
  1539.1 58.9 %all-gather.75.cloned.1.call-start = ((), (), s32[]{:S(2)}) async-start(), calls=%async_computation.59 | async-start | bytes 2654208 | tf_op jit(solution)/shard_map/all_gather | solution.py:237
  1539.9 174.3 %reduce-scatter.39.cloned.1.call-start = ((), (), s32[]{:S(2)}) async-start(), calls=%async_computation.33 | async-start | bytes 7864320 | tf_op jit(solution)/shard_map/reduce_scatter | solution.py:259
  1606.1 380.5 %all-gather.77.cloned.1.call-start = ((), (), s32[]{:S(2)}) async-start(), calls=%async_computation.60 | async-start | bytes 14155776 | tf_op jit(solution)/shard_map/all_gather | solution.py:238
  1717.3 588.6 %copy-start.54 = (bf16[256,1536]{1,0:T(8,128)(2,1)}, bf16[256,1536]{1,0:T(8,128)(2,1)S(1)}, u32[]{:S(2)}) copy-start(bf16[256,1536]{1,0:T(8,128)(2,1)S(1)} %multiply_convert_fusion.6) | copy-start | bytes 2359300
  1725.1 255.6 %all-to-all-start.2 = ((bf16[4,4,120,1536]{3,2,1,0:T(8,128)(2,1)}), bf16[4,4,120,1536]{3,2,1,0:T(8,128)(2,1)}, u32[]{:S(2)}, u32[]{:S(2)}) async-start(bf16[4,4,120,1536]{3,2,1,0:T(8,128)(2,1)} %bitcast.1133), calls=%async_computation.4 | async-start | bytes 11796480 | tf_op jit(solution)/shard_map/all_to_all | solution.py:269
  1730.6 269.8 %all-gather.79.cloned.1.call-start = ((), (), s32[]{:S(2)}) async-start(), calls=%async_computation.61 | async-start | bytes 7077888 | tf_op jit(solution)/shard_map/all_gather | solution.py:239
  1980.8 159.9 %all-to-all-start.4 = ((bf16[4,4,120,1536]{3,2,1,0:T(8,128)(2,1)}), bf16[4,4,120,1536]{3,2,1,0:T(8,128)(2,1)}, u32[]{:S(2)}, u32[]{:S(2)}) async-start(bf16[4,4,120,1536]{3,2,1,0:T(8,128)(2,1)} %bitcast.1134), calls=%async_computation.6 | async-start | bytes 11796480 | tf_op jit(solution)/shard_map/all_to_all | solution.py:269
  1985.9 319.9 %all-gather.81.cloned.1.call-start = ((), (), s32[]{:S(2)}) async-start(), calls=%async_computation.62 | async-start | bytes 6488064 | tf_op jit(solution)/shard_map/all_gather | solution.py:249
  2165.3 134.4 %all-to-all-start.3 = ((bf16[4,4,120,1536]{3,2,1,0:T(8,128)(2,1)}), bf16[4,4,120,1536]{3,2,1,0:T(8,128)(2,1)}, u32[]{:S(2)}, u32[]{:S(2)}) async-start(bf16[4,4,120,1536]{3,2,1,0:T(8,128)(2,1)} %copy.584), calls=%async_computation.5 | async-start | bytes 11796480 | tf_op jit(solution)/shard_map/all_to_all | solution.py:273
  2299.6 172.5 %all-to-all-start.5 = ((bf16[4,4,120,1536]{3,2,1,0:T(8,128)(2,1)}), bf16[4,4,120,1536]{3,2,1,0:T(8,128)(2,1)}, u32[]{:S(2)}, u32[]{:S(2)}) async-start(bf16[4,4,120,1536]{3,2,1,0:T(8,128)(2,1)} %copy.586), calls=%async_computation.7 | async-start | bytes 11796480 | tf_op jit(solution)/shard_map/all_to_all | solution.py:273
  2304.8 128.7 %all-gather.83.cloned.1.call-start = ((), (), s32[]{:S(2)}) async-start(), calls=%async_computation.63 | async-start | bytes 3244032 | tf_op jit(solution)/shard_map/all_gather | solution.py:250
  2305.4 285.4 %all-gather.53.cloned.1.call-start = ((), (), s32[]{:S(2)}) async-start(), calls=%async_computation.34 | async-start | bytes 3932160 | tf_op jit(solution)/shard_map/all_gather | solution.py:255
  2512.8 135.8 %all-gather.85.cloned.1.call-start = ((), (), s32[]{:S(2)}) async-start(), calls=%async_computation.64 | async-start | bytes 1769472 | tf_op jit(solution)/shard_map/all_gather | solution.py:55
  2623.9 464.6 %reduce-scatter.41.cloned.1.call-start = ((), (), s32[]{:S(2)}) async-start(), calls=%async_computation.35 | async-start | bytes 7864320 | tf_op jit(solution)/shard_map/reduce_scatter | solution.py:259
  2931.6 25.6 collective-permute-start.2
  3092.2 384.2 %copy-start.28 = (f32[256,1536]{1,0:T(8,128)}, f32[256,1536]{1,0:T(8,128)S(1)}, u32[]{:S(2)}) copy-start(f32[256,1536]{1,0:T(8,128)S(1)} %fusion.291) | copy-start | bytes 4718596
  3303.0 134.7 %all-to-all-start.7 = ((bf16[4,4,120,1536]{3,2,1,0:T(8,128)(2,1)}), bf16[4,4,120,1536]{3,2,1,0:T(8,128)(2,1)}, u32[]{:S(2)}, u32[]{:S(2)}) async-start(bf16[4,4,120,1536]{3,2,1,0:T(8,128)(2,1)} %copy.603), calls=%async_computation.10 | async-start | bytes 11796480 | tf_op jit(solution)/shard_map/all_to_all | solution.py:273
  3308.2 232.7 %all-gather.55.cloned.1.call-start = ((), (), s32[]{:S(2)}) async-start(), calls=%async_computation.36 | async-start | bytes 3932160 | tf_op jit(solution)/shard_map/all_gather | solution.py:255
  3478.3 159.5 %all-gather.87.cloned.1.call-start = ((), (), s32[]{:S(2)}) async-start(), calls=%async_computation.65 | async-start | bytes 1769472 | tf_op jit(solution)/shard_map/all_gather | solution.py:55
  3574.0 517.1 %reduce-scatter.79.cloned.1.call-start = ((), (), s32[]{:S(2)}) async-start(), calls=%async_computation.71 | async-start | bytes 811008
  3577.1 515.0 %reduce-scatter.71.cloned.1.call-start = ((), (), s32[]{:S(2)}) async-start(), calls=%async_computation.67 | async-start | bytes 442368
  3580.6 512.4 %reduce-scatter.75.cloned.1.call-start = ((), (), s32[]{:S(2)}) async-start(), calls=%async_computation.69 | async-start | bytes 811008
  3581.9 511.9 %reduce-scatter.77.cloned.1.call-start = ((), (), s32[]{:S(2)}) async-start(), calls=%async_computation.70 | async-start | bytes 811008
  3584.9 510.3 %reduce-scatter.67.cloned.1.call-start = ((), (), s32[]{:S(2)}) async-start(), calls=%async_computation.49 | async-start | bytes 6488064 | tf_op jit(solution)/shard_map/reduce_scatter | solution.py:606
  3590.2 585.1 %reduce-scatter.65.cloned.1.call-start = ((), (), s32[]{:S(2)}) async-start(), calls=%async_computation.48 | async-start | bytes 6488064 | tf_op jit(solution)/shard_map/reduce_scatter | solution.py:606
  3595.6 740.2 %reduce-scatter.63.cloned.1.call-start = ((), (), s32[]{:S(2)}) async-start(), calls=%async_computation.47 | async-start | bytes 12976128 | tf_op jit(solution)/shard_map/reduce_scatter | solution.py:605
  3603.9 893.9 %reduce-scatter.61.cloned.1.call-start = ((), (), s32[]{:S(2)}) async-start(), calls=%async_computation.46 | async-start | bytes 12976128 | tf_op jit(solution)/shard_map/reduce_scatter | solution.py:605
  3612.5 949.5 %reduce-scatter.59.cloned.1.call-start = ((), (), s32[]{:S(2)}) async-start(), calls=%async_computation.45 | async-start | bytes 7077888 | tf_op jit(solution)/shard_map/reduce_scatter | solution.py:591
  3622.0 1005.4 %reduce-scatter.57.cloned.1.call-start = ((), (), s32[]{:S(2)}) async-start(), calls=%async_computation.44 | async-start | bytes 7077888 | tf_op jit(solution)/shard_map/reduce_scatter | solution.py:591
  3631.5 1064.1 %reduce-scatter.69.cloned.1.call-start = ((), (), s32[]{:S(2)}) async-start(), calls=%async_computation.66 | async-start | bytes 442368
  3657.2 237.2 %copy-start.47 = (f32[12,64,128]{2,1,0:T(8,128)S(1)}, f32[12,64,128]{2,1,0:T(8,128)}, u32[]{:S(2)}) copy-start(f32[12,64,128]{2,1,0:T(8,128)} %copy-done.46) | copy-start | bytes 1179652
  3920.1 790.7 %reduce-scatter.51.cloned.1.call-start = ((), (), s32[]{:S(2)}) async-start(), calls=%async_computation.41 | async-start | bytes 2654208 | tf_op jit(solution)/shard_map/reduce_scatter | solution.py:585
  3927.4 829.4 %reduce-scatter.49.cloned.1.call-start = ((), (), s32[]{:S(2)}) async-start(), calls=%async_computation.40 | async-start | bytes 2654208 | tf_op jit(solution)/shard_map/reduce_scatter | solution.py:585
  3933.7 925.3 %reduce-scatter.47.cloned.1.call-start = ((), (), s32[]{:S(2)}) async-start(), calls=%async_computation.39 | async-start | bytes 1622016 | tf_op jit(solution)/shard_map/reduce_scatter | solution.py:596
  3940.9 1019.4 %reduce-scatter.45.cloned.1.call-start = ((), (), s32[]{:S(2)}) async-start(), calls=%async_computation.38 | async-start | bytes 1622016 | tf_op jit(solution)/shard_map/reduce_scatter | solution.py:596
  3977.4 3.1 collective-permute-start.3
  3987.9 1067.2 %reduce-scatter.55.cloned.1.call-start = ((), (), s32[]{:S(2)}) async-start(), calls=%async_computation.43 | async-start | bytes 14155776 | tf_op jit(solution)/shard_map/reduce_scatter | solution.py:588
  4002.6 1148.4 %reduce-scatter.53.cloned.1.call-start = ((), (), s32[]{:S(2)}) async-start(), calls=%async_computation.42 | async-start | bytes 14155776 | tf_op jit(solution)/shard_map/reduce_scatter | solution.py:588
  4016.5 1276.6 %all-reduce.67.cloned.1.call-start = ((), (), s32[]{:S(2)}) async-start(), calls=%async_computation.72 | async-start | bytes 18874368
  4070.6 1335.8 %reduce-scatter.43.cloned.1.call-start = ((), (), s32[]{:S(2)}) async-start(), calls=%async_computation.37 | async-start | bytes 7864320 | tf_op jit(solution)/shard_map/reduce_scatter | solution.py:259
  4084.8 1423.3 %reduce-scatter.73.cloned.1.call-start = ((), (), s32[]{:S(2)}) async-start(), calls=%async_computation.68 | async-start | bytes 811008
  4086.7 413.1 %copy-start.214 = (f32[1536]{0:T(1024)S(1)}, f32[1536]{0:T(1024)}, u32[]{:S(2)}) copy-start(f32[1536]{0:T(1024)} %get-tuple-element.1985) | copy-start | bytes 18436
  5156.0 250.3 %copy-start.27 = (f32[256,1536]{1,0:T(8,128)S(1)}, f32[256,1536]{1,0:T(8,128)}, u32[]{:S(2)}) copy-start(f32[256,1536]{1,0:T(8,128)} %param.47) | copy-start | bytes 4718596
  5156.0 250.3 %copy-start.164 = (f32[1536]{0:T(1024)S(1)}, f32[1536]{0:T(1024)}, u32[]{:S(2)}) copy-start(f32[1536]{0:T(1024)} %copy-done.163) | copy-start | bytes 18436
  5156.0 250.3 %copy-start.222 = (f32[256]{0:T(256)S(1)}, f32[256]{0:T(256)}, u32[]{:S(2)}) copy-start(f32[256]{0:T(256)} %copy-done.221) | copy-start | bytes 3076
  (356 other events, 7827.7 us)
Sparse Core Ops, SparseCore 0:
  113.1 61.8 all-gather.48
  177.5 40.3 all-gather.56
  458.3 24.1 all-gather.58
  484.8 28.9 all-gather.60
  536.9 109.2 reduce-scatter.36
  648.6 72.6 all-gather.62
  723.1 45.5 all-gather.64
  772.2 106.6 all-gather.66
  881.7 113.3 all-gather.68
  996.9 39.0 all-gather.70
  1196.8 63.4 all-gather.50
  1539.3 23.4 all-gather.72
  1564.7 29.0 all-gather.74
  1606.2 107.9 reduce-scatter.38
  1716.5 72.6 all-gather.76
  1791.6 46.0 all-gather.78
  1989.3 140.9 all-gather.80
  2308.8 124.7 all-gather.82
  2512.9 77.8 all-gather.52
  2624.0 24.5 all-gather.84
  2975.8 112.6 reduce-scatter.40
  3478.4 62.4 all-gather.54
  3574.1 24.5 all-gather.86
  3603.7 95.5 reduce-scatter.78
  3702.4 32.9 reduce-scatter.70
  3740.9 95.5 reduce-scatter.74
  3841.4 94.6 reduce-scatter.76
  3941.7 113.2 reduce-scatter.66
  4061.6 113.5 reduce-scatter.64
  4181.1 154.6 reduce-scatter.62
  4342.8 154.8 reduce-scatter.60
  4501.1 60.8 reduce-scatter.58
  4565.6 61.7 reduce-scatter.56
  4630.5 33.7 reduce-scatter.68
  4668.2 42.4 reduce-scatter.50
  4714.3 42.4 reduce-scatter.48
  4761.9 97.0 reduce-scatter.46
  4864.3 95.9 reduce-scatter.44
  4963.6 91.4 reduce-scatter.54
  5058.6 92.3 reduce-scatter.52
  5154.8 138.2 all-reduce.66
  5295.5 110.8 reduce-scatter.42
  5412.1 95.9 reduce-scatter.72
where the time goes:
time: 5550 us; the launch traced here: 5520 us
  waiting for transfers between devices  2410 us (43%)
  blocking collectives  1110 us (20%)
  local copies, waits for them, and re-layouts  869 us (16%)
  matrix products  607 us (11%)
  other arithmetic  441 us (8%)
    all_gather x2, blocking collectives, common_weights(): lax.all_gather(router[layer_index], ('seq', 'tp'), axis=0, tiled=True)  405 us
    reduce_scatter x4, waiting for transfers between devices, row_sums(): lax.psum_scatter(term(jnp.int32(0), own_rows * lax.axis_size('tp')), 'tp'...  402 us
    dynamic_update_slice x64, local copies, waits for them, and re-layouts, block_scan(): lax.scan(jax.checkpoint(block_step), start_state, (to_blocks(heads_in, bl...  323 us
    reduce_scatter x2, waiting for transfers between devices, local(): lax.psum_scatter(shared_in_grad, ('seq', 'tp'), scatter_dimension=0, tile...  321 us
    unnamed x50, waiting for transfers between devices  237 us
    all_to_all x4, waiting for transfers between devices, from_owners(): return lax.all_to_all(buffer, 'tp', split_axis=0, concat_axis=0, tiled=True)  229 us
    all_to_all x3, waiting for transfers between devices, to_owners(): return lax.all_to_all(buffer, 'tp', split_axis=0, concat_axis=0, tiled=True)  216 us
    reduce_scatter x2, waiting for transfers between devices, local(): lax.psum_scatter(bc_grad, ('seq', 'tp'), scatter_dimension=0, tiled=True)  201 us
  transfers between devices with their start and end apart: 54, of which 28 were waited for; matrix products, arithmetic and copies ran while one was open for 18% of the time, Pallas kernels for 0%

commit v1 on v0

v1 whole, which is shorter than its diff:
```python
from functools import partial

import jax
import jax.numpy as jnp
from jax import lax
from jax.experimental import pallas as pl
from jax.experimental.layout import Layout, with_layout_constraint
from jax.experimental.pallas import tpu as pltpu
from jax.sharding import PartitionSpec as P

HEAD_DIM = 64
STATE = 128
TOP = 6
CHUNK = 256
LANES = 128
FF_BLOCK = 256
ROW_TILE = 256
FAR = -1e30

epsilon = 1e-05
highest = lax.Precision.HIGHEST
bf16 = jnp.bfloat16
f32 = jnp.float32

NN = (((1,), (0,)), ((), ()))
NT = (((1,), (1,)), ((), ()))
TN = (((0,), (0,)), ((), ()))


def mm(a, b, dims=NN, precision=None):
    return lax.dot_general(a, b, dims, precision=precision, preferred_element_type=f32)


def row_major(value):
    return with_layout_constraint(value, Layout(tuple(range(value.ndim))))


def tie(*values):
    return lax.optimization_barrier(values)


def hop_both(v, x, riders=(), axis="tp"):
    n, me = lax.axis_size(axis), lax.axis_index(axis)
    riders = tuple(riders)
    rel = {0: v}
    ahead = right = left = None
    if v is not None:
        ahead = (v, v)
    if x is not None:
        rows = x.shape[0] // n

        def piece(k):
            return lax.dynamic_slice_in_dim(x, jnp.clip(k, 0, n - 1) * rows, rows, 0)

        right, left = piece(n - 1 + me), piece(me - (n - 1))
    lead = 1 if v is not None and x is not None else 0
    for step in range(1, n + lead):
        held = []
        gathers, scatters = ahead is not None and step < n, right is not None and step > lead
        if gathers:
            held += list(ahead)
        if scatters:
            held += [right, left]
        if step > 1:
            count = len(held)
            extra = riders if step == 2 else ()
            if step == 2 and lead and scatters and not gathers:
                extra = riders
            held = list(tie(*held, *extra))
            if extra:
                riders = tuple(held[count:])
            held = held[:count]
        if gathers:
            ahead = (
                lax.ppermute(held[0], axis, [(i, i + 1) for i in range(step - 1, n - 1)]),
                lax.ppermute(held[1], axis, [(i, i - 1) for i in range(1, n - step + 1)]),
            )
            rel[-step], rel[step] = ahead
            held = held[2:]
        if scatters:
            s = step - lead
            right = lax.ppermute(held[0], axis, [(i, i + 1) for i in range(0, s)])
            left = lax.ppermute(held[1], axis, [(i, i - 1) for i in range(n - s, n)])
            if s < n - 1:
                right = (right.astype(f32) + piece(n - 1 - s + me).astype(f32)).astype(x.dtype)
                left = (left.astype(f32) + piece(me - (n - 1 - s)).astype(f32)).astype(x.dtype)
    gathered = total = None
    if v is not None:
        outs = []
        for j in range(n):
            out = rel[j]
            for m in range(1, n):
                out = jnp.where(me == m, rel[j - m], out)
            outs.append(out)
        gathered = jnp.concatenate(outs, 0)
    if x is not None:
        total = piece(me).astype(f32) + right.astype(f32) + left.astype(f32)
    return gathered, total, riders


def hop_gather(v):
    return hop_both(v, None)[0]


def hop_scatter(x):
    return hop_both(None, x)[1]


def pair_total(v, axis):
    n = lax.axis_size(axis)
    bit = 1
    while bit < n:
        v = v + lax.ppermute(v, axis, [(i, i ^ bit) for i in range(n)])
        bit *= 2
    return v


def pair_gather(v, axis="tp"):
    n, me = lax.axis_size(axis), lax.axis_index(axis)
    bit = 1
    while bit < n:
        other = lax.ppermute(v, axis, [(i, i ^ bit) for i in range(n)])
        high = (me & bit) > 0
        v = jnp.concatenate([jnp.where(high, other, v), jnp.where(high, v, other)], 0)
        bit *= 2
    return v


def pair_scatter(v, axis="tp"):
    n, me = lax.axis_size(axis), lax.axis_index(axis)
    bit = n // 2
    while bit:
        half = v.shape[0] // 2
        side = (me & bit) > 0
        first, second = v[:half], v[half:]
        got = lax.ppermute(
            jnp.where(side, first, second), axis, [(i, i ^ bit) for i in range(n)]
        )
        v = jnp.where(side, second, first).astype(f32) + got.astype(f32)
        v = v.astype(first.dtype) if bit > 1 else v
        bit //= 2
    return v


def pair_swap(v, axis="tp"):
    n, me = lax.axis_size(axis), lax.axis_index(axis)
    got = [lax.dynamic_index_in_dim(v, me, 0, keepdims=False)]
    for d in range(1, n):
        send = lax.dynamic_index_in_dim(v, me ^ d, 0, keepdims=False)
        got.append(lax.ppermute(send, axis, [(i, i ^ d) for i in range(n)]))
    outs = []
    for j in range(n):
        out = got[j]
        for m in range(1, n):
            out = jnp.where(me == m, got[j ^ m], out)
        outs.append(out)
    return jnp.stack(outs, 0)


def carried_state(through, state, direction):
    n = lax.axis_size("seq")

    def fetch(steps):
        high, low = split16(through)
        rows = [state.astype(bf16), high, low, jnp.zeros((14, state.shape[1]), bf16)]
        block = jnp.concatenate(rows, 0)
        got = []
        for step in steps:
            part = shift_seq(block, direction * step)
            decay = part[STATE : STATE + 1].astype(f32) + part[STATE + 1 : STATE + 2].astype(f32)
            got.append((decay, part[:STATE].astype(f32)))
        return got

    window = 0
    while window < n - 1:
        if window == 0:
            steps = [k for k in (1, 2, 3) if k < n]
            terms = fetch(steps)
            reach = 3
        else:
            steps = [k * window for k in (1, 2) if k * window < n]
            terms = [(through, state)] + fetch(steps)
            reach = 3 * window
        through, state = terms[0]
        for decay, part in terms[1:]:
            state = state + through * part
            through = through * decay
        window = reach
    return state


def shift_seq(v, steps):
    n = lax.axis_size("seq")
    first, last = max(0, -steps), min(n, n - steps)
    return lax.ppermute(v, "seq", [(i, i + steps) for i in range(first, last)])


def sigmoid(v):
    return 1.0 / (1.0 + jnp.exp(-v))


def shift_down(block, halo, j):
    rolled = pltpu.roll(block, j, 0)
    edge = pltpu.roll(halo, j, 0)
    row = lax.broadcasted_iota(jnp.int32, halo.shape, 0)
    return jnp.concatenate([jnp.where(row < j, edge, rolled[:8]), rolled[8:]], 0)


def shift_up(block, after, j):
    rows = block.shape[0]
    rolled = pltpu.roll(block, rows - j, 0)
    edge = pltpu.roll(after, 8 - j, 0)
    row = lax.broadcasted_iota(jnp.int32, after.shape, 0)
    return jnp.concatenate(
        [rolled[: rows - 8], jnp.where(row >= 8 - j, edge, rolled[rows - 8 :])], 0
    )


def conv_pre(block, halo, taps_ref, aux):
    pre = taps_ref[0:1, :] * block
    for j in (1, 2, 3):
        pre = pre + taps_ref[j : j + 1, :] * (aux[:, j : j + 1] * shift_down(block, halo, j))
    return pre


def softplus(v):
    return jnp.maximum(v, 0.0) + jnp.log(1.0 + jnp.exp(-jnp.abs(v)))


def split16(value):
    high = value.astype(bf16)
    return high, (value - high.astype(f32)).astype(bf16)


def widen(value, ex_ref):
    high, low = split16(value)
    return mm(jnp.concatenate([high, low], 1), ex_ref[...])


def head_sums(value, ex_ref):
    high, low = split16(value)
    spread = ex_ref[:LANES, :]
    return mm(high, spread, NT) + mm(low, spread, NT)


def triangle(n, upper=False):
    row = lax.broadcasted_iota(jnp.int32, (n, n), 0)
    col = lax.broadcasted_iota(jnp.int32, (n, n), 1)
    return jnp.where(row <= col if upper else row >= col, 1.0, 0.0).astype(f32)


def gap_mask(aux, auxr):
    n = aux.shape[0]
    row = lax.broadcasted_iota(jnp.int32, (n, n), 0)
    col = lax.broadcasted_iota(jnp.int32, (n, n), 1)
    return jnp.where((row >= col) & (aux[:, 4:5] == auxr[0:1, :]), 0.0, FAR).astype(f32)


def states_kernel(
    u_ref, bc_ref, dt_ref, edge_ref, taps_ref, head_ref, aux_ref, ex_ref,
    xs_ref, bcs_ref, lc_ref, lt_ref, dtv_ref, thr_ref, ent_ref, fin_ref,
    halo, state,
):
    c = pl.program_id(0)
    n, inner = xs_ref.shape

    @pl.when(c == 0)
    def _():
        halo[...] = edge_ref[...]
        state[...] = jnp.zeros_like(state)

    aux = aux_ref[...]
    block = jnp.concatenate([u_ref[...], bc_ref[...]], 1)
    pre = conv_pre(block, halo[...], taps_ref, aux)
    halo[...] = block[n - 8 :]
    act = pre * sigmoid(pre)
    xs = act[:, :inner]
    bcs = act[:, inner:].astype(bf16)
    dtv = softplus(dt_ref[...] + head_ref[0:1, :])
    lc = mm(triangle(n), head_ref[1:2, :] * dtv, precision=highest)
    total = lc[n - 1 : n, :]
    xs_ref[...] = xs.astype(bf16)
    bcs_ref[...] = bcs
    lc_ref[...] = lc
    lt_ref[...] = lc.T
    dtv_ref[...] = dtv
    scale = widen(jnp.exp(total - lc) * aux[:, 6:7] * dtv, ex_ref)
    through = jnp.exp(jnp.broadcast_to(total, (8, LANES))) * aux[n - 1 : n, 5:6]
    through = widen(through, ex_ref)
    thr_ref[0] = through
    ent_ref[0] = state[...]
    state[...] = through[0:1, :] * state[...] + mm(
        bcs[:, :STATE], (xs * scale).astype(bf16), TN
    )
    fin_ref[...] = state[...]


def intra_kernel(xs_ref, bcs_ref, lc_ref, lt_ref, dtv_ref, aux_ref, auxr_ref, ex_ref, y_ref):
    inner = xs_ref.shape[1]
    mask = gap_mask(aux_ref[...], auxr_ref[...])
    scores = mm(bcs_ref[:, STATE:], bcs_ref[:, :STATE], NT)
    xd = xs_ref[...].astype(f32) * widen(dtv_ref[...], ex_ref)
    lane = lax.broadcasted_iota(jnp.int32, (1, LANES), 1)
    for p in range(inner // LANES):
        pair = xd[:, p * LANES : (p + 1) * LANES]
        total = None
        for side in range(2):
            h = 2 * p + side
            decay = jnp.exp(lc_ref[:, h : h + 1] - lt_ref[h : h + 1, :] + mask)
            mine = (lane < HEAD_DIM) if side == 0 else (lane >= HEAD_DIM)
            term = mm((decay * scores).astype(bf16), jnp.where(mine, pair, 0.0).astype(bf16))
            total = term if total is None else total + term
        y_ref[:, p * LANES : (p + 1) * LANES] = total


def read_kernel(
    z_ref, yi_ref, xs_ref, bcs_ref, lc_ref, aux_ref, ex_ref, ent_ref, car_ref, thr_ref, rows_ref,
    y_ref, gg_ref, ss_ref, st_ref, pre,
):
    c = pl.program_id(0)

    @pl.when(c == 0)
    def _():
        pre[...] = jnp.ones_like(pre)

    entering = ent_ref[0] + pre[0:1, :] * car_ref[...]
    pre[...] = pre[...] * thr_ref[0]
    st_ref[0] = entering
    read = mm(bcs_ref[:, STATE:], entering.astype(bf16))
    entry = widen(jnp.exp(lc_ref[...]) * aux_ref[:, 5:6], ex_ref)
    y = yi_ref[...] + entry * read + rows_ref[0:1, :] * xs_ref[...].astype(f32)
    z = z_ref[...]
    gated = y * (z * sigmoid(z))
    y_ref[...] = y
    gg_ref[...] = (gated * rows_ref[1:2, :]).astype(bf16)
    ss_ref[...] = jnp.broadcast_to(
        jnp.sum(gated * gated, axis=1, keepdims=True), ss_ref.shape
    )


def gate_back_kernel(
    dg_ref, z_ref, y_ref, c2_ref, rows_ref, xs_ref, bcs_ref, lc_ref, aux_ref, ex_ref, thr_ref,
    dy_ref, dz_ref, lg_ref, fin_ref, acc_ref, run,
):
    @pl.when(pl.program_id(0) == 0)
    def _():
        run[...] = jnp.zeros_like(run)
        acc_ref[...] = jnp.zeros_like(acc_ref)

    z, y, back = z_ref[...], y_ref[...], dg_ref[...]
    sig = sigmoid(z)
    open_ = z * sig
    gated = y * open_
    d_gated = back * rows_ref[1:2, :] - gated * c2_ref[:, 0:1]
    dy = d_gated * open_
    dz_ref[...] = (d_gated * y * (sig * (1.0 + z * (1.0 - sig)))).astype(bf16)
    dy_ref[...] = dy.astype(bf16)
    acc_ref[0:1, :] += jnp.sum(back * gated, axis=0, keepdims=True)
    acc_ref[1:2, :] += jnp.sum(dy * xs_ref[...].astype(f32), axis=0, keepdims=True)
    entry = widen(jnp.exp(lc_ref[...]) * aux_ref[:, 5:6], ex_ref)
    lg_ref[0] = run[...]
    run[...] = thr_ref[0, 0:1, :] * run[...] + mm(
        bcs_ref[:, STATE:], (entry * dy).astype(bf16), TN
    )
    fin_ref[...] = run[...]


def scan_back_kernel(
    u_ref, bc_ref, uh_ref, bch_ref, edge_ref, dt_ref, dz_ref, taps_ref, head_ref, rows_ref, aux_ref, auxr_ref, ex_ref,
    lc_ref, lt_ref, dtv_ref, dy_ref, st_ref, lg_ref, car_ref, thr_ref,
    dp_ref, last_ref, back_ref, tacc_ref, hacc_ref,
    post, nxt, later,
):
    step = pl.program_id(0)
    chunks = pl.num_programs(0)
    n, inner = dy_ref.shape

    @pl.when(step == 0)
    def _():
        post[...] = jnp.ones_like(post)
        nxt[...] = jnp.zeros_like(nxt)
        tacc_ref[...] = jnp.zeros_like(tacc_ref)
        hacc_ref[...] = jnp.zeros_like(hacc_ref)
        later[...] = jnp.zeros_like(later)

    aux = aux_ref[...]
    block = jnp.concatenate([u_ref[...], bc_ref[...]], 1)
    halo = jnp.concatenate([uh_ref[...], bch_ref[...]], 1)
    halo = jnp.where(step == chunks - 1, edge_ref[...], halo)
    shifted = [block] + [aux[:, j : j + 1] * shift_down(block, halo, j) for j in (1, 2, 3)]
    pre = taps_ref[0:1, :] * block
    for j in (1, 2, 3):
        pre = pre + taps_ref[j : j + 1, :] * shifted[j]
    sig = sigmoid(pre)
    act = pre * sig
    slope = sig * (1.0 + pre * (1.0 - sig))
    xs = act[:, :inner]
    bcs = act[:, inner:].astype(bf16)
    keys, queries = bcs[:, :STATE], bcs[:, STATE:]
    lc, dtv = lc_ref[...], dtv_ref[...]
    total = lc[n - 1 : n, :]
    dt_wide = widen(dtv, ex_ref)
    tail_wide = widen(jnp.exp(total - lc) * aux[:, 6:7], ex_ref)
    entry_wide = widen(jnp.exp(lc) * aux[:, 5:6], ex_ref)
    xd = xs * dt_wide
    dy = dy_ref[...]
    dyf = dy.astype(f32)
    entering = st_ref[0]
    leaving = lg_ref[0] + post[0:1, :] * car_ref[...]
    post[...] = post[...] * thr_ref[0]
    ent16, lea16 = entering.astype(bf16), leaving.astype(bf16)

    row = lax.broadcasted_iota(jnp.int32, (n, n), 0)
    col = lax.broadcasted_iota(jnp.int32, (n, n), 1)
    mask = jnp.where((row <= col) & (aux[:, 4:5] == auxr_ref[0:1, :]), 0.0, FAR).astype(f32)
    scores = mm(keys, queries, NT)
    lane = lax.broadcasted_iota(jnp.int32, (1, LANES), 1)
    earlier = jnp.zeros((n, LANES), f32)
    d_scores = jnp.zeros((n, n), f32)
    parts = []
    for p in range(inner // LANES):
        cut = slice(p * LANES, (p + 1) * LANES)
        xd_pair, dy_pair = xd[:, cut].astype(bf16), dyf[:, cut]
        d_pair = None
        for side in range(2):
            h = 2 * p + side
            mine = (lane < HEAD_DIM) if side == 0 else (lane >= HEAD_DIM)
            dy_mine = jnp.where(mine, dy_pair, 0.0).astype(bf16)
            decay = jnp.exp(lt_ref[h : h + 1, :] - lc_ref[:, h : h + 1] + mask)
            weights = decay * scores
            d_weights = mm(xd_pair, dy_mine, NT)
            both = weights * d_weights
            earlier = jnp.where(lane == h, jnp.sum(both, axis=1, keepdims=True), earlier)
            later[h : h + 1, :] = jnp.sum(both, axis=0, keepdims=True)
            d_scores = d_scores + decay * d_weights
            term = mm(weights.astype(bf16), dy_mine)
            d_pair = term if d_pair is None else d_pair + term
        parts.append(d_pair)
    d_scores16 = d_scores.astype(bf16)
    through_lea = tail_wide * mm(keys, lea16)
    dxd = jnp.concatenate(parts, 1) + through_lea
    dxs = dt_wide * dxd + rows_ref[0:1, :] * dyf
    entry_dy = entry_wide * dyf
    d_queries = mm(d_scores16, keys, TN) + mm(entry_dy.astype(bf16), ent16, NT)
    d_keys = mm(d_scores16, queries) + mm((tail_wide * xd).astype(bf16), lea16, NT)
    d_act = jnp.concatenate([dxs, d_keys, d_queries], 1)
    dpre = d_act * slope

    into = head_sums(entry_dy * mm(queries, ent16), ex_ref)
    outof = head_sums(xd * through_lea, ex_ref)
    ends = head_sums(
        jnp.sum(entering * leaving, axis=0, keepdims=True) * thr_ref[0], ex_ref
    )
    d_log = later[...].T - earlier + into - outof
    row = lax.broadcasted_iota(jnp.int32, (n, 1), 0)
    d_log = d_log + jnp.where(
        row == n - 1, jnp.sum(outof, axis=0, keepdims=True) + ends[0:1, :], 0.0
    )
    d_rate = mm(triangle(n, True), d_log, precision=highest)
    d_dt = head_sums(xs * dxd, ex_ref) + d_rate * head_ref[1:2, :]
    d_step = d_dt * sigmoid(dt_ref[...] + head_ref[0:1, :])
    hacc_ref[0:1, :] += jnp.sum(d_rate * dtv, axis=0, keepdims=True) * head_ref[1:2, :]
    hacc_ref[1:2, :] += jnp.sum(d_step, axis=0, keepdims=True)

    d_block = taps_ref[0:1, :] * dpre
    tacc_ref[0:1, :] += jnp.sum(dpre * block, axis=0, keepdims=True)
    before = jnp.zeros((8, block.shape[1]), f32)
    row8 = lax.broadcasted_iota(jnp.int32, (8, 1), 0)
    for j in (1, 2, 3):
        tacc_ref[j : j + 1, :] += jnp.sum(dpre * shifted[j], axis=0, keepdims=True)
        lagged = taps_ref[j : j + 1, :] * (dpre * aux[:, j : j + 1])
        d_block = d_block + shift_up(lagged, nxt[j - 1], j)
        nxt[j - 1] = lagged[:8]
        before = before + jnp.where(row8 >= 8 - j, pltpu.roll(lagged[:8], 8 - j, 0), 0.0)
    back_ref[...] = before

    @pl.when(step == 0)
    def _():
        last_ref[...] = d_block[n - 8 :]

    dp_ref[:, :inner] = dz_ref[...]
    dp_ref[:, inner : inner + block.shape[1]] = d_block.astype(bf16)
    ends_at = inner + block.shape[1] + LANES
    dp_ref[:, inner + block.shape[1] : ends_at] = d_step.astype(bf16)
    dp_ref[:, ends_at:] = jnp.zeros((n, LANES), bf16)


def sds(shape, dtype):
    return jax.ShapeDtypeStruct(shape, dtype)


def params(mib):
    return pltpu.CompilerParams(
        dimension_semantics=("arbitrary",), vmem_limit_bytes=mib * 1024 * 1024
    )


def whole(shape):
    return pl.BlockSpec(shape, lambda c: (0,) * len(shape))


def mixer_specs(rows, inner, reverse):
    chunks = rows // CHUNK
    at = (lambda c: chunks - 1 - c) if reverse else (lambda c: c)
    return {
        "uh": pl.BlockSpec(
            (8, inner), lambda c: (jnp.maximum(at(c) * (CHUNK // 8) - 1, 0), 0)
        ),
        "bch": pl.BlockSpec(
            (8, 2 * STATE),
            lambda c: (jnp.maximum(at(c) * (CHUNK // 8) - 1, 0), inner // (2 * STATE)),
        ),
        "bc": pl.BlockSpec((CHUNK, 2 * STATE), lambda c: (at(c), inner // (2 * STATE))),
        "dt": pl.BlockSpec((CHUNK, LANES), lambda c: (at(c), (inner + 2 * STATE) // LANES)),
        "wide": pl.BlockSpec((CHUNK, inner), lambda c: (at(c), 0)),
        "bcs": pl.BlockSpec((CHUNK, 2 * STATE), lambda c: (at(c), 0)),
        "col": pl.BlockSpec((CHUNK, LANES), lambda c: (at(c), 0)),
        "lt": pl.BlockSpec((LANES, CHUNK), lambda c: (0, at(c))),
        "auxr": pl.BlockSpec((8, CHUNK), lambda c: (0, at(c))),
        "state": pl.BlockSpec((1, STATE, inner), lambda c: (at(c), 0, 0)),
        "thr": pl.BlockSpec((1, 8, inner), lambda c: (at(c), 0, 0)),
        "dp": pl.BlockSpec((CHUNK, 2 * inner + 2 * STATE + 2 * LANES), lambda c: (at(c), 0)),
        "edge": whole((8, inner + 2 * STATE)),
        "head": whole((8, LANES)),
        "rows": whole((8, inner)),
        "ex": whole((2 * LANES, inner)),
        "one": whole((STATE, inner)),
    }


def mixer_states(pu, edge, taps, head, aux, ex, inner):
    rows = pu.shape[0]
    chunks = rows // CHUNK
    s = mixer_specs(rows, inner, False)
    return pl.pallas_call(
        states_kernel,
        grid=(chunks,),
        in_specs=[
            s["wide"], s["bc"], s["dt"], s["edge"], s["edge"], s["head"], s["col"], s["ex"],
        ],
        out_specs=[
            s["wide"], s["bcs"], s["col"], s["lt"], s["col"], s["thr"], s["state"], s["one"],
        ],
        out_shape=[
            sds((rows, inner), bf16),
            sds((rows, 2 * STATE), bf16),
            sds((rows, LANES), f32),
            sds((LANES, rows), f32),
            sds((rows, LANES), f32),
            sds((chunks, 8, inner), f32),
            sds((chunks, STATE, inner), f32),
            sds((STATE, inner), f32),
        ],
        scratch_shapes=[
            pltpu.VMEM((8, inner + 2 * STATE), f32),
            pltpu.VMEM((STATE, inner), f32),
        ],
        compiler_params=params(32),
        name="mixer_states",
    )(pu, pu, pu, edge, taps, head, aux, ex)


def mixer_intra(xs, bcs, lc, lt, dtv, aux, auxr, ex):
    rows, inner = xs.shape
    s = mixer_specs(rows, inner, False)
    return pl.pallas_call(
        intra_kernel,
        grid=(rows // CHUNK,),
        in_specs=[
            s["wide"], s["bcs"], s["col"], s["lt"], s["col"], s["col"], s["auxr"], s["ex"],
        ],
        out_specs=s["wide"],
        out_shape=sds((rows, inner), f32),
        compiler_params=params(32),
        name="mixer_intra",
    )(xs, bcs, lc, lt, dtv, aux, auxr, ex)


def mixer_read(pz, yi, xs, bcs, lc, aux, ex, ent, carried, thr, head_rows):
    rows, inner = xs.shape
    chunks = rows // CHUNK
    s = mixer_specs(rows, inner, False)
    return pl.pallas_call(
        read_kernel,
        grid=(chunks,),
        in_specs=[
            s["wide"], s["wide"], s["wide"], s["bcs"], s["col"], s["col"], s["ex"],
            s["state"], s["one"], s["thr"], s["rows"],
        ],
        out_specs=[s["wide"], s["wide"], s["col"], s["state"]],
        out_shape=[
            sds((rows, inner), f32),
            sds((rows, inner), bf16),
            sds((rows, LANES), f32),
            sds((chunks, STATE, inner), f32),
        ],
        scratch_shapes=[pltpu.VMEM((8, inner), f32)],
        compiler_params=params(32),
        name="mixer_read",
    )(pz, yi, xs, bcs, lc, aux, ex, ent, carried, thr, head_rows)


def mixer_gate_back(dg, pz, y, c2, head_rows, xs, bcs, lc, aux, ex, thr):
    rows, inner = xs.shape
    chunks = rows // CHUNK
    s = mixer_specs(rows, inner, True)
    return pl.pallas_call(
        gate_back_kernel,
        grid=(chunks,),
        in_specs=[
            s["wide"], s["wide"], s["wide"], s["col"], s["rows"], s["wide"], s["bcs"],
            s["col"], s["col"], s["ex"], s["thr"],
        ],
        out_specs=[s["wide"], s["wide"], s["state"], s["one"], s["rows"]],
        out_shape=[
            sds((rows, inner), bf16),
            sds((rows, inner), bf16),
            sds((chunks, STATE, inner), f32),
            sds((STATE, inner), f32),
            sds((8, inner), f32),
        ],
        scratch_shapes=[pltpu.VMEM((STATE, inner), f32)],
        compiler_params=params(40),
        name="mixer_gate_back",
    )(dg, pz, y, c2, head_rows, xs, bcs, lc, aux, ex, thr)


def mixer_scan_back(
    pu, edge, dz, taps, head, head_rows, aux, auxr, ex, lc, lt, dtv, dy, st, lg, carried, thr
):
    rows, inner = dy.shape
    chunks = rows // CHUNK
    s = mixer_specs(rows, inner, True)
    wide = inner + 2 * STATE
    return pl.pallas_call(
        scan_back_kernel,
        grid=(chunks,),
        in_specs=[
            s["wide"], s["bc"], s["uh"], s["bch"], s["edge"], s["dt"], s["wide"], s["edge"],
            s["head"], s["rows"], s["col"], s["auxr"], s["ex"], s["col"], s["lt"], s["col"], s["wide"], s["state"], s["state"],
            s["one"], s["thr"],
        ],
        out_specs=[s["dp"], s["edge"], s["edge"], s["edge"], s["head"]],
        out_shape=[
            sds((rows, wide + inner + 2 * LANES), bf16),
            sds((8, wide), f32),
            sds((8, wide), f32),
            sds((8, wide), f32),
            sds((8, LANES), f32),
        ],
        scratch_shapes=[
            pltpu.VMEM((8, inner), f32),
            pltpu.VMEM((3, 8, wide), f32),
            pltpu.VMEM((LANES, CHUNK), f32),
        ],
        compiler_params=params(48),
        name="mixer_scan_back",
    )(
        pu, pu, pu, pu, edge, pu, dz, taps, head, head_rows, aux, auxr, ex, lc, lt, dtv, dy, st,
        lg, carried, thr,
    )


def up_kernel(x_ref, w_ref, gate_ref, pat_ref, h_ref, act_ref):
    for start in range(0, x_ref.shape[0], ROW_TILE):
        cut = slice(start, start + ROW_TILE)
        hidden = mm(x_ref[cut, :], w_ref[...])
        g, w = hidden[:, :FF_BLOCK], hidden[:, FF_BLOCK:]
        gate = mm(gate_ref[cut, :], pat_ref[...])
        h_ref[cut, :] = hidden.astype(bf16)
        act_ref[cut, :] = (g * sigmoid(g) * w * gate).astype(bf16)


def down_back_kernel(gs_ref, w_ref, h_ref, gate_ref, pat_ref, dh_ref, dgate_ref):
    @pl.when(pl.program_id(0) == 0)
    def _():
        dgate_ref[...] = jnp.zeros_like(dgate_ref)

    for start in range(0, gs_ref.shape[0], ROW_TILE):
        cut = slice(start, start + ROW_TILE)
        q = mm(gs_ref[cut, :], w_ref[...], NT)
        g = h_ref[cut, :FF_BLOCK].astype(f32)
        w = h_ref[cut, FF_BLOCK:].astype(f32)
        sig = sigmoid(g)
        opened = g * sig
        gate = mm(gate_ref[cut, :], pat_ref[...])
        dgate_ref[cut, :] += mm((opened * w * q).astype(bf16), pat_ref[...], NT)
        d_act = gate * q
        dh_ref[cut, :FF_BLOCK] = (d_act * w * (sig * (1.0 + g * (1.0 - sig)))).astype(bf16)
        dh_ref[cut, FF_BLOCK:] = (d_act * opened).astype(bf16)


def experts_up(x, w_up, gates, pattern):
    rows, depth = x.shape
    blocks = w_up.shape[1] // (2 * FF_BLOCK)
    return pl.pallas_call(
        up_kernel,
        grid=(blocks,),
        in_specs=[
            whole((rows, depth)),
            pl.BlockSpec((depth, 2 * FF_BLOCK), lambda i: (0, i)),
            whole((rows, LANES)),
            pl.BlockSpec((LANES, FF_BLOCK), lambda i: (0, i)),
        ],
        out_specs=[
            pl.BlockSpec((rows, 2 * FF_BLOCK), lambda i: (0, i)),
            pl.BlockSpec((rows, FF_BLOCK), lambda i: (0, i)),
        ],
        out_shape=[
            sds((rows, 2 * FF_BLOCK * blocks), bf16),
            sds((rows, FF_BLOCK * blocks), bf16),
        ],
        compiler_params=params(32),
        name="experts_up",
    )(x, w_up, gates, pattern)


def experts_down_back(gs, w_down, hidden, gates, pattern):
    rows, depth = gs.shape
    blocks = w_down.shape[0] // FF_BLOCK
    return pl.pallas_call(
        down_back_kernel,
        grid=(blocks,),
        in_specs=[
            whole((rows, depth)),
            pl.BlockSpec((FF_BLOCK, depth), lambda i: (i, 0)),
            pl.BlockSpec((rows, 2 * FF_BLOCK), lambda i: (0, i)),
            whole((rows, LANES)),
            pl.BlockSpec((LANES, FF_BLOCK), lambda i: (0, i)),
        ],
        out_specs=[
            pl.BlockSpec((rows, 2 * FF_BLOCK), lambda i: (0, i)),
            whole((rows, LANES)),
        ],
        out_shape=[
            sds((rows, 2 * FF_BLOCK * blocks), bf16),
            sds((rows, LANES), f32),
        ],
        compiler_params=params(32),
        name="experts_down_back",
    )(gs, w_down, hidden, gates, pattern)


def row_norm(values):
    return lax.rsqrt(jnp.mean(values * values, axis=-1, keepdims=True) + epsilon)


def norm_back(values, inverse, gain, grad):
    weighted = grad * gain
    mean = jnp.mean(weighted * values, axis=-1, keepdims=True)
    return inverse * weighted - values * (inverse * inverse * inverse * mean)


def pad_rows(parts, rows, width):
    value = jnp.concatenate([jnp.atleast_2d(part) for part in parts], 0)
    return jnp.pad(value, ((0, rows - value.shape[0]), (0, width - value.shape[1])))


def to_line(column):
    value = column.reshape(-1, LANES)
    return jnp.pad(value, ((0, 8 - value.shape[0]), (0, 0)))


def local(
    tokens, inner_proj, step_proj, state_proj, inner_conv, state_conv, decay_log, step_bias,
    skip_gain, gate_gain, outer_proj, norm_gains, router, expert_up, expert_down, shared_up,
    shared_down, routes, packed_lengths, cotangent,
):
    ns, nt = lax.axis_size("seq"), lax.axis_size("tp")
    sq, tp = lax.axis_index("seq"), lax.axis_index("tp")
    layers = inner_proj.shape[0]
    own, depth = tokens.shape
    rows = own * nt
    chunks = rows // CHUNK
    inner = gate_gain.shape[1]
    heads = decay_log.shape[1]
    inner_all = inner * nt
    cut = inner_proj.shape[1]
    fine = state_proj.shape[1]
    devices = ns * nt
    experts = router.shape[2]
    mine = expert_up.shape[1]
    ff = expert_down.shape[2] * ns
    ff_cut = expert_down.shape[2]
    shared = shared_down.shape[1] * ns
    sh_cut = shared_down.shape[1]
    tap_cut = state_conv.shape[2]
    width = inner + 2 * STATE
    hidden_units = mine * ff + shared
    ff_blocks = hidden_units // FF_BLOCK
    per_seq = mine * ff_cut + sh_cut

    ends = jnp.cumsum(packed_lengths, dtype=jnp.int32)
    starts = ends - packed_lengths

    def count(positions):
        return jnp.sum(
            (starts[None, :] <= positions[:, None]).astype(f32), axis=1
        )

    first = sq * rows
    here = first + jnp.arange(rows, dtype=jnp.int32)
    seg = count(here)
    chunk_of = jnp.arange(rows, dtype=jnp.int32) // CHUNK
    lags = [jnp.ones_like(seg)] + [(count(here - j) == seg).astype(f32) for j in (1, 2, 3)]
    alive = (count(first + chunk_of * CHUNK - 1) == seg).astype(f32)
    tail = (count(first + chunk_of * CHUNK + CHUNK - 1) == seg).astype(f32)
    aux = jnp.pad(jnp.stack(lags + [seg, alive, tail], 1), ((0, 0), (0, LANES - 7)))
    auxr = jnp.broadcast_to(seg[None, :], (8, rows))
    lane_head = jnp.arange(inner, dtype=jnp.int32) // HEAD_DIM
    ex_row = jnp.arange(2 * LANES, dtype=jnp.int32)[:, None] % LANES
    ex = (ex_row == lane_head[None, :]).astype(bf16)
    unit = jnp.arange(hidden_units, dtype=jnp.int32) % per_seq
    unit_gate = jnp.where(unit < mine * ff_cut, unit // ff_cut, mine)
    pat_row = jnp.arange(LANES, dtype=jnp.int32)[:, None]
    pattern = ((pat_row == unit_gate[None, :]) | (pat_row == 16 + unit_gate[None, :])).astype(bf16)

    inv1 = row_norm(tokens)
    scaled = (tokens * inv1).astype(bf16)
    smalls, ups = [], []
    for l in range(layers):
        taps_col = jnp.pad(state_conv[l].reshape(-1), (0, fine - 4 * tap_cut))[:, None]
        small = jnp.concatenate([state_proj[l], router[l], norm_gains[l].T, taps_col], 1)
        smalls.append(jnp.pad(small, ((0, 0), (0, 2 * STATE + LANES - small.shape[1]))))
        up = shared_up[l].reshape(fine, 2, ns, nt, sh_cut)
        ups.append(jnp.transpose(up, (3, 0, 1, 2, 4)).reshape(nt, fine, 2 * shared))
    plain, _, riders = hop_both(
        scaled,
        None,
        (jnp.concatenate(smalls, 1), expert_up, jnp.stack(ups, 1), routes, expert_down, shared_down),
    )
    small_all, expert_up, ups, routes, expert_down, shared_down = riders
    small_all = pair_gather(small_all)
    up_all = pair_swap(ups)

    def mixer_weights(l):
        dt_cols = jnp.pad(step_proj[l], ((0, 0), (0, LANES - heads)))
        small = small_all[:, l * (2 * STATE + LANES) : (l + 1) * (2 * STATE + LANES)]
        pack = jnp.concatenate(
            [
                inner_proj[l, :, 0],
                inner_proj[l, :, 1],
                small[:, : 2 * STATE],
                dt_cols,
                small[:, 2 * STATE :],
            ],
            1,
        )
        return pack, outer_proj[l].T

    def over_seq(value):
        return lax.all_gather(value, "seq", axis=0, tiled=True)

    def expert_weights(l):
        halves = jnp.transpose(expert_up[l].reshape(mine, cut, 2, ns, ff_cut), (2, 1, 3, 0, 4))
        halves = halves.reshape(2, cut, ns, mine * ff_cut)
        extra = jnp.transpose(up_all[:, l].reshape(cut, 2, ns, sh_cut), (1, 0, 2, 3))
        halves = jnp.concatenate([halves, extra], 3).reshape(2, cut, ff_blocks, FF_BLOCK)
        local_up = jnp.transpose(halves, (1, 2, 0, 3)).reshape(cut, 2 * hidden_units)
        local_down = jnp.concatenate(
            [expert_down[l].reshape(mine * ff_cut, depth), shared_down[l]], 0
        )
        return local_up, local_down

    packs = [list(mixer_weights(l) + expert_weights(l)) for l in range(layers)]
    plain, *packs[0][2:] = tie(plain, *packs[0][2:])
    w_in, w_out, w_up, w_down = [[None] * layers for _ in range(4)]
    w_in[0], w_out[0] = over_seq(packs[0][0]), over_seq(packs[0][1])

    named = jnp.any(
        routes[:, :, :, None] == jnp.arange(experts, dtype=jnp.int32), axis=2
    ).astype(bf16)
    named = pair_gather(
        jnp.transpose(named, (1, 0, 2)).reshape(own, layers * experts)
    ).reshape(rows, layers, experts)

    residual = tokens
    saved = []
    last_cot = None
    for l in range(layers):
        small_in = tie(w_in[l][:, inner + width + LANES :].astype(f32).T)[0]
        router_w = small_in[:experts].astype(bf16)
        gain1 = small_in[experts]
        gain2 = small_in[experts + 1]
        taps_bc = small_in[experts + 2].reshape(devices, fine)[:, : 4 * tap_cut]
        taps_bc = jnp.transpose(taps_bc.reshape(devices, 4, tap_cut), (1, 0, 2))
        taps_bc = taps_bc.reshape(4, 2 * STATE)
        taps = jnp.pad(
            jnp.concatenate([inner_conv[l], taps_bc], 1), ((0, 4), (0, 0))
        )
        head = pad_rows([step_bias[l], -jnp.exp(decay_log[l])], 8, LANES)
        head_rows = pad_rows([jnp.repeat(skip_gain[l], HEAD_DIM), gate_gain[l]], 8, inner)

        if l > 0:
            inv1 = row_norm(residual)
            scaled = (residual * inv1).astype(bf16)
            plain = hop_gather(scaled)
        normed = (plain.astype(f32) * gain1).astype(bf16)
        pu = mm(normed, w_in[l][:, inner : inner + width + LANES])
        edge = shift_seq(pu[rows - 8 :, :width], 1)
        xs, bcs, lc, lt, dtv, thr, ent, fin = mixer_states(pu, edge, taps, head, aux, ex, inner)
        through = thr[0, 0:1]
        for c in range(1, chunks):
            through = through * thr[c, 0:1]
        carried = carried_state(through, fin, 1)
        pz = mm(normed, w_in[l][:, :inner])
        cot16 = cotangent.astype(bf16)
        if l == 0:
            pz, cot16 = tie(pz, cot16)
        yi = mixer_intra(xs, bcs, lc, lt, dtv, aux, auxr, ex)
        carried, up_pack, down_pack = tie(carried, packs[l][2], packs[l][3])
        w_up[l], w_down[l] = over_seq(up_pack), over_seq(down_pack)
        y, gg, ss, st = mixer_read(pz, yi, xs, bcs, lc, aux, ex, ent, carried, thr, head_rows)
        squares = pair_total(ss[:, 0].reshape(rows // LANES, LANES), "tp")
        squares = lax.dynamic_slice_in_dim(
            squares, tp * (own // LANES), own // LANES, 0
        ).reshape(own)
        partial_out = mm(gg, w_out[l], NT).astype(bf16)
        if l == 0:
            last_cot, out_sum, _ = hop_both(cot16, partial_out)
            out_sum, last_cot = tie(out_sum, last_cot)
        else:
            out_sum = hop_scatter(partial_out)
        inv_gate = lax.rsqrt(squares / inner_all + epsilon)
        mixed = inv_gate[:, None] * out_sum
        mid = residual + mixed

        inv2 = row_norm(mid)
        moe_own = (mid * inv2 * gain2).astype(bf16)
        moe_in = hop_gather(moe_own)
        if l < layers - 1:
            moe_in, *packs[l + 1] = tie(moe_in, *packs[l + 1])
            w_in[l + 1], w_out[l + 1] = over_seq(packs[l + 1][0]), over_seq(packs[l + 1][1])
        logits = mm(moe_in, router_w, NT)
        mask = named[:, l] > 0
        peak = jnp.max(jnp.where(mask, logits, FAR), axis=1, keepdims=True)
        raised = jnp.where(mask, jnp.exp(jnp.where(mask, logits - peak, 0.0)), 0.0)
        gates = raised / jnp.sum(raised, axis=1, keepdims=True)
        gates_mine = lax.dynamic_slice_in_dim(gates, tp * mine, mine, 1)
        gates_mine = jnp.concatenate([gates_mine, jnp.ones((rows, 1), f32)], 1)
        high, low = split16(gates_mine)
        gate_cols = jnp.concatenate(
            [jnp.pad(part, ((0, 0), (0, 15 - mine))) for part in (high, low)], 1
        )
        gate_cols = jnp.pad(gate_cols, ((0, 0), (0, LANES - 32)))
        hidden, act = experts_up(moe_in, w_up[l], gate_cols, pattern)
        saved.append(
            dict(
                router_w=router_w, gain1=gain1, gain2=gain2, taps=taps, head=head,
                head_rows=head_rows, residual=residual, inv1=inv1, plain=plain, normed=normed,
                pu=pu, pz=pz, edge=edge, xs=xs, bcs=bcs, lc=lc, lt=lt, dtv=dtv, thr=thr,
                through=through, y=y, gg=gg, st=st, inv_gate=inv_gate, mixed=mixed,
                mid=mid, inv2=inv2, moe_own=moe_own, moe_in=moe_in, gates=gates,
                gate_cols=gate_cols, hidden=hidden, act=act,
            )
        )
        if l < layers - 1:
            residual = mid + hop_scatter(mm(act, w_down[l]).astype(bf16))

    def finish(r):
        late, early, sums = r["late"], r["early"], r["sums"]
        halves = r["up"].reshape(cut, ff_blocks, 2, FF_BLOCK)
        halves = jnp.transpose(halves, (2, 0, 1, 3)).reshape(2, cut, ns, per_seq)
        mine_up = halves[..., : mine * ff_cut].reshape(2, cut, ns, mine, ff_cut)
        mine_up = jnp.transpose(mine_up, (3, 1, 0, 2, 4)).reshape(mine, cut, 2 * ff)
        mine_up = row_major(mine_up)
        shared_cols = jnp.transpose(halves[..., mine * ff_cut :], (1, 0, 2, 3))
        shared_grad = pair_swap(shared_cols.reshape(nt, fine, 2 * shared))
        shared_grad = jnp.transpose(
            shared_grad.reshape(nt, fine, 2, ns, sh_cut), (1, 2, 3, 0, 4)
        ).reshape(fine, -1)
        common = pair_scatter(late[:, inner:])
        small = common[:, 2 * STATE + heads :]
        return [
            jnp.stack([early[:, inner:], late[:, :inner]], 1),
            late[:, width : width + heads].astype(f32),
            common[:, : 2 * STATE],
            sums[:4],
            small[: 4 * tap_cut, experts + 2].reshape(4, tap_cut),
            sums[6, :heads],
            sums[6, LANES : LANES + heads],
            jnp.sum(sums[5].reshape(heads, HEAD_DIM), axis=1),
            sums[4],
            early[:, :inner].T,
            jnp.transpose(small[:, experts : experts + 2]),
            small[:, :experts],
            mine_up,
            r["down"][: mine * ff_cut].reshape(mine, ff_cut, depth),
            shared_grad,
            r["down"][mine * ff_cut :],
        ]

    grad = cotangent
    finished = [None] * layers
    for l in reversed(range(layers)):
        k = saved[l]
        top = l == layers - 1
        gs = last_cot if top else hop_gather(grad.astype(bf16))
        if not top:
            gs, above["late"] = tie(gs, above["late"])
        else:
            last_out = mm(k["act"], w_down[l]).astype(bf16)
        d_hidden, d_gate = experts_down_back(
            gs, w_down[l], k["hidden"], k["gate_cols"], pattern
        )
        d_gate_all = jnp.zeros((rows, experts), f32)
        d_gate_all = lax.dynamic_update_slice(d_gate_all, d_gate[:, :mine], (0, tp * mine))
        per_line = LANES // experts
        d_gate_all = pair_total(d_gate_all.reshape(rows // per_line, LANES), "tp")
        d_gate_own = lax.dynamic_slice_in_dim(
            d_gate_all, tp * (own // per_line), own // per_line, 0
        ).reshape(own, experts)
        d_moe = hop_scatter(mm(d_hidden, w_up[l], NT).astype(bf16))
        up_part = mm(k["moe_in"], d_hidden, TN).astype(bf16)
        down_part = mm(k["act"], gs, TN).astype(bf16)
        if top:
            d_moe, up_part, last_out = tie(d_moe, up_part, last_out)
        else:
            d_moe, up_part = tie(d_moe, up_part)
        up_grad = lax.psum_scatter(up_part, "seq", scatter_dimension=0, tiled=True)
        gates_own = lax.dynamic_slice_in_dim(k["gates"], tp * own, own, 0)
        d_logits = gates_own * (
            d_gate_own - jnp.sum(gates_own * d_gate_own, axis=1, keepdims=True)
        )
        d_logits16 = d_logits.astype(bf16)
        router_grad = mm(k["moe_own"], d_logits16, TN)
        d_moe = d_moe + mm(d_logits16, k["router_w"])
        gain2_grad = jnp.sum(d_moe * k["mid"] * k["inv2"], axis=0)
        grad_mid = grad + norm_back(k["mid"], k["inv2"], k["gain2"], d_moe)

        inv_gate = k["inv_gate"]
        cross = inv_gate * inv_gate * jnp.sum(grad_mid * k["mixed"], axis=1) / inner_all
        cross_all = pair_gather(to_line(cross)).reshape(nt, 8 * LANES)[:, :own].reshape(rows)
        c2 = jnp.broadcast_to(cross_all[:, None], (rows, LANES))
        send = (grad_mid * inv_gate[:, None]).astype(bf16)
        if top:
            d_mixed, moe_out, _ = hop_both(send, last_out)
            residual = k["mid"] + moe_out
        else:
            d_mixed = hop_gather(send)
        d_mixed, down_part = tie(d_mixed, down_part)
        down_grad = lax.psum_scatter(down_part, "seq", scatter_dimension=0, tiled=True)
        dg = mm(d_mixed, w_out[l])
        dy, dz, lg, fin, acc = mixer_gate_back(
            dg, k["pz"], k["y"], c2, k["head_rows"], k["xs"], k["bcs"], k["lc"], aux, ex, k["thr"]
        )
        carried = carried_state(k["through"], fin, -1)
        early = jnp.concatenate(
            [
                row_major(mm(d_mixed, k["gg"], TN).astype(bf16)),
                row_major(mm(k["normed"], dz, TN).astype(bf16)),
            ],
            1,
        )
        carried, early, up_grad = tie(carried, early, up_grad)
        if top:
            carried, residual = tie(carried, residual)
        early = lax.psum_scatter(early, "seq", scatter_dimension=0, tiled=True)
        dp, last, back, tacc, hacc = mixer_scan_back(
            k["pu"], k["edge"], dz, k["taps"], k["head"], k["head_rows"], aux, auxr, ex,
            k["lc"], k["lt"], k["dtv"], dy, k["st"], lg, carried, k["thr"],
        )
        last = (last + shift_seq(back, -1)).astype(bf16)
        dp = lax.dynamic_update_slice(dp, last, (rows - 8, inner))
        dp, down_grad = tie(dp, down_grad)
        d_normed = mm(dp, w_in[l], NT)
        gain1_grad = jnp.sum(d_normed * k["plain"].astype(f32), axis=0)
        if top:
            d_own = hop_scatter(d_normed.astype(bf16))
        else:
            names = ("up", "down", "early", "late")
            _, d_own, riders = hop_both(
                None, d_normed.astype(bf16), [above[name] for name in names]
            )
            above.update(zip(names, riders))
            finished[l + 1] = finish(above)
        taps_col = jnp.transpose(tacc[:4, inner:].reshape(4, devices, tap_cut), (1, 0, 2))
        taps_col = jnp.pad(taps_col.reshape(devices, 4 * tap_cut), ((0, 0), (0, fine - 4 * tap_cut)))
        small = jnp.concatenate(
            [router_grad, gain1_grad[:, None], gain2_grad[:, None], taps_col.reshape(-1)[:, None]],
            1,
        )
        late = mm(k["normed"], dp[:, inner : inner + width + LANES], TN).astype(bf16)
        block = late[:, width:] + jnp.pad(
            small, ((0, 0), (heads, LANES - heads - small.shape[1]))
        ).astype(bf16)
        late = lax.dynamic_update_slice(late, block, (0, width))
        d_own, late, early = tie(d_own, late, early)
        late = lax.psum_scatter(late, "seq", scatter_dimension=0, tiled=True)
        sums = pair_total(
            jnp.concatenate(
                [tacc[:4, :inner], acc[:2], pad_rows([hacc[:2].reshape(-1)], 2, inner)], 0
            ),
            "seq",
        )
        grad = grad_mid + norm_back(k["residual"], k["inv1"], k["gain1"], d_own)
        above = dict(up=up_grad, down=down_grad, early=early, late=late, sums=sums)

    finished[0] = finish(above)
    stacked = [jnp.stack([part[i] for part in finished], 0).astype(f32) for i in range(16)]
    return (residual, grad, *stacked)


def solution(mesh):
    both = ("seq", "tp")
    in_specs = (
        P(both, None),
        P(None, "seq", None, "tp"),
        P(None, "seq", "tp"),
        P(None, both, None),
        P(None, None, "tp"),
        P(None, None, both),
        P(None, "tp"),
        P(None, "tp"),
        P(None, "tp"),
        P(None, "tp"),
        P(None, "tp", "seq"),
        P(None, None, both),
        P(None, both, None),
        P(None, "tp", "seq", None),
        P(None, "tp", "seq", None),
        P(None, both, None),
        P(None, both, None),
        P(None, both, None),
        P(),
        P(both, None),
    )
    out_specs = (
        P(both, None),
        P(both, None),
        P(None, "seq", None, "tp"),
        P(None, "seq", "tp"),
        P(None, both, None),
        P(None, None, "tp"),
        P(None, None, both),
        P(None, "tp"),
        P(None, "tp"),
        P(None, "tp"),
        P(None, "tp"),
        P(None, "tp", "seq"),
        P(None, None, both),
        P(None, both, None),
        P(None, "tp", "seq", None),
        P(None, "tp", "seq", None),
        P(None, both, None),
        P(None, both, None),
    )
    return jax.shard_map(local, mesh=mesh, in_specs=in_specs, out_specs=out_specs, check_vma=False)
```

time: 5550 us -> 1750 us (0.32)
  waiting for transfers between devices: 2410 us -> 666 us
  blocking collectives: 1110 us -> 0 us
  local copies, waits for them, and re-layouts: 869 us -> 191 us
  matrix products: 607 us -> 223 us
  other arithmetic: 441 us -> 154 us
  starting transfers between devices: 46.7 us -> 312 us
  Pallas kernels: 0 us -> 177 us
    reduce_scatter x16 -> x8, waiting for transfers between devices: 1380 us -> 5.27 us  [the longest x2 5.24 us: local(): late = lax.psum_scatter(late, 'seq', scatter_dimension=0, tiled=True)]
    all_gather x12 -> x0, blocking collectives: 871 us -> none  [the longest x2 405 us: common_weights(): lax.all_gather(router[layer_index], ('seq', 'tp'), axis=0, tiled=True)]
    ppermute x4 -> x155, waiting for transfers between devices: 0.21 us -> 659 us  [the longest x24 210 us: hop_both(): lax.ppermute(held[1], axis, [(i, i - 1) for i in range(1, n - step + 1)])]
    all_to_all x7 -> x0, waiting for transfers between devices: 445 us -> none  [the longest x4 229 us: from_owners(): return lax.all_to_all(buffer, 'tp', split_axis=0, concat_axis=0, tiled=True)]
    dot_general x170 -> x30, matrix products: 601 us -> 223 us  [mm(): lax.dot_general(a, b, dims, precision=precision, preferred_element_type=f32)]
    all_gather x20 -> x8, waiting for transfers between devices: 344 us -> 0.07 us  [over_seq(): return lax.all_gather(value, 'seq', axis=0, tiled=True)]
    dynamic_update_slice x64 -> x4, local copies, waits for them, and re-layouts: 323 us -> 1.23 us  [local(): lax.dynamic_update_slice(d_gate_all, d_gate[:, :mine], (0, tp * mine))]
    ppermute x4 -> x155, starting transfers between devices: 6.27 us -> 310 us  [the longest x24 106 us: hop_both(): right = lax.ppermute(held[0], axis, [(i, i + 1) for i in range(0, s)])]
  transfers between devices with their start and end apart: 54 -> 171, of which waited for: 28 -> 88; matrix products, arithmetic and copies ran while one was open for 18% -> 25% of each run, Pallas kernels for 0% -> 8%
where the time goes in v1:
time: 1750 us; the launch traced here: 1740 us
  waiting for transfers between devices  666 us (38%)
  starting transfers between devices  312 us (18%)
  matrix products  223 us (13%)
  local copies, waits for them, and re-layouts  191 us (11%)
  Pallas kernels  177 us (10%)
  other arithmetic  154 us (9%)
  between operations  19.8 us (1%)
    dot_general x30, matrix products, mm(): lax.dot_general(a, b, dims, precision=precision, preferred_element_type=f32)  223 us
    ppermute x24, waiting for transfers between devices, hop_both(): lax.ppermute(held[1], axis, [(i, i - 1) for i in range(1, n - step + 1)])  210 us
    ppermute x24, waiting for transfers between devices, hop_both(): right = lax.ppermute(held[0], axis, [(i, i + 1) for i in range(0, s)])  178 us
    ppermute x24, starting transfers between devices, hop_both(): right = lax.ppermute(held[0], axis, [(i, i + 1) for i in range(0, s)])  106 us
    ppermute x24, waiting for transfers between devices, hop_both(): lax.ppermute(held[0], axis, [(i, i + 1) for i in range(step - 1, n - 1)])  82.1 us
    unnamed x524, local copies, waits for them, and re-layouts  72.5 us
    ppermute x14, waiting for transfers between devices, pair_total(): v = v + lax.ppermute(v, axis, [(i, i ^ bit) for i in range(n)])  63.3 us
    ppermute x24, waiting for transfers between devices, shift_seq(): return lax.ppermute(v, 'seq', [(i, i + steps) for i in range(first, last)])  63.1 us
  transfers between devices with their start and end apart: 171, of which 88 were waited for; matrix products, arithmetic and copies ran while one was open for 25% of the time, Pallas kernels for 8%

profile of v1, /device:TPU:0, one launch (start us, length us, event | category | flops | bytes accessed | tf_op | source)
XLA Modules:
  0.0 1742.5 jit_solution(5904534276055870494)
XLA Ops:
  25.5 7.9 collective-permute-done
  77.8 9.7 collective-permute-done.3
  130.9 6.6 mixer_states.2
  182.5 7.1 collective-permute-start.19
  220.3 12.7 collective-permute-done.23
  245.0 15.4 collective-permute-done.17
  273.0 10.9 collective-permute-done.30
  287.7 13.1 collective-permute-done.28
  306.6 15.8 collective-permute-done.31
  329.5 20.5 %collective-permute-done.34 = bf16[256,1536]{1,0:T(8,128)(2,1)} collective-permute-done((bf16[256,1536]{1,0:T(8,128)(2,1)S(1)}, bf16[256,1536]{1,0:T(8,128)(2,1)}, u32[]{:S(2)}, u32[]{:S(2)}) %collective-permute-start.34) | collective-permute-done | bytes 786464 | tf_op jit(solution)/shard_map/ppermute | solution.py:76
  389.8 20.0 %experts_up.2 = (bf16[1024,4608]{1,0:T(8,128)(2,1)S(1)}, bf16[1024,2304]{1,0:T(8,128)(2,1)S(1)}) custom-call(bf16[1024,1536]{1,0:T(8,128)(2,1)S(1)} %copy-done.3, bf16[1536,4608]{1,0:T(8,128)(2,1)} %all-gather.13.cloned.1.call-done.w_ref, bf16[1024,128]{1,0:T(8,128)(2,1)S(1)} %pad.112.gate_ref, bf16[128,2304]{1,0:T(8,128)(2,1)S(1)} %fusion.23.pat_ref), custom_call_target="tpu_custom_call" | custom-call | tf_op jit(solution)/shard_map/experts_up/pallas_call | solution.py:696
  415.6 11.1 convolution_convert_fusion.10
  429.6 12.1 collective-permute-done.39
  447.3 10.9 collective-permute-done.41
  458.7 7.6 collective-permute-start.43
  467.5 9.3 collective-permute-done.43
  485.3 8.4 collective-permute-done.45
  502.8 15.5 collective-permute-done.48
  525.4 8.8 collective-permute-done.50
  536.9 7.4 fusion.4.u_ref.bc_ref.dt_ref.uh_ref.bch_ref
  546.4 6.6 mixer_states.3
  559.6 9.9 collective-permute-start.53
  613.6 14.2 collective-permute-done.59
  633.5 14.9 collective-permute-done.61
  659.4 16.9 collective-permute-done.57
  684.8 15.8 collective-permute-done.65
  706.9 20.0 %collective-permute-done.68 = bf16[256,1536]{1,0:T(8,128)(2,1)S(1)} collective-permute-done((bf16[256,1536]{1,0:T(8,128)(2,1)S(1)}, bf16[256,1536]{1,0:T(8,128)(2,1)S(1)}, u32[]{:S(2)}, u32[]{:S(2)}) %collective-permute-start.68) | collective-permute-done | bytes 786464 | tf_op jit(solution)/shard_map/ppermute | solution.py:76
  729.3 18.1 %collective-permute-done.70 = bf16[256,1536]{1,0:T(8,128)(2,1)S(1)} collective-permute-done((bf16[256,1536]{1,0:T(8,128)(2,1)S(1)}, bf16[256,1536]{1,0:T(8,128)(2,1)S(1)}, u32[]{:S(2)}, u32[]{:S(2)}) %collective-permute-start.70) | collective-permute-done | bytes 786464 | tf_op jit(solution)/shard_map/ppermute | solution.py:76
  755.7 20.0 %experts_up.3 = (bf16[1024,4608]{1,0:T(8,128)(2,1)S(1)}, bf16[1024,2304]{1,0:T(8,128)(2,1)S(1)}) custom-call(bf16[1024,1536]{1,0:T(8,128)(2,1)S(1)} %copy-done.6, bf16[1536,4608]{1,0:T(8,128)(2,1)} %all-gather.23.cloned.1.call-done.w_ref, bf16[1024,128]{1,0:T(8,128)(2,1)S(1)} %pad.118.gate_ref, bf16[128,2304]{1,0:T(8,128)(2,1)S(1)} %fusion.23.pat_ref), custom_call_target="tpu_custom_call" | custom-call | tf_op jit(solution)/shard_map/experts_up/pallas_call | solution.py:696
  786.4 22.1 %experts_down_back.2 = (bf16[1024,4608]{1,0:T(8,128)(2,1)S(1)}, f32[1024,128]{1,0:T(8,128)S(1)}) custom-call(bf16[1024,1536]{1,0:T(8,128)(2,1)S(1)} %copy-done.10, bf16[2304,1536]{1,0:T(8,128)(2,1)S(1)} %copy-done.25, bf16[1024,4608]{1,0:T(8,128)(2,1)} %copy-done.17, bf16[1024,128]{1,0:T(8,128)(2,1)S(1)} %pad.118.gate_ref, bf16[128,2304]{1,0:T(8,128)(2,1)S(1)} %fusion.23.pat_ref), custom_call_target="tpu_custom_call" | custom-call | tf_op jit(solution)/shard_map/experts_down_back/pallas_call | solution.py:721
  808.5 17.7 %convolution_convert_fusion.7 = bf16[1024,1536]{1,0:T(8,128)(2,1)S(1)} fusion(bf16[1024,4608]{1,0:T(8,128)(2,1)S(1)} %get-tuple-element.275, bf16[1536,4608]{1,0:T(8,128)(2,1)} %all-gather.23.cloned.1.call-done.w_ref), kind=kOutput, calls=%fused_computation.17 | convolution fusion | flops 14497087488 | bytes 26738688 | tf_op jit(solution)/shard_map/dot_general | solution.py:31
  829.2 13.7 collective-permute-done.71
  851.4 17.7 %convolution_convert_fusion.1 = bf16[1536,4608]{1,0:T(8,128)(2,1)} fusion(bf16[1024,1536]{1,0:T(8,128)(2,1)S(1)} %copy-done.7, bf16[1024,4608]{1,0:T(8,128)(2,1)S(1)} %get-tuple-element.275), kind=kOutput, calls=%fused_computation.1 | convolution fusion | flops 14502592512 | bytes 26738688 | tf_op jit(solution)/shard_map/dot_general | solution.py:31
  874.0 12.3 convolution_convert_fusion.8
  922.1 10.1 collective-permute-done.79
  940.9 6.7 collective-permute-done.83
  949.2 11.6 collective-permute-done.82
  963.9 9.4 convolution_convert_fusion.3
  1030.2 7.8 collective-permute-done.92
  1053.2 27.0 %mixer_scan_back.2 = (bf16[1024,2048]{1,0:T(8,128)(2,1)}, f32[8,1024]{1,0:T(8,128)S(1)}, f32[8,1024]{1,0:T(8,128)}, f32[8,1024]{1,0:T(8,128)S(1)}, f32[8,128]{1,0:T(8,128)S(1)}) custom-call(f32[1024,1152]{1,0:T(8,128)} %copy-done.2, f32[1024,1152]{1,0:T(8,128)} %copy-done.2, f32[1024,1152]{1,0:T(8,128)} %copy-done.2, f32[1024,1152]{1,0:T(8,128)} %copy-done.2, ...), custom_call_target="tpu_custom_call" | custom-call | tf_op jit(solution)/shard_map/mixer_scan_back/pallas_call | solution.py:635
  1090.0 11.7 fusion.3
  1107.4 15.7 collective-permute-done.99
  1132.8 12.8 collective-permute-done.101
  1149.0 8.2 collective-permute-start.103
  1158.5 8.0 convolution_convert_fusion.5
  1189.5 15.7 collective-permute-done.105
  1211.4 19.1 %collective-permute-done.108 = bf16[256,1536]{1,0:T(8,128)(2,1)S(1)} collective-permute-done((bf16[256,1536]{1,0:T(8,128)(2,1)S(1)}, bf16[256,1536]{1,0:T(8,128)(2,1)S(1)}, u32[]{:S(2)}, u32[]{:S(2)}) %collective-permute-start.108) | collective-permute-done | bytes 786464 | tf_op jit(solution)/shard_map/ppermute | solution.py:76
  1232.8 18.0 %collective-permute-done.110 = bf16[256,1536]{1,0:T(8,128)(2,1)S(1)} collective-permute-done((bf16[256,1536]{1,0:T(8,128)(2,1)S(1)}, bf16[256,1536]{1,0:T(8,128)(2,1)S(1)}, u32[]{:S(2)}, u32[]{:S(2)}) %collective-permute-start.110) | collective-permute-done | bytes 786464 | tf_op jit(solution)/shard_map/ppermute | solution.py:76
  1257.9 22.1 %experts_down_back.3 = (bf16[1024,4608]{1,0:T(8,128)(2,1)S(1)}, f32[1024,128]{1,0:T(8,128)S(1)}) custom-call(bf16[1024,1536]{1,0:T(8,128)(2,1)S(1)} %copy-done.12, bf16[2304,1536]{1,0:T(8,128)(2,1)S(1)} %copy-done.24, bf16[1024,4608]{1,0:T(8,128)(2,1)} %copy-done.16, bf16[1024,128]{1,0:T(8,128)(2,1)S(1)} %copy-done.34, bf16[128,2304]{1,0:T(8,128)(2,1)S(1)} %fusion.23.pat_ref), custom_call_target="tpu_custom_call" | custom-call | tf_op jit(solution)/shard_map/experts_down_back/pallas_call | solution.py:721
  1280.0 17.6 %convolution_convert_fusion.6 = bf16[1024,1536]{1,0:T(8,128)(2,1)S(1)} fusion(bf16[1024,4608]{1,0:T(8,128)(2,1)S(1)} %get-tuple-element.324, bf16[1536,4608]{1,0:T(8,128)(2,1)} %all-gather.13.cloned.1.call-done.w_ref), kind=kOutput, calls=%fused_computation.16 | convolution fusion | flops 14497087488 | bytes 26738688 | tf_op jit(solution)/shard_map/dot_general | solution.py:31
  1299.9 13.6 collective-permute-done.111
  1319.3 12.6 collective-permute-done.113
  1333.2 7.2 collective-permute-start.115
  1341.7 17.7 %convolution_convert_fusion = bf16[1536,4608]{1,0:T(8,128)(2,1)} fusion(bf16[1024,1536]{1,0:T(8,128)(2,1)S(1)} %copy-done.4, bf16[1024,4608]{1,0:T(8,128)(2,1)S(1)} %get-tuple-element.324), kind=kOutput, calls=%fused_computation | convolution fusion | flops 14502592512 | bytes 26738688 | tf_op jit(solution)/shard_map/dot_general | solution.py:31
  1389.0 8.2 collective-permute-done.119
  1405.7 14.6 collective-permute-done.122
  1423.2 9.5 convolution_convert_fusion.2
  1498.1 14.0 collective-permute-done.130
  1519.8 27.0 %mixer_scan_back.3 = (bf16[1024,2048]{1,0:T(8,128)(2,1)}, f32[8,1024]{1,0:T(8,128)S(1)}, f32[8,1024]{1,0:T(8,128)S(1)}, f32[8,1024]{1,0:T(8,128)S(1)}, f32[8,128]{1,0:T(8,128)S(1)}) custom-call(f32[1024,1152]{1,0:T(8,128)} %copy-done, f32[1024,1152]{1,0:T(8,128)} %copy-done, f32[1024,1152]{1,0:T(8,128)} %copy-done, f32[1024,1152]{1,0:T(8,128)} %copy-done, ...), custom_call_target="tpu_custom_call" | custom-call | tf_op jit(solution)/shard_map/mixer_scan_back/pallas_call | solution.py:635
  1571.7 12.4 fusion.1
  1585.1 8.8 convolution_convert_fusion.4
  1607.7 9.2 collective-permute-done.133
  1643.5 8.5 collective-permute-start.137
  1656.1 9.4 collective-permute-done.137
  (1284 shorter events, 877.9 us)
Async XLA Ops:
  7.2 106.8 %all-gather.9.cloned.1.call-start = ((), (), s32[]{:S(2)}) async-start(), calls=%async_computation.8 | async-start | bytes 7077888 | tf_op jit(solution)/shard_map/all_gather | solution.py:852
  11.4 22.0 %collective-permute-start = (bf16[256,1536]{1,0:T(8,128)(2,1)}, bf16[256,1536]{1,0:T(8,128)(2,1)}, u32[]{:S(2)}, u32[]{:S(2)}) collective-permute-start(bf16[256,1536]{1,0:T(8,128)(2,1)} %multiply_convert_fusion.5), channel_id=1, source_target_pairs={{0,1},{1,2},{2,3},{4,5},{5,6},{6,7},{8,9},{9,10},{10,11},{12,13},{... | collective-permute-start | bytes 2359304 | tf_op jit(solution)/shard_map/ppermute | solution.py:75
  17.3 21.2 %collective-permute-start.1 = (bf16[256,1536]{1,0:T(8,128)(2,1)}, bf16[256,1536]{1,0:T(8,128)(2,1)}, u32[]{:S(2)}, u32[]{:S(2)}) collective-permute-start(bf16[256,1536]{1,0:T(8,128)(2,1)} %multiply_convert_fusion.5), channel_id=1, source_target_pairs={{1,0},{2,1},{3,2},{5,4},{6,5},{7,6},{9,8},{10,9},{11,10},{13,12},{... | collective-permute-start | bytes 2359304 | tf_op jit(solution)/shard_map/ppermute | solution.py:76
  52.6 150.6 %all-gather.11.cloned.1.call-start = ((), (), s32[]{:S(2)}) async-start(), calls=%async_computation.9 | async-start | bytes 2654208 | tf_op jit(solution)/shard_map/all_gather | solution.py:852
  54.8 333.0 %all-gather.13.cloned.1.call-start = ((), (), s32[]{:S(2)}) async-start(), calls=%async_computation.10 | async-start | bytes 15925248 | tf_op jit(solution)/shard_map/all_gather | solution.py:852
  58.3 35.1 %collective-permute-start.6 = (bf16[2,48,512]{2,1,0:T(8,128)(2,1)}, bf16[2,48,512]{2,1,0:T(8,128)(2,1)}, u32[]{:S(2)}, u32[]{:S(2)}) collective-permute-start(bf16[2,48,512]{2,1,0:T(8,128)(2,1)} %get-tuple-element.630), channel_id=1, source_target_pairs={{0,3},{1,2},{2,1},{3,0},{4,7},{5,6},{6,5},{7,4},{8,11},{9,10},{10,... | collective-permute-start | bytes 294920 | tf_op jit(solution)/shard_map/ppermute | solution.py:150
  59.4 34.0 %collective-permute-start.7 = (bf16[2,48,512]{2,1,0:T(8,128)(2,1)}, bf16[2,48,512]{2,1,0:T(8,128)(2,1)}, u32[]{:S(2)}, u32[]{:S(2)}) collective-permute-start(bf16[2,48,512]{2,1,0:T(8,128)(2,1)} %get-tuple-element.632), channel_id=1, source_target_pairs={{0,2},{1,3},{2,0},{3,1},{4,6},{5,7},{6,4},{7,5},{8,10},{9,11},{10,... | collective-permute-start | bytes 294920 | tf_op jit(solution)/shard_map/ppermute | solution.py:150
  59.4 34.0 %collective-permute-start.8 = (bf16[2,48,512]{2,1,0:T(8,128)(2,1)}, bf16[2,48,512]{2,1,0:T(8,128)(2,1)}, u32[]{:S(2)}, u32[]{:S(2)}) collective-permute-start(bf16[2,48,512]{2,1,0:T(8,128)(2,1)} %get-tuple-element.631), channel_id=1, source_target_pairs={{0,1},{1,0},{2,3},{3,2},{4,5},{5,4},{6,7},{7,6},{8,9},{9,8},{10,11... | collective-permute-start | bytes 294920 | tf_op jit(solution)/shard_map/ppermute | solution.py:150
  87.6 22.1 %collective-permute-start.4 = (bf16[256,1536]{1,0:T(8,128)(2,1)}, bf16[256,1536]{1,0:T(8,128)(2,1)}, u32[]{:S(2)}, u32[]{:S(2)}) collective-permute-start(bf16[256,1536]{1,0:T(8,128)(2,1)} %collective-permute-done.2), channel_id=1, source_target_pairs={{2,3},{6,7},{10,11},{14,15},{18,19},{22,23},{26,27},{30,31}} | collective-permute-start | bytes 2359304 | tf_op jit(solution)/shard_map/ppermute | solution.py:75
  89.1 20.5 %collective-permute-start.5 = (bf16[256,1536]{1,0:T(8,128)(2,1)}, bf16[256,1536]{1,0:T(8,128)(2,1)}, u32[]{:S(2)}, u32[]{:S(2)}) collective-permute-start(bf16[256,1536]{1,0:T(8,128)(2,1)} %collective-permute-done.3), channel_id=1, source_target_pairs={{1,0},{5,4},{9,8},{13,12},{17,16},{21,20},{25,24},{29,28}} | collective-permute-start | bytes 2359304 | tf_op jit(solution)/shard_map/ppermute | solution.py:76
  168.7 246.9 %all-gather.15.cloned.1.call-start = ((), (), s32[]{:S(2)}) async-start(), calls=%async_computation.11 | async-start | bytes 7962624 | tf_op jit(solution)/shard_map/all_gather | solution.py:852
  169.3 352.3 %all-gather.17.cloned.1.call-start = ((), (), s32[]{:S(2)}) async-start(), calls=%async_computation.12 | async-start | bytes 7077888 | tf_op jit(solution)/shard_map/all_gather | solution.py:852
  182.5 28.3 %collective-permute-start.19 = (bf16[256,1536]{1,0:T(8,128)(2,1)}, bf16[256,1536]{1,0:T(8,128)(2,1)}, u32[]{:S(2)}, u32[]{:S(2)}) collective-permute-start(bf16[256,1536]{1,0:T(8,128)(2,1)} %convert_element_type.980), channel_id=1, source_target_pairs={{0,1},{1,2},{2,3},{4,5},{5,6},{6,7},{8,9},{9,10},{10,11},{12,13},{... | collective-permute-start | bytes 2359304 | tf_op jit(solution)/shard_map/ppermute | solution.py:75
  189.6 21.2 %collective-permute-start.20 = (bf16[256,1536]{1,0:T(8,128)(2,1)}, bf16[256,1536]{1,0:T(8,128)(2,1)}, u32[]{:S(2)}, u32[]{:S(2)}) collective-permute-start(bf16[256,1536]{1,0:T(8,128)(2,1)} %convert_element_type.980), channel_id=1, source_target_pairs={{1,0},{2,1},{3,2},{5,4},{6,5},{7,6},{9,8},{10,9},{11,10},{13,12},{... | collective-permute-start | bytes 2359304 | tf_op jit(solution)/shard_map/ppermute | solution.py:76
  210.8 22.1 %collective-permute-start.23 = (bf16[256,1536]{1,0:T(8,128)(2,1)}, bf16[256,1536]{1,0:T(8,128)(2,1)}, u32[]{:S(2)}, u32[]{:S(2)}) collective-permute-start(bf16[256,1536]{1,0:T(8,128)(2,1)} %get-tuple-element.222), channel_id=1, source_target_pairs={{0,1},{4,5},{8,9},{12,13},{16,17},{20,21},{24,25},{28,29}} | collective-permute-start | bytes 2359304 | tf_op jit(solution)/shard_map/ppermute | solution.py:82
  219.0 21.7 %collective-permute-start.22 = (bf16[256,1536]{1,0:T(8,128)(2,1)}, bf16[256,1536]{1,0:T(8,128)(2,1)S(1)}, u32[]{:S(2)}, u32[]{:S(2)}) collective-permute-start(bf16[256,1536]{1,0:T(8,128)(2,1)} %collective-permute-done.20), channel_id=1, source_target_pairs={{1,0},{2,1},{5,4},{6,5},{9,8},{10,9},{13,12},{14,13},{17,16},{18,1... | collective-permute-start | bytes 2359304 | tf_op jit(solution)/shard_map/ppermute | solution.py:76
  240.7 24.3 %collective-permute-start.25 = (bf16[256,1536]{1,0:T(8,128)(2,1)}, bf16[256,1536]{1,0:T(8,128)(2,1)}, u32[]{:S(2)}, u32[]{:S(2)}) collective-permute-start(bf16[256,1536]{1,0:T(8,128)(2,1)} %get-tuple-element.224), channel_id=1, source_target_pairs={{0,1},{1,2},{4,5},{5,6},{8,9},{9,10},{12,13},{13,14},{16,17},{17,1... | collective-permute-start | bytes 2359304 | tf_op jit(solution)/shard_map/ppermute | solution.py:82
  243.2 21.8 %collective-permute-start.26 = (bf16[256,1536]{1,0:T(8,128)(2,1)}, bf16[256,1536]{1,0:T(8,128)(2,1)}, u32[]{:S(2)}, u32[]{:S(2)}) collective-permute-start(bf16[256,1536]{1,0:T(8,128)(2,1)} %get-tuple-element.225), channel_id=1, source_target_pairs={{2,1},{3,2},{6,5},{7,6},{10,9},{11,10},{14,13},{15,14},{18,17},{19... | collective-permute-start | bytes 2359304 | tf_op jit(solution)/shard_map/ppermute | solution.py:83
  261.6 22.3 %collective-permute-start.30 = (bf16[256,1536]{1,0:T(8,128)(2,1)S(1)}, bf16[256,1536]{1,0:T(8,128)(2,1)S(1)}, u32[]{:S(2)}, u32[]{:S(2)}) collective-permute-start(bf16[256,1536]{1,0:T(8,128)(2,1)S(1)} %collective-permute-done.22), channel_id=1, source_target_pairs={{1,0},{5,4},{9,8},{13,12},{17,16},{21,20},{25,24},{29,28}} | collective-permute-start | bytes 2359304 | tf_op jit(solution)/shard_map/ppermute | solution.py:76
  267.3 20.5 %collective-permute-start.27 = (bf16[256,1536]{1,0:T(8,128)(2,1)S(1)}, bf16[256,1536]{1,0:T(8,128)(2,1)S(1)}, u32[]{:S(2)}, u32[]{:S(2)}) collective-permute-start(bf16[256,1536]{1,0:T(8,128)(2,1)S(1)} %get-tuple-element.226), channel_id=1, source_target_pairs={{0,1},{1,2},{2,3},{4,5},{5,6},{6,7},{8,9},{9,10},{10,11},{12,13},{... | collective-permute-start | bytes 2359304 | tf_op jit(solution)/shard_map/ppermute | solution.py:82
  271.7 29.1 %collective-permute-start.28 = (bf16[256,1536]{1,0:T(8,128)(2,1)S(1)}, bf16[256,1536]{1,0:T(8,128)(2,1)S(1)}, u32[]{:S(2)}, u32[]{:S(2)}) collective-permute-start(bf16[256,1536]{1,0:T(8,128)(2,1)S(1)} %get-tuple-element.227), channel_id=1, source_target_pairs={{1,0},{2,1},{3,2},{5,4},{6,5},{7,6},{9,8},{10,9},{11,10},{13,12},{... | collective-permute-start | bytes 2359304 | tf_op jit(solution)/shard_map/ppermute | solution.py:83
  305.3 21.3 %collective-permute-start.32 = (bf16[256,1536]{1,0:T(8,128)(2,1)S(1)}, bf16[256,1536]{1,0:T(8,128)(2,1)S(1)}, u32[]{:S(2)}, u32[]{:S(2)}) collective-permute-start(bf16[256,1536]{1,0:T(8,128)(2,1)S(1)} %multiply_convert_fusion.4), channel_id=1, source_target_pairs={{1,0},{2,1},{3,2},{5,4},{6,5},{7,6},{9,8},{10,9},{11,10},{13,12},{... | collective-permute-start | bytes 2359304 | tf_op jit(solution)/shard_map/ppermute | solution.py:76
  328.2 21.8 %collective-permute-start.34 = (bf16[256,1536]{1,0:T(8,128)(2,1)S(1)}, bf16[256,1536]{1,0:T(8,128)(2,1)}, u32[]{:S(2)}, u32[]{:S(2)}) collective-permute-start(bf16[256,1536]{1,0:T(8,128)(2,1)S(1)} %collective-permute-done.32), channel_id=1, source_target_pairs={{1,0},{2,1},{5,4},{6,5},{9,8},{10,9},{13,12},{14,13},{17,16},{18,1... | collective-permute-start | bytes 2359304 | tf_op jit(solution)/shard_map/ppermute | solution.py:76
  350.1 22.3 %collective-permute-start.35 = (bf16[256,1536]{1,0:T(8,128)(2,1)}, bf16[256,1536]{1,0:T(8,128)(2,1)}, u32[]{:S(2)}, u32[]{:S(2)}) collective-permute-start(bf16[256,1536]{1,0:T(8,128)(2,1)} %collective-permute-done.33), channel_id=1, source_target_pairs={{2,3},{6,7},{10,11},{14,15},{18,19},{22,23},{26,27},{30,31}} | collective-permute-start | bytes 2359304 | tf_op jit(solution)/shard_map/ppermute | solution.py:75
  351.6 20.8 %collective-permute-start.36 = (bf16[256,1536]{1,0:T(8,128)(2,1)}, bf16[256,1536]{1,0:T(8,128)(2,1)}, u32[]{:S(2)}, u32[]{:S(2)}) collective-permute-start(bf16[256,1536]{1,0:T(8,128)(2,1)} %collective-permute-done.34), channel_id=1, source_target_pairs={{1,0},{5,4},{9,8},{13,12},{17,16},{21,20},{25,24},{29,28}} | collective-permute-start | bytes 2359304 | tf_op jit(solution)/shard_map/ppermute | solution.py:76
  354.5 22.4 %collective-permute-start.37 = (bf16[256,32]{0,1:T(8,128)(2,1)S(1)}, bf16[256,32]{0,1:T(8,128)(2,1)}, u32[]{:S(2)}, u32[]{:S(2)}) collective-permute-start(bf16[256,32]{0,1:T(8,128)(2,1)S(1)} %bitcast.424), channel_id=1, source_target_pairs={{0,1},{1,0},{2,3},{3,2},{4,5},{5,4},{6,7},{7,6},{8,9},{9,8},{10,11... | collective-permute-start | bytes 49160 | tf_op jit(solution)/shard_map/ppermute | solution.py:122
  376.7 229.4 %all-gather.19.cloned.1.call-start = ((), (), s32[]{:S(2)}) async-start(), calls=%async_computation.13 | async-start | bytes 2654208 | tf_op jit(solution)/shard_map/all_gather | solution.py:852
  521.3 232.5 %all-gather.23.cloned.1.call-start = ((), (), s32[]{:S(2)}) async-start(), calls=%async_computation.15 | async-start | bytes 15925248 | tf_op jit(solution)/shard_map/all_gather | solution.py:852
  587.7 193.8 %all-gather.21.cloned.1.call-start = ((), (), s32[]{:S(2)}) async-start(), calls=%async_computation.14 | async-start | bytes 7962624 | tf_op jit(solution)/shard_map/all_gather | solution.py:852
  588.4 460.9 %reduce-scatter.9.cloned.1.call-start = ((), (), s32[]{:S(2)}) async-start(), calls=%async_computation.16 | async-start | bytes 15925248 | tf_op jit(solution)/shard_map/reduce_scatter | solution.py:1020
  628.3 20.2 %collective-permute-start.61 = (bf16[256,1536]{1,0:T(8,128)(2,1)S(1)}, bf16[256,1536]{1,0:T(8,128)(2,1)S(1)}, u32[]{:S(2)}, u32[]{:S(2)}) collective-permute-start(bf16[256,1536]{1,0:T(8,128)(2,1)S(1)} %get-tuple-element.263), channel_id=1, source_target_pairs={{0,1},{1,2},{4,5},{5,6},{8,9},{9,10},{12,13},{13,14},{16,17},{17,1... | collective-permute-start | bytes 2359304 | tf_op jit(solution)/shard_map/ppermute | solution.py:82
  648.8 32.0 %collective-permute-start.63 = (bf16[256,1536]{1,0:T(8,128)(2,1)S(1)}, bf16[256,1536]{1,0:T(8,128)(2,1)S(1)}, u32[]{:S(2)}, u32[]{:S(2)}) collective-permute-start(bf16[256,1536]{1,0:T(8,128)(2,1)S(1)} %get-tuple-element.265), channel_id=1, source_target_pairs={{0,1},{1,2},{2,3},{4,5},{5,6},{6,7},{8,9},{9,10},{10,11},{12,13},{... | collective-permute-start | bytes 2359304 | tf_op jit(solution)/shard_map/ppermute | solution.py:82
  655.2 25.7 %collective-permute-start.64 = (bf16[256,1536]{1,0:T(8,128)(2,1)S(1)}, bf16[256,1536]{1,0:T(8,128)(2,1)S(1)}, u32[]{:S(2)}, u32[]{:S(2)}) collective-permute-start(bf16[256,1536]{1,0:T(8,128)(2,1)S(1)} %get-tuple-element.266), channel_id=1, source_target_pairs={{1,0},{2,1},{3,2},{5,4},{6,5},{7,6},{9,8},{10,9},{11,10},{13,12},{... | collective-permute-start | bytes 2359304 | tf_op jit(solution)/shard_map/ppermute | solution.py:83
  656.7 19.6 %collective-permute-start.57 = (f32[8,128]{1,0:T(8,128)S(1)}, f32[8,128]{1,0:T(8,128)S(1)}, u32[]{:S(2)}, u32[]{:S(2)}) collective-permute-start(f32[8,128]{1,0:T(8,128)S(1)} %bitcast.433), channel_id=1, source_target_pairs={{0,1},{1,0},{2,3},{3,2},{4,5},{5,4},{6,7},{7,6},{8,9},{9,8},{10,11... | collective-permute-start | bytes 12296 | tf_op jit(solution)/shard_map/ppermute | solution.py:113
  683.5 21.3 %collective-permute-start.66 = (bf16[256,1536]{1,0:T(8,128)(2,1)S(1)}, bf16[256,1536]{1,0:T(8,128)(2,1)S(1)}, u32[]{:S(2)}, u32[]{:S(2)}) collective-permute-start(bf16[256,1536]{1,0:T(8,128)(2,1)S(1)} %multiply_convert_fusion.2), channel_id=1, source_target_pairs={{1,0},{2,1},{3,2},{5,4},{6,5},{7,6},{9,8},{10,9},{11,10},{13,12},{... | collective-permute-start | bytes 2359304 | tf_op jit(solution)/shard_map/ppermute | solution.py:76
  705.5 21.3 %collective-permute-start.68 = (bf16[256,1536]{1,0:T(8,128)(2,1)S(1)}, bf16[256,1536]{1,0:T(8,128)(2,1)S(1)}, u32[]{:S(2)}, u32[]{:S(2)}) collective-permute-start(bf16[256,1536]{1,0:T(8,128)(2,1)S(1)} %collective-permute-done.66), channel_id=1, source_target_pairs={{1,0},{2,1},{5,4},{6,5},{9,8},{10,9},{13,12},{14,13},{17,16},{18,1... | collective-permute-start | bytes 2359304 | tf_op jit(solution)/shard_map/ppermute | solution.py:76
  727.6 19.9 %collective-permute-start.70 = (bf16[256,1536]{1,0:T(8,128)(2,1)S(1)}, bf16[256,1536]{1,0:T(8,128)(2,1)S(1)}, u32[]{:S(2)}, u32[]{:S(2)}) collective-permute-start(bf16[256,1536]{1,0:T(8,128)(2,1)S(1)} %collective-permute-done.68), channel_id=1, source_target_pairs={{1,0},{5,4},{9,8},{13,12},{17,16},{21,20},{25,24},{29,28}} | collective-permute-start | bytes 2359304 | tf_op jit(solution)/shard_map/ppermute | solution.py:76
  844.4 24.7 %collective-permute-start.73 = (bf16[256,1536]{1,0:T(8,128)(2,1)}, bf16[256,1536]{1,0:T(8,128)(2,1)}, u32[]{:S(2)}, u32[]{:S(2)}) collective-permute-start(bf16[256,1536]{1,0:T(8,128)(2,1)} %get-tuple-element.276), channel_id=1, source_target_pairs={{0,1},{1,2},{4,5},{5,6},{8,9},{9,10},{12,13},{13,14},{16,17},{17,1... | collective-permute-start | bytes 2359304 | tf_op jit(solution)/shard_map/ppermute | solution.py:82
  893.1 196.9 %reduce-scatter.11.cloned.1.call-start = ((), (), s32[]{:S(2)}) async-start(), calls=%async_computation.17 | async-start | bytes 7962624 | tf_op jit(solution)/shard_map/reduce_scatter | solution.py:1042
  939.6 21.1 %collective-permute-start.82 = (bf16[256,1536]{1,0:T(8,128)(2,1)S(1)}, bf16[256,1536]{1,0:T(8,128)(2,1)}, u32[]{:S(2)}, u32[]{:S(2)}) collective-permute-start(bf16[256,1536]{1,0:T(8,128)(2,1)S(1)} %collective-permute-done.80), channel_id=1, source_target_pairs={{1,0},{2,1},{5,4},{6,5},{9,8},{10,9},{13,12},{14,13},{17,16},{18,1... | collective-permute-start | bytes 2359304 | tf_op jit(solution)/shard_map/ppermute | solution.py:76
  981.6 201.0 %reduce-scatter.13.cloned.1.call-start = ((), (), s32[]{:S(2)}) async-start(), calls=%async_computation.18 | async-start | bytes 5308416 | tf_op jit(solution)/shard_map/reduce_scatter | solution.py:1058
  1011.1 34.6 %collective-permute-start.96 = (bf16[256,1536]{1,0:T(8,128)(2,1)}, bf16[256,1536]{1,0:T(8,128)(2,1)}, u32[]{:S(2)}, u32[]{:S(2)}) collective-permute-start(bf16[256,1536]{1,0:T(8,128)(2,1)} %get-tuple-element.298), channel_id=1, source_target_pairs={{0,1},{1,2},{2,3},{4,5},{5,6},{6,7},{8,9},{9,10},{10,11},{12,13},{... | collective-permute-start | bytes 2359304 | tf_op jit(solution)/shard_map/ppermute | solution.py:82
  1016.5 29.3 %collective-permute-start.97 = (bf16[256,1536]{1,0:T(8,128)(2,1)}, bf16[256,1536]{1,0:T(8,128)(2,1)}, u32[]{:S(2)}, u32[]{:S(2)}) collective-permute-start(bf16[256,1536]{1,0:T(8,128)(2,1)} %get-tuple-element.299), channel_id=1, source_target_pairs={{1,0},{2,1},{3,2},{5,4},{6,5},{7,6},{9,8},{10,9},{11,10},{13,12},{... | collective-permute-start | bytes 2359304 | tf_op jit(solution)/shard_map/ppermute | solution.py:83
  1082.9 170.1 %reduce-scatter.15.cloned.1.call-start = ((), (), s32[]{:S(2)}) async-start(), calls=%async_computation.19 | async-start | bytes 3981312 | tf_op jit(solution)/shard_map/reduce_scatter | solution.py:1089
  1102.7 20.4 %collective-permute-start.99 = (bf16[256,1536]{1,0:T(8,128)(2,1)S(1)}, bf16[256,1536]{1,0:T(8,128)(2,1)S(1)}, u32[]{:S(2)}, u32[]{:S(2)}) collective-permute-start(bf16[256,1536]{1,0:T(8,128)(2,1)S(1)} %get-tuple-element.541), channel_id=1, source_target_pairs={{0,1},{4,5},{8,9},{12,13},{16,17},{20,21},{24,25},{28,29}} | collective-permute-start | bytes 2359304 | tf_op jit(solution)/shard_map/ppermute | solution.py:82
  1124.4 21.1 %collective-permute-start.101 = (bf16[256,1536]{1,0:T(8,128)(2,1)}, bf16[256,1536]{1,0:T(8,128)(2,1)}, u32[]{:S(2)}, u32[]{:S(2)}) collective-permute-start(bf16[256,1536]{1,0:T(8,128)(2,1)} %get-tuple-element.310), channel_id=1, source_target_pairs={{0,1},{1,2},{4,5},{5,6},{8,9},{9,10},{12,13},{13,14},{16,17},{17,1... | collective-permute-start | bytes 2359304 | tf_op jit(solution)/shard_map/ppermute | solution.py:82
  1149.0 25.5 %collective-permute-start.103 = (bf16[256,1536]{1,0:T(8,128)(2,1)}, bf16[256,1536]{1,0:T(8,128)(2,1)}, u32[]{:S(2)}, u32[]{:S(2)}) collective-permute-start(bf16[256,1536]{1,0:T(8,128)(2,1)} %get-tuple-element.312), channel_id=1, source_target_pairs={{0,1},{1,2},{2,3},{4,5},{5,6},{6,7},{8,9},{9,10},{10,11},{12,13},{... | collective-permute-start | bytes 2359304 | tf_op jit(solution)/shard_map/ppermute | solution.py:82
  1157.2 22.4 %collective-permute-start.104 = (bf16[256,1536]{1,0:T(8,128)(2,1)}, bf16[256,1536]{1,0:T(8,128)(2,1)}, u32[]{:S(2)}, u32[]{:S(2)}) collective-permute-start(bf16[256,1536]{1,0:T(8,128)(2,1)} %get-tuple-element.313), channel_id=1, source_target_pairs={{1,0},{2,1},{3,2},{5,4},{6,5},{7,6},{9,8},{10,9},{11,10},{13,12},{... | collective-permute-start | bytes 2359304 | tf_op jit(solution)/shard_map/ppermute | solution.py:83
  1182.6 335.7 %reduce-scatter.17.cloned.1.call-start = ((), (), s32[]{:S(2)}) async-start(), calls=%async_computation.20 | async-start | bytes 15925248 | tf_op jit(solution)/shard_map/reduce_scatter | solution.py:1020
  1188.2 21.2 %collective-permute-start.106 = (bf16[256,1536]{1,0:T(8,128)(2,1)S(1)}, bf16[256,1536]{1,0:T(8,128)(2,1)S(1)}, u32[]{:S(2)}, u32[]{:S(2)}) collective-permute-start(bf16[256,1536]{1,0:T(8,128)(2,1)S(1)} %get-tuple-element.492), channel_id=1, source_target_pairs={{1,0},{2,1},{3,2},{5,4},{6,5},{7,6},{9,8},{10,9},{11,10},{13,12},{... | collective-permute-start | bytes 2359304 | tf_op jit(solution)/shard_map/ppermute | solution.py:76
  1210.1 20.4 %collective-permute-start.108 = (bf16[256,1536]{1,0:T(8,128)(2,1)S(1)}, bf16[256,1536]{1,0:T(8,128)(2,1)S(1)}, u32[]{:S(2)}, u32[]{:S(2)}) collective-permute-start(bf16[256,1536]{1,0:T(8,128)(2,1)S(1)} %collective-permute-done.106), channel_id=1, source_target_pairs={{1,0},{2,1},{5,4},{6,5},{9,8},{10,9},{13,12},{14,13},{17,16},{18,1... | collective-permute-start | bytes 2359304 | tf_op jit(solution)/shard_map/ppermute | solution.py:76
  1333.2 26.2 %collective-permute-start.115 = (bf16[256,1536]{1,0:T(8,128)(2,1)}, bf16[256,1536]{1,0:T(8,128)(2,1)}, u32[]{:S(2)}, u32[]{:S(2)}) collective-permute-start(bf16[256,1536]{1,0:T(8,128)(2,1)} %get-tuple-element.327), channel_id=1, source_target_pairs={{0,1},{1,2},{2,3},{4,5},{5,6},{6,7},{8,9},{9,10},{10,11},{12,13},{... | collective-permute-start | bytes 2359304 | tf_op jit(solution)/shard_map/ppermute | solution.py:82
  1362.5 209.2 %reduce-scatter.19.cloned.1.call-start = ((), (), s32[]{:S(2)}) async-start(), calls=%async_computation.21 | async-start | bytes 7962624 | tf_op jit(solution)/shard_map/reduce_scatter | solution.py:1042
  1440.6 233.1 %reduce-scatter.21.cloned.1.call-start = ((), (), s32[]{:S(2)}) async-start(), calls=%async_computation.22 | async-start | bytes 5308416 | tf_op jit(solution)/shard_map/reduce_scatter | solution.py:1058
  1494.2 22.7 %collective-permute-start.131 = (bf16[144,768]{1,0:T(8,128)(2,1)}, bf16[144,768]{1,0:T(8,128)(2,1)}, u32[]{:S(2)}, u32[]{:S(2)}) collective-permute-start(bf16[144,768]{1,0:T(8,128)(2,1)} %maximum_maximum_fusion.3), channel_id=1, source_target_pairs={{24,0},{28,4},{25,1},{29,5},{26,2},{30,6},{27,3},{31,7}} | collective-permute-start | bytes 663560 | tf_op jit(solution)/shard_map/ppermute | solution.py:195
  1546.8 24.3 %collective-permute-start.132 = (f32[8,1024]{1,0:T(8,128)S(1)}, f32[8,1024]{1,0:T(8,128)S(1)}, u32[]{:S(2)}, u32[]{:S(2)}) collective-permute-start(f32[8,1024]{1,0:T(8,128)S(1)} %get-tuple-element.346), channel_id=1, source_target_pairs={{4,0},{8,4},{12,8},{16,12},{20,16},{24,20},{28,24},{5,1},{9,5},{13... | collective-permute-start | bytes 98312 | tf_op jit(solution)/shard_map/ppermute | solution.py:195
  1561.4 39.7 %collective-permute-start.149 = (bf16[48,512]{1,0:T(8,128)(2,1)S(1)}, bf16[48,512]{1,0:T(8,128)(2,1)S(1)}, u32[]{:S(2)}, u32[]{:S(2)}) collective-permute-start(bf16[48,512]{1,0:T(8,128)(2,1)S(1)} %bitcast.429), channel_id=1, source_target_pairs={{0,3},{1,2},{2,1},{3,0},{4,7},{5,6},{6,5},{7,4},{8,11},{9,10},{10,... | collective-permute-start | bytes 147464 | tf_op jit(solution)/shard_map/ppermute | solution.py:150
  1561.6 41.2 %collective-permute-start.150 = (bf16[48,512]{1,0:T(8,128)(2,1)S(1)}, bf16[48,512]{1,0:T(8,128)(2,1)S(1)}, u32[]{:S(2)}, u32[]{:S(2)}) collective-permute-start(bf16[48,512]{1,0:T(8,128)(2,1)S(1)} %bitcast.427), channel_id=1, source_target_pairs={{0,2},{1,3},{2,0},{3,1},{4,6},{5,7},{6,4},{7,5},{8,10},{9,11},{10,... | collective-permute-start | bytes 147464 | tf_op jit(solution)/shard_map/ppermute | solution.py:150
  1561.8 41.0 %collective-permute-start.151 = (bf16[48,512]{1,0:T(8,128)(2,1)S(1)}, bf16[48,512]{1,0:T(8,128)(2,1)S(1)}, u32[]{:S(2)}, u32[]{:S(2)}) collective-permute-start(bf16[48,512]{1,0:T(8,128)(2,1)S(1)} %bitcast.428), channel_id=1, source_target_pairs={{0,1},{1,0},{2,3},{3,2},{4,5},{5,4},{6,7},{7,6},{8,9},{9,8},{10,11... | collective-permute-start | bytes 147464 | tf_op jit(solution)/shard_map/ppermute | solution.py:150
  1570.9 148.7 %reduce-scatter.23.cloned.1.call-start = ((), (), s32[]{:S(2)}) async-start(), calls=%async_computation.23 | async-start | bytes 3981312 | tf_op jit(solution)/shard_map/reduce_scatter | solution.py:1089
  1571.0 32.6 %collective-permute-start.144 = (f32[8,768]{1,0:T(8,128)S(1)}, f32[8,768]{1,0:T(8,128)S(1)}, u32[]{:S(2)}, u32[]{:S(2)}) collective-permute-start(f32[8,768]{1,0:T(8,128)S(1)} %fusion.173), channel_id=1, source_target_pairs={{0,8},{4,12},{8,0},{12,4},{16,24},{20,28},{24,16},{28,20},{1,9},{5... | collective-permute-start | bytes 73736 | tf_op jit(solution)/shard_map/ppermute | solution.py:113
  1620.0 20.2 %collective-permute-start.135 = (bf16[256,1536]{1,0:T(8,128)(2,1)}, bf16[256,1536]{1,0:T(8,128)(2,1)}, u32[]{:S(2)}, u32[]{:S(2)}) collective-permute-start(bf16[256,1536]{1,0:T(8,128)(2,1)} %get-tuple-element.353), channel_id=1, source_target_pairs={{0,1},{1,2},{4,5},{5,6},{8,9},{9,10},{12,13},{13,14},{16,17},{17,1... | collective-permute-start | bytes 2359304 | tf_op jit(solution)/shard_map/ppermute | solution.py:82
  1643.5 22.0 %collective-permute-start.137 = (bf16[256,1536]{1,0:T(8,128)(2,1)}, bf16[256,1536]{1,0:T(8,128)(2,1)}, u32[]{:S(2)}, u32[]{:S(2)}) collective-permute-start(bf16[256,1536]{1,0:T(8,128)(2,1)} %get-tuple-element.355), channel_id=1, source_target_pairs={{0,1},{1,2},{2,3},{4,5},{5,6},{6,7},{8,9},{9,10},{10,11},{12,13},{... | collective-permute-start | bytes 2359304 | tf_op jit(solution)/shard_map/ppermute | solution.py:82
  1677.8 19.6 %collective-permute-start.152 = (bf16[48,512]{1,0:T(8,128)(2,1)}, bf16[48,512]{1,0:T(8,128)(2,1)}, u32[]{:S(2)}, u32[]{:S(2)}) collective-permute-start(bf16[48,512]{1,0:T(8,128)(2,1)} %bitcast.132), channel_id=1, source_target_pairs={{0,3},{1,2},{2,1},{3,0},{4,7},{5,6},{6,5},{7,4},{8,11},{9,10},{10,... | collective-permute-start | bytes 147464 | tf_op jit(solution)/shard_map/ppermute | solution.py:150
  (363 other events, 5313.7 us)
Sparse Core Ops, SparseCore 0:
  52.7 44.3 all-gather.8
  99.5 29.0 all-gather.10
  168.9 83.1 all-gather.12
  254.4 48.8 all-gather.14
  376.8 43.0 all-gather.16
  521.4 34.7 all-gather.18
  587.8 81.1 all-gather.22
  670.8 48.8 all-gather.20
  893.3 101.4 reduce-scatter.8
  998.1 76.1 reduce-scatter.10
  1083.0 60.5 reduce-scatter.12
  1182.7 43.9 reduce-scatter.14
  1362.6 100.0 reduce-scatter.16
  1466.0 72.3 reduce-scatter.18
  1571.0 49.9 reduce-scatter.20
  1673.8 45.7 reduce-scatter.22

commit v2 on v1

--- a/solution.py
+++ b/solution.py
@@ -98,6 +98,33 @@
     return gathered, total, riders
 
 
+def choose(options, me):
+    out = options[0]
+    for m in range(1, len(options)):
+        out = jnp.where(me == m, options[m], out)
+    return out
+
+
+def gather_work(v, work, axis="tp"):
+    n, me = lax.axis_size(axis), lax.axis_index(axis)
+    near = [sorted((j for j in range(n) if j != m), key=lambda j: abs(j - m)) for m in range(n)]
+    right = left = block = v
+    at, state, rel = me, None, {0: v}
+    for d in range(1, n):
+        right = lax.ppermute(right, axis, [(i, i + 1) for i in range(d - 1, n - 1)])
+        left = lax.ppermute(left, axis, [(i, i - 1) for i in range(1, n - d + 1)])
+        state = work(block, at, state)
+        right, left, *state = tie(right, left, *state)
+        rel[-d], rel[d] = right, left
+        block = choose([rel[near[m][d - 1] - m] for m in range(n)], me)
+        at = choose([near[m][d - 1] for m in range(n)], me)
+    state = work(block, at, state)
+    whole_v = jnp.concatenate(
+        [choose([rel[j - m] for m in range(n)], me) for j in range(n)], 0
+    )
+    return whole_v, state
+
+
 def hop_gather(v):
     return hop_both(v, None)[0]
 
@@ -157,16 +184,20 @@
     return jnp.stack(outs, 0)
 
 
-def carried_state(through, state, direction):
+def carried_state(through, state, direction, *beside):
     n = lax.axis_size("seq")
+    rest = []
 
     def fetch(steps):
         high, low = split16(through)
         rows = [state.astype(bf16), high, low, jnp.zeros((14, state.shape[1]), bf16)]
         block = jnp.concatenate(rows, 0)
         got = []
-        for step in steps:
-            part = shift_seq(block, direction * step)
+        parts = [shift_seq(block, direction * step) for step in steps]
+        if window == 0:
+            parts = tie(*parts, *beside)
+            rest[:] = parts[len(steps) :]
+        for part in parts[: len(steps)]:
             decay = part[STATE : STATE + 1].astype(f32) + part[STATE + 1 : STATE + 2].astype(f32)
             got.append((decay, part[:STATE].astype(f32)))
         return got
@@ -186,7 +217,7 @@
             state = state + through * part
             through = through * decay
         window = reach
-    return state
+    return state, *rest
 
 
 def shift_seq(v, steps):
@@ -661,20 +692,39 @@
     )
 
 
-def up_kernel(x_ref, w_ref, gate_ref, pat_ref, h_ref, act_ref):
-    for start in range(0, x_ref.shape[0], ROW_TILE):
-        cut = slice(start, start + ROW_TILE)
-        hidden = mm(x_ref[cut, :], w_ref[...])
-        g, w = hidden[:, :FF_BLOCK], hidden[:, FF_BLOCK:]
-        gate = mm(gate_ref[cut, :], pat_ref[...])
-        h_ref[cut, :] = hidden.astype(bf16)
-        act_ref[cut, :] = (g * sigmoid(g) * w * gate).astype(bf16)
-
-
-def down_back_kernel(gs_ref, w_ref, h_ref, gate_ref, pat_ref, dh_ref, dgate_ref):
+def up_kernel(at_ref, x_ref, w_ref, router_ref, named_ref, pat_ref, *refs):
+    h_ref, act_ref, gates_ref, cols = refs[-4:]
+
+    @pl.when(pl.program_id(0) == 0)
+    def _():
+        logits = mm(x_ref[...], router_ref[...], NT)
+        mask = named_ref[...] > 0
+        peak = jnp.max(jnp.where(mask, logits, FAR), axis=1, keepdims=True)
+        raised = jnp.where(mask, jnp.exp(jnp.where(mask, logits - peak, 0.0)), 0.0)
+        gates = raised / jnp.sum(raised, axis=1, keepdims=True)
+        gates_ref[...] = gates
+        cols[...] = gate_columns(gates)
+
+    hidden = mm(x_ref[...], w_ref[...])
+    g, w = hidden[:, :FF_BLOCK], hidden[:, FF_BLOCK:]
+    gate = mm(cols[...], pat_ref[...])
+    h_ref[...] = hidden.astype(bf16)
+    act_ref[...] = (g * sigmoid(g) * w * gate).astype(bf16)
+
+
+def gate_columns(gates):
+    lane = lax.broadcasted_iota(jnp.int32, gates.shape, 1)
+    high, low = split16(jnp.where(lane == LANES - 1, 1.0, gates))
+    return jnp.concatenate([high, low], 1)
+
+
+def down_back_kernel(at_ref, gs_ref, w_ref, h_ref, gates_ref, pat_ref, *refs):
+    dh_ref, dgate_ref, cols = refs[-3:]
+
     @pl.when(pl.program_id(0) == 0)
     def _():
         dgate_ref[...] = jnp.zeros_like(dgate_ref)
+        cols[...] = gate_columns(gates_ref[...])
 
     for start in range(0, gs_ref.shape[0], ROW_TILE):
         cut = slice(start, start + ROW_TILE)
@@ -683,62 +733,88 @@
         w = h_ref[cut, FF_BLOCK:].astype(f32)
         sig = sigmoid(g)
         opened = g * sig
-        gate = mm(gate_ref[cut, :], pat_ref[...])
-        dgate_ref[cut, :] += mm((opened * w * q).astype(bf16), pat_ref[...], NT)
+        gate = mm(cols[cut, :], pat_ref[...])
+        dgate_ref[cut, :] += mm((opened * w * q).astype(bf16), pat_ref[:LANES, :], NT)
         d_act = gate * q
         dh_ref[cut, :FF_BLOCK] = (d_act * w * (sig * (1.0 + g * (1.0 - sig)))).astype(bf16)
         dh_ref[cut, FF_BLOCK:] = (d_act * opened).astype(bf16)
 
 
-def experts_up(x, w_up, gates, pattern):
-    rows, depth = x.shape
+def in_place(state, inputs):
+    held = [] if state is None else list(state)
+    specs = [pl.BlockSpec(memory_space=pl.ANY)] * len(held)
+    return held, specs, {inputs + 1 + i: i for i in range(len(held))}
+
+
+def experts_up(x, at, w_up, router_w, named, pattern, state):
+    own, depth = x.shape
+    rows = named.shape[0]
     blocks = w_up.shape[1] // (2 * FF_BLOCK)
+    held, specs, aliases = in_place(state, 5)
     return pl.pallas_call(
         up_kernel,
-        grid=(blocks,),
-        in_specs=[
-            whole((rows, depth)),
-            pl.BlockSpec((depth, 2 * FF_BLOCK), lambda i: (0, i)),
-            whole((rows, LANES)),
-            pl.BlockSpec((LANES, FF_BLOCK), lambda i: (0, i)),
-        ],
-        out_specs=[
-            pl.BlockSpec((rows, 2 * FF_BLOCK), lambda i: (0, i)),
-            pl.BlockSpec((rows, FF_BLOCK), lambda i: (0, i)),
-        ],
+        grid_spec=pltpu.PrefetchScalarGridSpec(
+            num_scalar_prefetch=1,
+            grid=(blocks,),
+            in_specs=[
+                pl.BlockSpec((own, depth), lambda i, at: (0, 0)),
+                pl.BlockSpec((depth, 2 * FF_BLOCK), lambda i, at: (0, i)),
+                pl.BlockSpec((LANES, depth), lambda i, at: (0, 0)),
+                pl.BlockSpec((own, LANES), lambda i, at: (at[0], 0)),
+                pl.BlockSpec((2 * LANES, FF_BLOCK), lambda i, at: (0, i)),
+            ]
+            + specs,
+            out_specs=[
+                pl.BlockSpec((own, 2 * FF_BLOCK), lambda i, at: (at[0], i)),
+                pl.BlockSpec((own, FF_BLOCK), lambda i, at: (at[0], i)),
+                pl.BlockSpec((own, LANES), lambda i, at: (at[0], 0)),
+            ],
+            scratch_shapes=[pltpu.VMEM((own, 2 * LANES), bf16)],
+        ),
         out_shape=[
             sds((rows, 2 * FF_BLOCK * blocks), bf16),
             sds((rows, FF_BLOCK * blocks), bf16),
-        ],
-        compiler_params=params(32),
+            sds((rows, LANES), f32),
+        ],
+        input_output_aliases=aliases,
+        compiler_params=params(58),
         name="experts_up",
-    )(x, w_up, gates, pattern)
-
-
-def experts_down_back(gs, w_down, hidden, gates, pattern):
-    rows, depth = gs.shape
+    )(at.astype(jnp.int32).reshape(1), x, w_up, router_w, named, pattern, *held)
+
+
+def experts_down_back(gs, at, w_down, hidden, gates, pattern, state):
+    depth = gs.shape[1]
+    rows = hidden.shape[0]
+    own = gs.shape[0]
     blocks = w_down.shape[0] // FF_BLOCK
+    held, specs, aliases = in_place(state, 5)
     return pl.pallas_call(
         down_back_kernel,
-        grid=(blocks,),
-        in_specs=[
-            whole((rows, depth)),
-            pl.BlockSpec((FF_BLOCK, depth), lambda i: (i, 0)),
-            pl.BlockSpec((rows, 2 * FF_BLOCK), lambda i: (0, i)),
-            whole((rows, LANES)),
-            pl.BlockSpec((LANES, FF_BLOCK), lambda i: (0, i)),
-        ],
-        out_specs=[
-            pl.BlockSpec((rows, 2 * FF_BLOCK), lambda i: (0, i)),
-            whole((rows, LANES)),
-        ],
+        grid_spec=pltpu.PrefetchScalarGridSpec(
+            num_scalar_prefetch=1,
+            grid=(blocks,),
+            in_specs=[
+                pl.BlockSpec((own, depth), lambda i, at: (0, 0)),
+                pl.BlockSpec((FF_BLOCK, depth), lambda i, at: (i, 0)),
+                pl.BlockSpec((own, 2 * FF_BLOCK), lambda i, at: (at[0], i)),
+                pl.BlockSpec((own, LANES), lambda i, at: (at[0], 0)),
+                pl.BlockSpec((2 * LANES, FF_BLOCK), lambda i, at: (0, i)),
+            ]
+            + specs,
+            out_specs=[
+                pl.BlockSpec((own, 2 * FF_BLOCK), lambda i, at: (at[0], i)),
+                pl.BlockSpec((own, LANES), lambda i, at: (at[0], 0)),
+            ],
+            scratch_shapes=[pltpu.VMEM((own, 2 * LANES), bf16)],
+        ),
         out_shape=[
             sds((rows, 2 * FF_BLOCK * blocks), bf16),
             sds((rows, LANES), f32),
         ],
-        compiler_params=params(32),
+        input_output_aliases=aliases,
+        compiler_params=params(32 if own == rows else 58),
         name="experts_down_back",
-    )(gs, w_down, hidden, gates, pattern)
+    )(at.astype(jnp.int32).reshape(1), gs, w_down, hidden, gates, pattern, *held)
 
 
 def row_norm(values):
@@ -811,9 +887,9 @@
     ex_row = jnp.arange(2 * LANES, dtype=jnp.int32)[:, None] % LANES
     ex = (ex_row == lane_head[None, :]).astype(bf16)
     unit = jnp.arange(hidden_units, dtype=jnp.int32) % per_seq
-    unit_gate = jnp.where(unit < mine * ff_cut, unit // ff_cut, mine)
-    pat_row = jnp.arange(LANES, dtype=jnp.int32)[:, None]
-    pattern = ((pat_row == unit_gate[None, :]) | (pat_row == 16 + unit_gate[None, :])).astype(bf16)
+    unit_gate = jnp.where(unit < mine * ff_cut, tp * mine + unit // ff_cut, LANES - 1)
+    pat_row = jnp.arange(2 * LANES, dtype=jnp.int32)[:, None] % LANES
+    pattern = (pat_row == unit_gate[None, :]).astype(bf16)
 
     inv1 = row_norm(tokens)
     scaled = (tokens * inv1).astype(bf16)
@@ -873,13 +949,14 @@
     named = pair_gather(
         jnp.transpose(named, (1, 0, 2)).reshape(own, layers * experts)
     ).reshape(rows, layers, experts)
+    named = jnp.pad(named, ((0, 0), (0, 0), (0, LANES - experts))).astype(f32)
 
     residual = tokens
     saved = []
     last_cot = None
     for l in range(layers):
         small_in = tie(w_in[l][:, inner + width + LANES :].astype(f32).T)[0]
-        router_w = small_in[:experts].astype(bf16)
+        router_w = jnp.pad(small_in[:experts], ((0, LANES - experts), (0, 0))).astype(bf16)
         gain1 = small_in[experts]
         gain2 = small_in[experts + 1]
         taps_bc = small_in[experts + 2].reshape(devices, fine)[:, : 4 * tap_cut]
@@ -902,12 +979,12 @@
         through = thr[0, 0:1]
         for c in range(1, chunks):
             through = through * thr[c, 0:1]
-        carried = carried_state(through, fin, 1)
         pz = mm(normed, w_in[l][:, :inner])
+        yi = mixer_intra(xs, bcs, lc, lt, dtv, aux, auxr, ex)
+        carried, pz, yi = carried_state(through, fin, 1, pz, yi)
         cot16 = cotangent.astype(bf16)
         if l == 0:
-            pz, cot16 = tie(pz, cot16)
-        yi = mixer_intra(xs, bcs, lc, lt, dtv, aux, auxr, ex)
+            carried, cot16 = tie(carried, cot16)
         carried, up_pack, down_pack = tie(carried, packs[l][2], packs[l][3])
         w_up[l], w_down[l] = over_seq(up_pack), over_seq(down_pack)
         y, gg, ss, st = mixer_read(pz, yi, xs, bcs, lc, aux, ex, ent, carried, thr, head_rows)
@@ -917,33 +994,25 @@
         ).reshape(own)
         partial_out = mm(gg, w_out[l], NT).astype(bf16)
         if l == 0:
-            last_cot, out_sum, _ = hop_both(cot16, partial_out)
+            last_cot, out_sum, (squares,) = hop_both(cot16, partial_out, (squares,))
             out_sum, last_cot = tie(out_sum, last_cot)
         else:
-            out_sum = hop_scatter(partial_out)
+            _, out_sum, (squares,) = hop_both(None, partial_out, (squares,))
         inv_gate = lax.rsqrt(squares / inner_all + epsilon)
         mixed = inv_gate[:, None] * out_sum
         mid = residual + mixed
 
         inv2 = row_norm(mid)
         moe_own = (mid * inv2 * gain2).astype(bf16)
-        moe_in = hop_gather(moe_own)
+        mask = named[:, l]
+
+        def up_block(block, at, state):
+            return experts_up(block, at, w_up[l], router_w, mask, pattern, state)
+
+        moe_in, (hidden, act, gates) = gather_work(moe_own, up_block)
         if l < layers - 1:
-            moe_in, *packs[l + 1] = tie(moe_in, *packs[l + 1])
+            act, *packs[l + 1][:2] = tie(act, *packs[l + 1][:2])
             w_in[l + 1], w_out[l + 1] = over_seq(packs[l + 1][0]), over_seq(packs[l + 1][1])
-        logits = mm(moe_in, router_w, NT)
-        mask = named[:, l] > 0
-        peak = jnp.max(jnp.where(mask, logits, FAR), axis=1, keepdims=True)
-        raised = jnp.where(mask, jnp.exp(jnp.where(mask, logits - peak, 0.0)), 0.0)
-        gates = raised / jnp.sum(raised, axis=1, keepdims=True)
-        gates_mine = lax.dynamic_slice_in_dim(gates, tp * mine, mine, 1)
-        gates_mine = jnp.concatenate([gates_mine, jnp.ones((rows, 1), f32)], 1)
-        high, low = split16(gates_mine)
-        gate_cols = jnp.concatenate(
-            [jnp.pad(part, ((0, 0), (0, 15 - mine))) for part in (high, low)], 1
-        )
-        gate_cols = jnp.pad(gate_cols, ((0, 0), (0, LANES - 32)))
-        hidden, act = experts_up(moe_in, w_up[l], gate_cols, pattern)
         saved.append(
             dict(
                 router_w=router_w, gain1=gain1, gain2=gain2, taps=taps, head=head,
@@ -951,11 +1020,14 @@
                 pu=pu, pz=pz, edge=edge, xs=xs, bcs=bcs, lc=lc, lt=lt, dtv=dtv, thr=thr,
                 through=through, y=y, gg=gg, st=st, inv_gate=inv_gate, mixed=mixed,
                 mid=mid, inv2=inv2, moe_own=moe_own, moe_in=moe_in, gates=gates,
-                gate_cols=gate_cols, hidden=hidden, act=act,
+                hidden=hidden, act=act,
             )
         )
         if l < layers - 1:
-            residual = mid + hop_scatter(mm(act, w_down[l]).astype(bf16))
+
+            moe_out = hop_scatter(mm(act, w_down[l]).astype(bf16))
+            moe_out, *packs[l + 1][2:] = tie(moe_out, *packs[l + 1][2:])
+            residual = mid + moe_out
 
     def finish(r):
         late, early, sums = r["late"], r["early"], r["sums"]
@@ -995,35 +1067,45 @@
     for l in reversed(range(layers)):
         k = saved[l]
         top = l == layers - 1
-        gs = last_cot if top else hop_gather(grad.astype(bf16))
-        if not top:
-            gs, above["late"] = tie(gs, above["late"])
+        state = None
+
+        def back_block(block, at, state):
+            return experts_down_back(
+                block, at, w_down[l], k["hidden"], k["gates"], pattern, state
+            )
+
+        def gate_sums():
+            lines = state[1][:, :experts].reshape(rows // per_line, LANES)
+            return pair_total(lines, "tp")
+
+        per_line = LANES // experts
+        if top:
+            gs = last_cot
+            last_out = mm(k["act"], w_down[l]).astype(bf16)
+            state = back_block(gs, jnp.int32(0), None)
         else:
-            last_out = mm(k["act"], w_down[l]).astype(bf16)
-        d_hidden, d_gate = experts_down_back(
-            gs, w_down[l], k["hidden"], k["gate_cols"], pattern
+            gs, state = gather_work(grad.astype(bf16), back_block)
+            first, above["late"] = tie(state[0], above["late"])
+            state = (first, state[1])
+        d_hidden = state[0]
+        up_part = mm(k["moe_in"], d_hidden, TN).astype(bf16)
+        _, d_moe, (d_gate_all, up_part) = hop_both(
+            None, mm(d_hidden, w_up[l], NT).astype(bf16), (gate_sums(), up_part)
         )
-        d_gate_all = jnp.zeros((rows, experts), f32)
-        d_gate_all = lax.dynamic_update_slice(d_gate_all, d_gate[:, :mine], (0, tp * mine))
-        per_line = LANES // experts
-        d_gate_all = pair_total(d_gate_all.reshape(rows // per_line, LANES), "tp")
+        up_grad = lax.psum_scatter(up_part, "seq", scatter_dimension=0, tiled=True)
+        down_part = mm(k["act"], gs, TN).astype(bf16)
+        if top:
+            d_moe, last_out = tie(d_moe, last_out)
         d_gate_own = lax.dynamic_slice_in_dim(
             d_gate_all, tp * (own // per_line), own // per_line, 0
         ).reshape(own, experts)
-        d_moe = hop_scatter(mm(d_hidden, w_up[l], NT).astype(bf16))
-        up_part = mm(k["moe_in"], d_hidden, TN).astype(bf16)
-        down_part = mm(k["act"], gs, TN).astype(bf16)
-        if top:
-            d_moe, up_part, last_out = tie(d_moe, up_part, last_out)
-        else:
-            d_moe, up_part = tie(d_moe, up_part)
-        up_grad = lax.psum_scatter(up_part, "seq", scatter_dimension=0, tiled=True)
+        d_gate_own = jnp.pad(d_gate_own, ((0, 0), (0, LANES - experts)))
         gates_own = lax.dynamic_slice_in_dim(k["gates"], tp * own, own, 0)
         d_logits = gates_own * (
             d_gate_own - jnp.sum(gates_own * d_gate_own, axis=1, keepdims=True)
         )
         d_logits16 = d_logits.astype(bf16)
-        router_grad = mm(k["moe_own"], d_logits16, TN)
+        router_grad = mm(k["moe_own"], d_logits16, TN)[:, :experts]
         d_moe = d_moe + mm(d_logits16, k["router_w"])
         gain2_grad = jnp.sum(d_moe * k["mid"] * k["inv2"], axis=0)
         grad_mid = grad + norm_back(k["mid"], k["inv2"], k["gain2"], d_moe)
@@ -1031,27 +1113,23 @@
         inv_gate = k["inv_gate"]
         cross = inv_gate * inv_gate * jnp.sum(grad_mid * k["mixed"], axis=1) / inner_all
         cross_all = pair_gather(to_line(cross)).reshape(nt, 8 * LANES)[:, :own].reshape(rows)
-        c2 = jnp.broadcast_to(cross_all[:, None], (rows, LANES))
         send = (grad_mid * inv_gate[:, None]).astype(bf16)
         if top:
-            d_mixed, moe_out, _ = hop_both(send, last_out)
+            d_mixed, moe_out, riders = hop_both(send, last_out, (cross_all, down_part))
             residual = k["mid"] + moe_out
         else:
-            d_mixed = hop_gather(send)
-        d_mixed, down_part = tie(d_mixed, down_part)
+            d_mixed, _, riders = hop_both(send, None, (cross_all, down_part))
+        cross_all, down_part = riders
         down_grad = lax.psum_scatter(down_part, "seq", scatter_dimension=0, tiled=True)
+        c2 = jnp.broadcast_to(cross_all[:, None], (rows, LANES))
         dg = mm(d_mixed, w_out[l])
         dy, dz, lg, fin, acc = mixer_gate_back(
             dg, k["pz"], k["y"], c2, k["head_rows"], k["xs"], k["bcs"], k["lc"], aux, ex, k["thr"]
         )
-        carried = carried_state(k["through"], fin, -1)
-        early = jnp.concatenate(
-            [
-                row_major(mm(d_mixed, k["gg"], TN).astype(bf16)),
-                row_major(mm(k["normed"], dz, TN).astype(bf16)),
-            ],
-            1,
-        )
+        early_out = row_major(mm(d_mixed, k["gg"], TN).astype(bf16))
+        early_z = row_major(mm(k["normed"], dz, TN).astype(bf16))
+        carried, early_out, early_z = carried_state(k["through"], fin, -1, early_out, early_z)
+        early = jnp.concatenate([early_out, early_z], 1)
         carried, early, up_grad = tie(carried, early, up_grad)
         if top:
             carried, residual = tie(carried, residual)
@@ -1065,15 +1143,6 @@
         dp, down_grad = tie(dp, down_grad)
         d_normed = mm(dp, w_in[l], NT)
         gain1_grad = jnp.sum(d_normed * k["plain"].astype(f32), axis=0)
-        if top:
-            d_own = hop_scatter(d_normed.astype(bf16))
-        else:
-            names = ("up", "down", "early", "late")
-            _, d_own, riders = hop_both(
-                None, d_normed.astype(bf16), [above[name] for name in names]
-            )
-            above.update(zip(names, riders))
-            finished[l + 1] = finish(above)
         taps_col = jnp.transpose(tacc[:4, inner:].reshape(4, devices, tap_cut), (1, 0, 2))
         taps_col = jnp.pad(taps_col.reshape(devices, 4 * tap_cut), ((0, 0), (0, fine - 4 * tap_cut)))
         small = jnp.concatenate(
@@ -1085,16 +1154,28 @@
             small, ((0, 0), (heads, LANES - heads - small.shape[1]))
         ).astype(bf16)
         late = lax.dynamic_update_slice(late, block, (0, width))
-        d_own, late, early = tie(d_own, late, early)
-        late = lax.psum_scatter(late, "seq", scatter_dimension=0, tiled=True)
-        sums = pair_total(
-            jnp.concatenate(
-                [tacc[:4, :inner], acc[:2], pad_rows([hacc[:2].reshape(-1)], 2, inner)], 0
-            ),
-            "seq",
+        sums = jnp.concatenate(
+            [tacc[:4, :inner], acc[:2], pad_rows([hacc[:2].reshape(-1)], 2, inner)], 0
         )
+        names = ("up", "down", "early", "sums")
+        now = dict(up=up_grad, down=down_grad, early=early, sums=sums)
+        held = [late]
+        if not top:
+            held += [now[name] for name in names] + [above[name] for name in names]
+            held += [above["late"]]
+        _, d_own, riders = hop_both(None, d_normed.astype(bf16), held)
+        late = lax.psum_scatter(riders[0], "seq", scatter_dimension=0, tiled=True)
+        if top:
+            d_own, now["early"] = tie(d_own, early)
+        else:
+            now.update(zip(names, riders[1:5]))
+            above.update(zip(names, riders[5:9]))
+            above["late"] = riders[9]
+            both = pair_total(jnp.concatenate([now["sums"], above["sums"]], 0), "seq")
+            now["sums"], above["sums"] = both[: sums.shape[0]], both[sums.shape[0] :]
+            finished[l + 1] = finish(above)
         grad = grad_mid + norm_back(k["residual"], k["inv1"], k["gain1"], d_own)
-        above = dict(up=up_grad, down=down_grad, early=early, late=late, sums=sums)
+        above = dict(now, late=late)
 
     finished[0] = finish(above)
     stacked = [jnp.stack([part[i] for part in finished], 0).astype(f32) for i in range(16)]

time: 1750 us -> 1620 us (0.926)
  waiting for transfers between devices: 666 us -> 434 us
  Pallas kernels: 177 us -> 260 us
  starting transfers between devices: 312 us -> 338 us
  local copies, waits for them, and re-layouts: 191 us -> 173 us
    ppermute x24 -> x15, waiting for transfers between devices: 210 us -> 119 us  [hop_both(): lax.ppermute(held[1], axis, [(i, i - 1) for i in range(1, n - step + 1)])]
    pallas_call x4 -> x13, Pallas kernels: 84.1 us -> 167 us  [the longest x8 102 us: experts_up(): pl.pallas_call(up_kernel, grid_spec=pltpu.PrefetchScalarGridSpec(num_scal...]
    ppermute x24 -> x15, waiting for transfers between devices: 82.1 us -> 2.67 us  [hop_both(): lax.ppermute(held[0], axis, [(i, i + 1) for i in range(step - 1, n - 1)])]
    ppermute x24, waiting for transfers between devices: 178 us -> 135 us  [hop_both(): right = lax.ppermute(held[0], axis, [(i, i + 1) for i in range(0, s)])]
    ppermute x14 -> x11, waiting for transfers between devices: 63.3 us -> 22 us  [pair_total(): v = v + lax.ppermute(v, axis, [(i, i ^ bit) for i in range(n)])]
    ppermute x0 -> x18, starting transfers between devices: none -> 34 us  [the longest x9 21.5 us: gather_work(): right = lax.ppermute(right, axis, [(i, i + 1) for i in range(d - 1, n - 1)])]
    select_n x1 -> x10, other arithmetic: 0.02 us -> 21.3 us  [the longest x9 21.3 us: choose(): out = jnp.where(me == m, options[m], out)]
    ppermute x0 -> x18, waiting for transfers between devices: none -> 18.5 us  [the longest x9 17.3 us: gather_work(): left = lax.ppermute(left, axis, [(i, i - 1) for i in range(1, n - d + 1)])]
  transfers between devices with their start and end apart: 171 -> 168, of which waited for: 88 -> 62; matrix products, arithmetic and copies ran while one was open for 25% -> 29% of each run, Pallas kernels for 8% -> 15%
where the time goes in v2:
time: 1620 us; the launch traced here: 1600 us
  waiting for transfers between devices  434 us (27%)
  starting transfers between devices  338 us (21%)
  Pallas kernels  260 us (16%)
  matrix products  216 us (13%)
  local copies, waits for them, and re-layouts  173 us (11%)
  other arithmetic  159 us (10%)
  between operations  20.5 us (1%)
    dot_general x28, matrix products, mm(): lax.dot_general(a, b, dims, precision=precision, preferred_element_type=f32)  216 us
    ppermute x24, waiting for transfers between devices, hop_both(): right = lax.ppermute(held[0], axis, [(i, i + 1) for i in range(0, s)])  135 us
    ppermute x15, waiting for transfers between devices, hop_both(): lax.ppermute(held[1], axis, [(i, i - 1) for i in range(1, n - step + 1)])  119 us
    ppermute x24, starting transfers between devices, hop_both(): right = lax.ppermute(held[0], axis, [(i, i + 1) for i in range(0, s)])  113 us
    pallas_call x8, Pallas kernels, experts_up(): pl.pallas_call(up_kernel, grid_spec=pltpu.PrefetchScalarGridSpec(num_scal...  102 us
    pallas_call x5, Pallas kernels, experts_down_back(): pl.pallas_call(down_back_kernel, grid_spec=pltpu.PrefetchScalarGridSpec(n...  65.3 us
    ppermute x24, starting transfers between devices, shift_seq(): return lax.ppermute(v, 'seq', [(i, i + steps) for i in range(first, last)])  60.8 us
    unnamed x587, local copies, waits for them, and re-layouts  58 us
  transfers between devices with their start and end apart: 168, of which 62 were waited for; matrix products, arithmetic and copies ran while one was open for 29% of the time, Pallas kernels for 15%

profile of v2, /device:TPU:0, one launch (start us, length us, event | category | flops | bytes accessed | tf_op | source)
XLA Modules:
  0.0 1601.2 jit_solution(4846601152632697107)
XLA Ops:
  12.7 6.5 collective-permute-start
  26.0 8.2 collective-permute-done.1
  76.4 7.6 collective-permute-done.3
  113.0 7.2 fusion.6.u_ref.bc_ref.dt_ref.uh_ref.bch_ref
  122.4 6.6 mixer_states.2
  171.2 6.5 collective-permute-start.17
  209.3 10.8 collective-permute-done.33
  264.2 7.0 collective-permute-done.28
  282.7 12.7 experts_up.8
  299.8 12.6 experts_up.9
  318.0 12.6 experts_up.10
  335.1 12.6 experts_up.11
  347.9 11.1 convolution_convert_fusion.10
  364.8 12.6 collective-permute-done.39
  383.1 9.8 collective-permute-done.41
  394.5 7.3 collective-permute-start.43
  427.8 8.0 collective-permute-done.46
  439.2 29.3 %collective-permute-done.48 = bf16[256,1536]{1,0:T(8,128)(2,1)} collective-permute-done((bf16[256,1536]{1,0:T(8,128)(2,1)S(1)}, bf16[256,1536]{1,0:T(8,128)(2,1)}, u32[]{:S(2)}, u32[]{:S(2)}) %collective-permute-start.48) | collective-permute-done | bytes 786464 | tf_op jit(solution)/shard_map/ppermute | solution.py:76
  471.7 12.5 collective-permute-done.50
  490.5 8.3 fusion.4.u_ref.bc_ref.dt_ref.uh_ref.bch_ref
  501.0 6.6 mixer_states.3
  508.0 17.2 %collective-permute-start.54 = (bf16[144,768]{1,0:T(8,128)(2,1)S(1)}, bf16[144,768]{1,0:T(8,128)(2,1)S(1)}, u32[]{:S(2)}, u32[]{:S(2)}) collective-permute-start(bf16[144,768]{1,0:T(8,128)(2,1)S(1)} %fusion.52), channel_id=1, source_target_pairs={{0,12},{4,16},{8,20},{12,24},{16,28},{1,13},{5,17},{9,21},{13,25},... | collective-permute-start | bytes 663560 | tf_op jit(solution)/shard_map/ppermute | solution.py:226
  581.0 16.0 collective-permute-done.59
  607.3 13.5 collective-permute-done.61
  628.9 12.1 collective-permute-done.63
  653.9 13.0 experts_up.12
  671.0 12.8 experts_up.13
  687.3 12.7 experts_up.14
  704.3 12.8 experts_up.15
  723.0 23.0 %experts_down_back.5 = (bf16[1024,4608]{1,0:T(8,128)(2,1)S(1)}, f32[1024,128]{1,0:T(8,128)S(1)}) custom-call(s32[1]{0:T(128)} %constant.179.clone.1.at_ref, bf16[1024,1536]{1,0:T(8,128)(2,1)S(1)} %copy-done.11, bf16[2304,1536]{1,0:T(8,128)(2,1)S(1)} %copy-done.25, bf16[1024,4608]{1,0:T(8,128)(2,1)} %get-tuple-element.410.h_ref, f32[1024,128]{1,0:T(8,128)S(1)} %copy-done.19, ...), custom_call_target="tpu_custom_call" | custom-call | tf_op jit(solution)/shard_map/experts_down_back/pallas_call | solution.py:791
  752.2 21.5 %convolution_convert_fusion.7 = bf16[1024,1536]{1,0:T(8,128)(2,1)S(1)} fusion(bf16[1024,4608]{1,0:T(8,128)(2,1)} %copy-done.80, bf16[1536,4608]{1,0:T(8,128)(2,1)} %all-gather.23.cloned.1.call-done.w_ref), kind=kOutput, calls=%fused_computation.17 | convolution fusion | flops 14497087488 | bytes 26738688 | tf_op jit(solution)/shard_map/dot_general | solution.py:31
  779.2 17.7 %convolution_convert_fusion.1 = bf16[1536,4608]{1,0:T(8,128)(2,1)} fusion(bf16[1024,4608]{1,0:T(8,128)(2,1)S(1)} %copy-done.81, bf16[256,1536]{1,0:T(8,128)(2,1)S(1)} %copy-done.170, bf16[256,1536]{1,0:T(8,128)(2,1)S(1)} %copy-done.169, bf16[256,1536]{1,0:T(8,128)(2,1)S(1)} %copy-done.168, bf16[256,1536]{1,0:T(8,128)(2,1)S(1)} %copy-done.167), kind=kOutput, calls=%fused_computation.1 | convolution fusion | flops 14515175424 | bytes 26738688 | tf_op jit(solution)/shard_map/dot_general | solution.py:31
  800.0 6.6 collective-permute-start.75
  808.2 11.7 convolution_convert_fusion.3
  829.0 13.1 convolution_convert_fusion.8
  859.9 9.4 collective-permute-done.82
  877.7 7.0 collective-permute-done.85
  886.5 11.6 collective-permute-done.84
  905.6 7.2 collective-permute-done.88
  947.9 17.5 %collective-permute-done.92 = bf16[144,768]{1,0:T(8,128)(2,1)S(1)} collective-permute-done((bf16[144,768]{1,0:T(8,128)(2,1)S(1)}, bf16[144,768]{1,0:T(8,128)(2,1)S(1)}, u32[]{:S(2)}, u32[]{:S(2)}) %collective-permute-start.92) | collective-permute-done | bytes 221216 | tf_op jit(solution)/shard_map/ppermute | solution.py:226
  972.6 27.1 %mixer_scan_back.2 = (bf16[1024,2048]{1,0:T(8,128)(2,1)}, f32[8,1024]{1,0:T(8,128)S(1)}, f32[8,1024]{1,0:T(8,128)S(1)}, f32[8,1024]{1,0:T(8,128)S(1)}, f32[8,128]{1,0:T(8,128)S(1)}) custom-call(f32[1024,1152]{1,0:T(8,128)} %copy-done.1, f32[1024,1152]{1,0:T(8,128)} %copy-done.1, f32[1024,1152]{1,0:T(8,128)} %copy-done.1, f32[1024,1152]{1,0:T(8,128)} %copy-done.1, ...), custom_call_target="tpu_custom_call" | custom-call | tf_op jit(solution)/shard_map/mixer_scan_back/pallas_call | solution.py:666
  1003.4 11.7 fusion.3
  1030.0 9.7 collective-permute-done.99
  1046.5 16.0 collective-permute-done.101
  1064.1 7.5 collective-permute-start.103
  1072.9 14.0 collective-permute-done.103
  1104.8 10.6 experts_down_back.6
  1122.9 10.6 experts_down_back.7
  1133.4 8.0 collective-permute-done.108
  1145.5 10.6 experts_down_back.8
  1164.5 10.5 experts_down_back.9
  1176.4 20.5 %convolution_convert_fusion.6 = bf16[1024,1536]{1,0:T(8,128)(2,1)S(1)} fusion(bf16[1024,4608]{1,0:T(8,128)(2,1)} %get-tuple-element.482, bf16[1536,4608]{1,0:T(8,128)(2,1)} %all-gather.13.cloned.1.call-done.w_ref), kind=kOutput, calls=%fused_computation.16 | convolution fusion | flops 14497087488 | bytes 26738688 | tf_op jit(solution)/shard_map/dot_general | solution.py:31
  1207.7 17.8 %convolution_convert_fusion = bf16[1536,4608]{1,0:T(8,128)(2,1)} fusion(bf16[1024,4608]{1,0:T(8,128)(2,1)S(1)} %copy-done.86, bf16[256,1536]{1,0:T(8,128)(2,1)S(1)} %copy-done.158, bf16[256,1536]{1,0:T(8,128)(2,1)S(1)} %copy-done.157, bf16[256,1536]{1,0:T(8,128)(2,1)S(1)} %copy-done.156, bf16[256,1536]{1,0:T(8,128)(2,1)S(1)} %copy-done.155), kind=kOutput, calls=%fused_computation | convolution fusion | flops 14515175424 | bytes 26738688 | tf_op jit(solution)/shard_map/dot_general | solution.py:31
  1231.2 11.9 collective-permute-done.115
  1246.2 10.5 collective-permute-start.117
  1283.1 9.5 convolution_convert_fusion.2
  1295.9 19.6 %collective-permute-done.124 = bf16[256,1536]{1,0:T(8,128)(2,1)S(1)} collective-permute-done((bf16[256,1536]{1,0:T(8,128)(2,1)}, bf16[256,1536]{1,0:T(8,128)(2,1)S(1)}, u32[]{:S(2)}, u32[]{:S(2)}) %collective-permute-start.124) | collective-permute-done | bytes 786464 | tf_op jit(solution)/shard_map/ppermute | solution.py:76
  1317.4 12.6 collective-permute-done.126
  1359.2 13.1 collective-permute-done.130
  1379.8 27.1 %mixer_scan_back.3 = (bf16[1024,2048]{1,0:T(8,128)(2,1)}, f32[8,1024]{1,0:T(8,128)S(1)}, f32[8,1024]{1,0:T(8,128)S(1)}, f32[8,1024]{1,0:T(8,128)S(1)}, f32[8,128]{1,0:T(8,128)S(1)}) custom-call(f32[1024,1152]{1,0:T(8,128)} %copy-done, f32[1024,1152]{1,0:T(8,128)} %copy-done, f32[1024,1152]{1,0:T(8,128)} %copy-done, f32[1024,1152]{1,0:T(8,128)} %copy-done, ...), custom_call_target="tpu_custom_call" | custom-call | tf_op jit(solution)/shard_map/mixer_scan_back/pallas_call | solution.py:666
  1412.5 11.1 fusion.1
  1446.8 16.9 %reduce-scatter.21.cloned.1.call-done = bf16[192,1536]{1,0:T(8,128)(2,1)} async-done(((bf16[1536,1536]{1,0:T(8,128)(2,1)}), bf16[192,1536]{1,0:T(8,128)(2,1)}) %reduce-scatter.21.cloned.1.call-update) | async-done | bytes 589840 | tf_op jit(solution)/shard_map/reduce_scatter | solution.py:1136
  1539.2 6.7 collective-permute-done.142
  1559.7 11.4 collective-permute-done.137
  (1326 shorter events, 783.1 us)
Async XLA Ops:
  7.2 104.0 %all-gather.9.cloned.1.call-start = ((), (), s32[]{:S(2)}) async-start(), calls=%async_computation.8 | async-start | bytes 7077888 | tf_op jit(solution)/shard_map/all_gather | solution.py:928
  11.4 22.8 %collective-permute-start.1 = (bf16[256,1536]{1,0:T(8,128)(2,1)}, bf16[256,1536]{1,0:T(8,128)(2,1)}, u32[]{:S(2)}, u32[]{:S(2)}) collective-permute-start(bf16[256,1536]{1,0:T(8,128)(2,1)} %multiply_convert_fusion.5), channel_id=1, source_target_pairs={{1,0},{2,1},{3,2},{5,4},{6,5},{7,6},{9,8},{10,9},{11,10},{13,12},{... | collective-permute-start | bytes 2359304 | tf_op jit(solution)/shard_map/ppermute | solution.py:76
  12.7 22.7 %collective-permute-start = (bf16[256,1536]{1,0:T(8,128)(2,1)}, bf16[256,1536]{1,0:T(8,128)(2,1)}, u32[]{:S(2)}, u32[]{:S(2)}) collective-permute-start(bf16[256,1536]{1,0:T(8,128)(2,1)} %multiply_convert_fusion.5), channel_id=1, source_target_pairs={{0,1},{1,2},{2,3},{4,5},{5,6},{6,7},{8,9},{9,10},{10,11},{12,13},{... | collective-permute-start | bytes 2359304 | tf_op jit(solution)/shard_map/ppermute | solution.py:75
  51.1 142.1 %all-gather.11.cloned.1.call-start = ((), (), s32[]{:S(2)}) async-start(), calls=%async_computation.9 | async-start | bytes 2654208 | tf_op jit(solution)/shard_map/all_gather | solution.py:928
  53.1 229.6 %all-gather.13.cloned.1.call-start = ((), (), s32[]{:S(2)}) async-start(), calls=%async_computation.10 | async-start | bytes 15925248 | tf_op jit(solution)/shard_map/all_gather | solution.py:928
  57.5 32.3 %collective-permute-start.6 = (bf16[2,48,512]{2,1,0:T(8,128)(2,1)}, bf16[2,48,512]{2,1,0:T(8,128)(2,1)S(1)}, u32[]{:S(2)}, u32[]{:S(2)}) collective-permute-start(bf16[2,48,512]{2,1,0:T(8,128)(2,1)} %get-tuple-element.804), channel_id=1, source_target_pairs={{0,3},{1,2},{2,1},{3,0},{4,7},{5,6},{6,5},{7,4},{8,11},{9,10},{10,... | collective-permute-start | bytes 294920 | tf_op jit(solution)/shard_map/ppermute | solution.py:177
  61.1 28.8 %collective-permute-start.8 = (bf16[2,48,512]{2,1,0:T(8,128)(2,1)}, bf16[2,48,512]{2,1,0:T(8,128)(2,1)}, u32[]{:S(2)}, u32[]{:S(2)}) collective-permute-start(bf16[2,48,512]{2,1,0:T(8,128)(2,1)} %get-tuple-element.805), channel_id=1, source_target_pairs={{0,1},{1,0},{2,3},{3,2},{4,5},{5,4},{6,7},{7,6},{8,9},{9,8},{10,11... | collective-permute-start | bytes 294920 | tf_op jit(solution)/shard_map/ppermute | solution.py:177
  61.1 29.4 %collective-permute-start.7 = (bf16[2,48,512]{2,1,0:T(8,128)(2,1)}, bf16[2,48,512]{2,1,0:T(8,128)(2,1)}, u32[]{:S(2)}, u32[]{:S(2)}) collective-permute-start(bf16[2,48,512]{2,1,0:T(8,128)(2,1)} %get-tuple-element.806), channel_id=1, source_target_pairs={{0,2},{1,3},{2,0},{3,1},{4,6},{5,7},{6,4},{7,5},{8,10},{9,11},{10,... | collective-permute-start | bytes 294920 | tf_op jit(solution)/shard_map/ppermute | solution.py:177
  63.5 20.5 %collective-permute-start.3 = (bf16[256,1536]{1,0:T(8,128)(2,1)}, bf16[256,1536]{1,0:T(8,128)(2,1)}, u32[]{:S(2)}, u32[]{:S(2)}) collective-permute-start(bf16[256,1536]{1,0:T(8,128)(2,1)} %collective-permute-done.1), channel_id=1, source_target_pairs={{1,0},{2,1},{5,4},{6,5},{9,8},{10,9},{13,12},{14,13},{17,16},{18,1... | collective-permute-start | bytes 2359304 | tf_op jit(solution)/shard_map/ppermute | solution.py:76
  84.0 22.7 %collective-permute-start.4 = (bf16[256,1536]{1,0:T(8,128)(2,1)}, bf16[256,1536]{1,0:T(8,128)(2,1)}, u32[]{:S(2)}, u32[]{:S(2)}) collective-permute-start(bf16[256,1536]{1,0:T(8,128)(2,1)} %collective-permute-done.2), channel_id=1, source_target_pairs={{2,3},{6,7},{10,11},{14,15},{18,19},{22,23},{26,27},{30,31}} | collective-permute-start | bytes 2359304 | tf_op jit(solution)/shard_map/ppermute | solution.py:75
  85.6 21.2 %collective-permute-start.5 = (bf16[256,1536]{1,0:T(8,128)(2,1)}, bf16[256,1536]{1,0:T(8,128)(2,1)}, u32[]{:S(2)}, u32[]{:S(2)}) collective-permute-start(bf16[256,1536]{1,0:T(8,128)(2,1)} %collective-permute-done.3), channel_id=1, source_target_pairs={{1,0},{5,4},{9,8},{13,12},{17,16},{21,20},{25,24},{29,28}} | collective-permute-start | bytes 2359304 | tf_op jit(solution)/shard_map/ppermute | solution.py:76
  129.3 24.4 %collective-permute-start.14 = (bf16[144,768]{1,0:T(8,128)(2,1)S(1)}, bf16[144,768]{1,0:T(8,128)(2,1)S(1)}, u32[]{:S(2)}, u32[]{:S(2)}) collective-permute-start(bf16[144,768]{1,0:T(8,128)(2,1)S(1)} %fusion.54), channel_id=1, source_target_pairs={{0,12},{4,16},{8,20},{12,24},{16,28},{1,13},{5,17},{9,21},{13,25},... | collective-permute-start | bytes 663560 | tf_op jit(solution)/shard_map/ppermute | solution.py:226
  165.9 182.0 %all-gather.15.cloned.1.call-start = ((), (), s32[]{:S(2)}) async-start(), calls=%async_computation.11 | async-start | bytes 7962624 | tf_op jit(solution)/shard_map/all_gather | solution.py:928
  166.4 322.1 %all-gather.17.cloned.1.call-start = ((), (), s32[]{:S(2)}) async-start(), calls=%async_computation.12 | async-start | bytes 7077888 | tf_op jit(solution)/shard_map/all_gather | solution.py:928
  169.9 32.7 %collective-permute-start.18 = (bf16[256,1536]{1,0:T(8,128)(2,1)}, bf16[256,1536]{1,0:T(8,128)(2,1)}, u32[]{:S(2)}, u32[]{:S(2)}) collective-permute-start(bf16[256,1536]{1,0:T(8,128)(2,1)} %convert_element_type.996), channel_id=1, source_target_pairs={{1,0},{2,1},{3,2},{5,4},{6,5},{7,6},{9,8},{10,9},{11,10},{13,12},{... | collective-permute-start | bytes 2359304 | tf_op jit(solution)/shard_map/ppermute | solution.py:76
  171.2 31.4 %collective-permute-start.17 = (bf16[256,1536]{1,0:T(8,128)(2,1)}, bf16[256,1536]{1,0:T(8,128)(2,1)}, u32[]{:S(2)}, u32[]{:S(2)}) collective-permute-start(bf16[256,1536]{1,0:T(8,128)(2,1)} %convert_element_type.996), channel_id=1, source_target_pairs={{0,1},{1,2},{2,3},{4,5},{5,6},{6,7},{8,9},{9,10},{10,11},{12,13},{... | collective-permute-start | bytes 2359304 | tf_op jit(solution)/shard_map/ppermute | solution.py:75
  202.6 21.9 %collective-permute-start.23 = (bf16[256,1536]{1,0:T(8,128)(2,1)}, bf16[256,1536]{1,0:T(8,128)(2,1)S(1)}, u32[]{:S(2)}, u32[]{:S(2)}) collective-permute-start(bf16[256,1536]{1,0:T(8,128)(2,1)} %get-tuple-element.311), channel_id=1, source_target_pairs={{0,1},{4,5},{8,9},{12,13},{16,17},{20,21},{24,25},{28,29}} | collective-permute-start | bytes 2359304 | tf_op jit(solution)/shard_map/ppermute | solution.py:82
  207.3 21.4 %collective-permute-start.21 = (bf16[256,1536]{1,0:T(8,128)(2,1)}, bf16[256,1536]{1,0:T(8,128)(2,1)S(1)}, u32[]{:S(2)}, u32[]{:S(2)}) collective-permute-start(bf16[256,1536]{1,0:T(8,128)(2,1)} %collective-permute-done.17), channel_id=1, source_target_pairs={{1,2},{2,3},{5,6},{6,7},{9,10},{10,11},{13,14},{14,15},{17,18},{18... | collective-permute-start | bytes 2359304 | tf_op jit(solution)/shard_map/ppermute | solution.py:75
  208.0 21.0 %collective-permute-start.22 = (bf16[256,1536]{1,0:T(8,128)(2,1)}, bf16[256,1536]{1,0:T(8,128)(2,1)S(1)}, u32[]{:S(2)}, u32[]{:S(2)}) collective-permute-start(bf16[256,1536]{1,0:T(8,128)(2,1)} %collective-permute-done.18), channel_id=1, source_target_pairs={{1,0},{2,1},{5,4},{6,5},{9,8},{10,9},{13,12},{14,13},{17,16},{18,1... | collective-permute-start | bytes 2359304 | tf_op jit(solution)/shard_map/ppermute | solution.py:76
  273.8 21.5 %collective-permute-start.32 = (bf16[256,1536]{1,0:T(8,128)(2,1)S(1)}, bf16[256,1536]{1,0:T(8,128)(2,1)}, u32[]{:S(2)}, u32[]{:S(2)}) collective-permute-start(bf16[256,1536]{1,0:T(8,128)(2,1)S(1)} %multiply_convert_fusion.4.x_ref), channel_id=1, source_target_pairs={{1,0},{2,1},{3,2},{5,4},{6,5},{7,6},{9,8},{10,9},{11,10},{13,12},{... | collective-permute-start | bytes 2359304 | tf_op jit(solution)/shard_map/ppermute | solution.py:115
  347.8 225.8 %all-gather.19.cloned.1.call-start = ((), (), s32[]{:S(2)}) async-start(), calls=%async_computation.13 | async-start | bytes 2654208 | tf_op jit(solution)/shard_map/all_gather | solution.py:928
  394.5 24.4 %collective-permute-start.43 = (bf16[256,1536]{1,0:T(8,128)(2,1)}, bf16[256,1536]{1,0:T(8,128)(2,1)}, u32[]{:S(2)}, u32[]{:S(2)}) collective-permute-start(bf16[256,1536]{1,0:T(8,128)(2,1)} %get-tuple-element.351), channel_id=1, source_target_pairs={{0,1},{1,2},{2,3},{4,5},{5,6},{6,7},{8,9},{9,10},{10,11},{12,13},{... | collective-permute-start | bytes 2359304 | tf_op jit(solution)/shard_map/ppermute | solution.py:82
  437.9 30.6 %collective-permute-start.48 = (bf16[256,1536]{1,0:T(8,128)(2,1)S(1)}, bf16[256,1536]{1,0:T(8,128)(2,1)}, u32[]{:S(2)}, u32[]{:S(2)}) collective-permute-start(bf16[256,1536]{1,0:T(8,128)(2,1)S(1)} %collective-permute-done.46), channel_id=1, source_target_pairs={{1,0},{2,1},{5,4},{6,5},{9,8},{10,9},{13,12},{14,13},{17,16},{18,1... | collective-permute-start | bytes 2359304 | tf_op jit(solution)/shard_map/ppermute | solution.py:76
  471.4 182.4 %all-gather.23.cloned.1.call-start = ((), (), s32[]{:S(2)}) async-start(), calls=%async_computation.15 | async-start | bytes 15925248 | tf_op jit(solution)/shard_map/all_gather | solution.py:928
  508.0 34.4 %collective-permute-start.54 = (bf16[144,768]{1,0:T(8,128)(2,1)S(1)}, bf16[144,768]{1,0:T(8,128)(2,1)S(1)}, u32[]{:S(2)}, u32[]{:S(2)}) collective-permute-start(bf16[144,768]{1,0:T(8,128)(2,1)S(1)} %fusion.52), channel_id=1, source_target_pairs={{0,12},{4,16},{8,20},{12,24},{16,28},{1,13},{5,17},{9,21},{13,25},... | collective-permute-start | bytes 663560 | tf_op jit(solution)/shard_map/ppermute | solution.py:226
  553.1 164.0 %all-gather.21.cloned.1.call-start = ((), (), s32[]{:S(2)}) async-start(), calls=%async_computation.14 | async-start | bytes 7962624 | tf_op jit(solution)/shard_map/all_gather | solution.py:928
  553.9 414.8 %reduce-scatter.9.cloned.1.call-start = ((), (), s32[]{:S(2)}) async-start(), calls=%async_computation.16 | async-start | bytes 15925248 | tf_op jit(solution)/shard_map/reduce_scatter | solution.py:1095
  578.6 23.0 %collective-permute-start.58 = (bf16[256,1536]{1,0:T(8,128)(2,1)S(1)}, bf16[256,1536]{1,0:T(8,128)(2,1)S(1)}, u32[]{:S(2)}, u32[]{:S(2)}) collective-permute-start(bf16[256,1536]{1,0:T(8,128)(2,1)S(1)} %get-tuple-element.727), channel_id=1, source_target_pairs={{3,2},{7,6},{11,10},{15,14},{19,18},{23,22},{27,26},{31,30}} | collective-permute-start | bytes 2359304 | tf_op jit(solution)/shard_map/ppermute | solution.py:83
  579.4 22.2 %collective-permute-start.57 = (bf16[256,1536]{1,0:T(8,128)(2,1)S(1)}, bf16[256,1536]{1,0:T(8,128)(2,1)S(1)}, u32[]{:S(2)}, u32[]{:S(2)}) collective-permute-start(bf16[256,1536]{1,0:T(8,128)(2,1)S(1)} %get-tuple-element.728), channel_id=1, source_target_pairs={{0,1},{4,5},{8,9},{12,13},{16,17},{20,21},{24,25},{28,29}} | collective-permute-start | bytes 2359304 | tf_op jit(solution)/shard_map/ppermute | solution.py:82
  646.2 20.7 %collective-permute-start.66 = (bf16[256,1536]{1,0:T(8,128)(2,1)S(1)}, bf16[256,1536]{1,0:T(8,128)(2,1)S(1)}, u32[]{:S(2)}, u32[]{:S(2)}) collective-permute-start(bf16[256,1536]{1,0:T(8,128)(2,1)S(1)} %multiply_convert_fusion.2.x_ref), channel_id=1, source_target_pairs={{1,0},{2,1},{3,2},{5,4},{6,5},{7,6},{9,8},{10,9},{11,10},{13,12},{... | collective-permute-start | bytes 2359304 | tf_op jit(solution)/shard_map/ppermute | solution.py:115
  749.9 29.1 %collective-permute-start.73 = (f32[128,128]{1,0:T(8,128)S(1)}, f32[128,128]{1,0:T(8,128)S(1)}, u32[]{:S(2)}, u32[]{:S(2)}) collective-permute-start(f32[128,128]{1,0:T(8,128)S(1)} %reshape.654), channel_id=1, source_target_pairs={{0,1},{1,0},{2,3},{3,2},{4,5},{5,4},{6,7},{7,6},{8,9},{9,8},{10,11... | collective-permute-start | bytes 196616 | tf_op jit(solution)/shard_map/ppermute | solution.py:140
  775.0 21.9 %collective-permute-start.72 = (bf16[256,1536]{1,0:T(8,128)(2,1)}, bf16[256,1536]{1,0:T(8,128)(2,1)}, u32[]{:S(2)}, u32[]{:S(2)}) collective-permute-start(bf16[256,1536]{1,0:T(8,128)(2,1)} %get-tuple-element.721), channel_id=1, source_target_pairs={{3,2},{7,6},{11,10},{15,14},{19,18},{23,22},{27,26},{31,30}} | collective-permute-start | bytes 2359304 | tf_op jit(solution)/shard_map/ppermute | solution.py:83
  776.7 20.3 %collective-permute-start.71 = (bf16[256,1536]{1,0:T(8,128)(2,1)}, bf16[256,1536]{1,0:T(8,128)(2,1)}, u32[]{:S(2)}, u32[]{:S(2)}) collective-permute-start(bf16[256,1536]{1,0:T(8,128)(2,1)} %get-tuple-element.722), channel_id=1, source_target_pairs={{0,1},{4,5},{8,9},{12,13},{16,17},{20,21},{24,25},{28,29}} | collective-permute-start | bytes 2359304 | tf_op jit(solution)/shard_map/ppermute | solution.py:82
  800.0 203.4 %reduce-scatter.11.cloned.1.call-start = ((), (), s32[]{:S(2)}) async-start(), calls=%async_computation.17 | async-start | bytes 7962624 | tf_op jit(solution)/shard_map/reduce_scatter | solution.py:1123
  870.6 224.4 %reduce-scatter.13.cloned.1.call-start = ((), (), s32[]{:S(2)}) async-start(), calls=%async_computation.18 | async-start | bytes 5308416 | tf_op jit(solution)/shard_map/reduce_scatter | solution.py:1136
  876.4 21.7 %collective-permute-start.84 = (bf16[256,1536]{1,0:T(8,128)(2,1)}, bf16[256,1536]{1,0:T(8,128)(2,1)S(1)}, u32[]{:S(2)}, u32[]{:S(2)}) collective-permute-start(bf16[256,1536]{1,0:T(8,128)(2,1)} %copy-done.185), channel_id=1, source_target_pairs={{1,0},{2,1},{5,4},{6,5},{9,8},{10,9},{13,12},{14,13},{17,16},{18,1... | collective-permute-start | bytes 2359304 | tf_op jit(solution)/shard_map/ppermute | solution.py:76
  900.2 27.1 %collective-permute-start.94 = (bf16[256,1536]{1,0:T(8,128)(2,1)S(1)}, bf16[256,1536]{1,0:T(8,128)(2,1)S(1)}, u32[]{:S(2)}, u32[]{:S(2)}) collective-permute-start(bf16[256,1536]{1,0:T(8,128)(2,1)S(1)} %get-tuple-element.439), channel_id=1, source_target_pairs={{0,1},{1,2},{4,5},{5,6},{8,9},{9,10},{12,13},{13,14},{16,17},{17,1... | collective-permute-start | bytes 2359304 | tf_op jit(solution)/shard_map/ppermute | solution.py:82
  904.9 22.4 %collective-permute-start.95 = (bf16[256,1536]{1,0:T(8,128)(2,1)S(1)}, bf16[256,1536]{1,0:T(8,128)(2,1)S(1)}, u32[]{:S(2)}, u32[]{:S(2)}) collective-permute-start(bf16[256,1536]{1,0:T(8,128)(2,1)S(1)} %get-tuple-element.440), channel_id=1, source_target_pairs={{2,1},{3,2},{6,5},{7,6},{10,9},{11,10},{14,13},{15,14},{18,17},{19... | collective-permute-start | bytes 2359304 | tf_op jit(solution)/shard_map/ppermute | solution.py:83
  928.9 39.9 %collective-permute-start.96 = (bf16[256,1536]{1,0:T(8,128)(2,1)}, bf16[256,1536]{1,0:T(8,128)(2,1)}, u32[]{:S(2)}, u32[]{:S(2)}) collective-permute-start(bf16[256,1536]{1,0:T(8,128)(2,1)} %get-tuple-element.441), channel_id=1, source_target_pairs={{0,1},{1,2},{2,3},{4,5},{5,6},{6,7},{8,9},{9,10},{10,11},{12,13},{... | collective-permute-start | bytes 2359304 | tf_op jit(solution)/shard_map/ppermute | solution.py:82
  931.3 37.5 %collective-permute-start.97 = (bf16[256,1536]{1,0:T(8,128)(2,1)}, bf16[256,1536]{1,0:T(8,128)(2,1)}, u32[]{:S(2)}, u32[]{:S(2)}) collective-permute-start(bf16[256,1536]{1,0:T(8,128)(2,1)} %get-tuple-element.442), channel_id=1, source_target_pairs={{1,0},{2,1},{3,2},{5,4},{6,5},{7,6},{9,8},{10,9},{11,10},{13,12},{... | collective-permute-start | bytes 2359304 | tf_op jit(solution)/shard_map/ppermute | solution.py:83
  942.6 25.0 %collective-permute-start.93 = (bf16[144,768]{1,0:T(8,128)(2,1)S(1)}, bf16[144,768]{1,0:T(8,128)(2,1)S(1)}, u32[]{:S(2)}, u32[]{:S(2)}) collective-permute-start(bf16[144,768]{1,0:T(8,128)(2,1)S(1)} %maximum_maximum_fusion.2), channel_id=1, source_target_pairs={{24,0},{28,4},{25,1},{29,5},{26,2},{30,6},{27,3},{31,7}} | collective-permute-start | bytes 663560 | tf_op jit(solution)/shard_map/ppermute | solution.py:226
  943.9 21.6 %collective-permute-start.92 = (bf16[144,768]{1,0:T(8,128)(2,1)S(1)}, bf16[144,768]{1,0:T(8,128)(2,1)S(1)}, u32[]{:S(2)}, u32[]{:S(2)}) collective-permute-start(bf16[144,768]{1,0:T(8,128)(2,1)S(1)} %maximum_maximum_fusion.2), channel_id=1, source_target_pairs={{12,0},{16,4},{20,8},{24,12},{28,16},{13,1},{17,5},{21,9},{25,13},... | collective-permute-start | bytes 663560 | tf_op jit(solution)/shard_map/ppermute | solution.py:226
  968.7 207.6 %reduce-scatter.15.cloned.1.call-start = ((), (), s32[]{:S(2)}) async-start(), calls=%async_computation.19 | async-start | bytes 3981312 | tf_op jit(solution)/shard_map/reduce_scatter | solution.py:1167
  1017.2 22.4 %collective-permute-start.99 = (bf16[256,1536]{1,0:T(8,128)(2,1)}, bf16[256,1536]{1,0:T(8,128)(2,1)S(1)}, u32[]{:S(2)}, u32[]{:S(2)}) collective-permute-start(bf16[256,1536]{1,0:T(8,128)(2,1)} %get-tuple-element.710), channel_id=1, source_target_pairs={{0,1},{4,5},{8,9},{12,13},{16,17},{20,21},{24,25},{28,29}} | collective-permute-start | bytes 2359304 | tf_op jit(solution)/shard_map/ppermute | solution.py:82
  1041.4 21.0 %collective-permute-start.101 = (bf16[256,1536]{1,0:T(8,128)(2,1)S(1)}, bf16[256,1536]{1,0:T(8,128)(2,1)S(1)}, u32[]{:S(2)}, u32[]{:S(2)}) collective-permute-start(bf16[256,1536]{1,0:T(8,128)(2,1)S(1)} %get-tuple-element.454), channel_id=1, source_target_pairs={{0,1},{1,2},{4,5},{5,6},{8,9},{9,10},{12,13},{13,14},{16,17},{17,1... | collective-permute-start | bytes 2359304 | tf_op jit(solution)/shard_map/ppermute | solution.py:82
  1064.1 22.9 %collective-permute-start.103 = (bf16[256,1536]{1,0:T(8,128)(2,1)}, bf16[256,1536]{1,0:T(8,128)(2,1)}, u32[]{:S(2)}, u32[]{:S(2)}) collective-permute-start(bf16[256,1536]{1,0:T(8,128)(2,1)} %get-tuple-element.456), channel_id=1, source_target_pairs={{0,1},{1,2},{2,3},{4,5},{5,6},{6,7},{8,9},{9,10},{10,11},{12,13},{... | collective-permute-start | bytes 2359304 | tf_op jit(solution)/shard_map/ppermute | solution.py:82
  1071.5 20.4 %collective-permute-start.104 = (bf16[256,1536]{1,0:T(8,128)(2,1)}, bf16[256,1536]{1,0:T(8,128)(2,1)}, u32[]{:S(2)}, u32[]{:S(2)}) collective-permute-start(bf16[256,1536]{1,0:T(8,128)(2,1)} %get-tuple-element.457), channel_id=1, source_target_pairs={{1,0},{2,1},{3,2},{5,4},{6,5},{7,6},{9,8},{10,9},{11,10},{13,12},{... | collective-permute-start | bytes 2359304 | tf_op jit(solution)/shard_map/ppermute | solution.py:83
  1072.9 302.4 %reduce-scatter.17.cloned.1.call-start = ((), (), s32[]{:S(2)}) async-start(), calls=%async_computation.20 | async-start | bytes 15925248 | tf_op jit(solution)/shard_map/reduce_scatter | solution.py:1095
  1120.6 20.9 %collective-permute-start.108 = (bf16[256,1536]{1,0:T(8,128)(2,1)S(1)}, bf16[256,1536]{1,0:T(8,128)(2,1)S(1)}, u32[]{:S(2)}, u32[]{:S(2)}) collective-permute-start(bf16[256,1536]{1,0:T(8,128)(2,1)S(1)} %collective-permute-done.106), channel_id=1, source_target_pairs={{1,0},{2,1},{5,4},{6,5},{9,8},{10,9},{13,12},{14,13},{17,16},{18,1... | collective-permute-start | bytes 2359304 | tf_op jit(solution)/shard_map/ppermute | solution.py:115
  1176.3 31.2 %collective-permute-start.113 = (f32[128,128]{1,0:T(8,128)S(1)}, f32[128,128]{1,0:T(8,128)S(1)}, u32[]{:S(2)}, u32[]{:S(2)}) collective-permute-start(f32[128,128]{1,0:T(8,128)S(1)} %reshape.661), channel_id=1, source_target_pairs={{0,1},{1,0},{2,3},{3,2},{4,5},{5,4},{6,7},{7,6},{8,9},{9,8},{10,11... | collective-permute-start | bytes 196616 | tf_op jit(solution)/shard_map/ppermute | solution.py:140
  1199.9 25.6 %collective-permute-start.112 = (bf16[256,1536]{1,0:T(8,128)(2,1)}, bf16[256,1536]{1,0:T(8,128)(2,1)}, u32[]{:S(2)}, u32[]{:S(2)}) collective-permute-start(bf16[256,1536]{1,0:T(8,128)(2,1)} %get-tuple-element.703), channel_id=1, source_target_pairs={{3,2},{7,6},{11,10},{15,14},{19,18},{23,22},{27,26},{31,30}} | collective-permute-start | bytes 2359304 | tf_op jit(solution)/shard_map/ppermute | solution.py:83
  1201.5 24.0 %collective-permute-start.111 = (bf16[256,1536]{1,0:T(8,128)(2,1)}, bf16[256,1536]{1,0:T(8,128)(2,1)}, u32[]{:S(2)}, u32[]{:S(2)}) collective-permute-start(bf16[256,1536]{1,0:T(8,128)(2,1)} %get-tuple-element.704), channel_id=1, source_target_pairs={{0,1},{4,5},{8,9},{12,13},{16,17},{20,21},{24,25},{28,29}} | collective-permute-start | bytes 2359304 | tf_op jit(solution)/shard_map/ppermute | solution.py:82
  1228.9 183.5 %reduce-scatter.19.cloned.1.call-start = ((), (), s32[]{:S(2)}) async-start(), calls=%async_computation.21 | async-start | bytes 7962624 | tf_op jit(solution)/shard_map/reduce_scatter | solution.py:1123
  1246.2 20.3 %collective-permute-start.117 = (bf16[256,1536]{1,0:T(8,128)(2,1)}, bf16[256,1536]{1,0:T(8,128)(2,1)}, u32[]{:S(2)}, u32[]{:S(2)}) collective-permute-start(bf16[256,1536]{1,0:T(8,128)(2,1)} %get-tuple-element.486), channel_id=1, source_target_pairs={{0,1},{1,2},{2,3},{4,5},{5,6},{6,7},{8,9},{9,10},{10,11},{12,13},{... | collective-permute-start | bytes 2359304 | tf_op jit(solution)/shard_map/ppermute | solution.py:82
  1293.5 170.1 %reduce-scatter.21.cloned.1.call-start = ((), (), s32[]{:S(2)}) async-start(), calls=%async_computation.22 | async-start | bytes 5308416 | tf_op jit(solution)/shard_map/reduce_scatter | solution.py:1136
  1294.4 21.0 %collective-permute-start.124 = (bf16[256,1536]{1,0:T(8,128)(2,1)}, bf16[256,1536]{1,0:T(8,128)(2,1)S(1)}, u32[]{:S(2)}, u32[]{:S(2)}) collective-permute-start(bf16[256,1536]{1,0:T(8,128)(2,1)} %copy-done.189), channel_id=1, source_target_pairs={{1,0},{2,1},{5,4},{6,5},{9,8},{10,9},{13,12},{14,13},{17,16},{18,1... | collective-permute-start | bytes 2359304 | tf_op jit(solution)/shard_map/ppermute | solution.py:76
  1375.3 202.9 %reduce-scatter.23.cloned.1.call-start = ((), (), s32[]{:S(2)}) async-start(), calls=%async_computation.23 | async-start | bytes 3981312 | tf_op jit(solution)/shard_map/reduce_scatter | solution.py:1167
  1488.2 47.1 %collective-permute-start.141 = (bf16[96,384]{1,0:T(8,128)(2,1)}, bf16[96,384]{1,0:T(8,128)(2,1)}, u32[]{:S(2)}, u32[]{:S(2)}) collective-permute-start(bf16[96,384]{1,0:T(8,128)(2,1)} %broadcast_select_fusion.8), channel_id=1, source_target_pairs={{0,2},{1,3},{2,0},{3,1},{4,6},{5,7},{6,4},{7,5},{8,10},{9,11},{10,... | collective-permute-start | bytes 221192 | tf_op jit(solution)/shard_map/ppermute | solution.py:163
  1498.1 20.8 %collective-permute-start.147 = (bf16[48,512]{1,0:T(8,128)(2,1)}, bf16[48,512]{1,0:T(8,128)(2,1)}, u32[]{:S(2)}, u32[]{:S(2)}) collective-permute-start(bf16[48,512]{1,0:T(8,128)(2,1)} %bitcast.129), channel_id=1, source_target_pairs={{0,2},{1,3},{2,0},{3,1},{4,6},{5,7},{6,4},{7,5},{8,10},{9,11},{10,... | collective-permute-start | bytes 147464 | tf_op jit(solution)/shard_map/ppermute | solution.py:177
  1498.6 20.8 %collective-permute-start.148 = (bf16[48,512]{1,0:T(8,128)(2,1)}, bf16[48,512]{1,0:T(8,128)(2,1)}, u32[]{:S(2)}, u32[]{:S(2)}) collective-permute-start(bf16[48,512]{1,0:T(8,128)(2,1)} %bitcast.130), channel_id=1, source_target_pairs={{0,1},{1,0},{2,3},{3,2},{4,5},{5,4},{6,7},{7,6},{8,9},{9,8},{10,11... | collective-permute-start | bytes 147464 | tf_op jit(solution)/shard_map/ppermute | solution.py:177
  1500.1 21.4 %collective-permute-start.146 = (bf16[48,512]{1,0:T(8,128)(2,1)}, bf16[48,512]{1,0:T(8,128)(2,1)}, u32[]{:S(2)}, u32[]{:S(2)}) collective-permute-start(bf16[48,512]{1,0:T(8,128)(2,1)} %bitcast.128), channel_id=1, source_target_pairs={{0,3},{1,2},{2,1},{3,0},{4,7},{5,6},{6,5},{7,4},{8,11},{9,10},{10,... | collective-permute-start | bytes 147464 | tf_op jit(solution)/shard_map/ppermute | solution.py:177
  1526.7 20.3 %collective-permute-start.135 = (bf16[256,1536]{1,0:T(8,128)(2,1)}, bf16[256,1536]{1,0:T(8,128)(2,1)}, u32[]{:S(2)}, u32[]{:S(2)}) collective-permute-start(bf16[256,1536]{1,0:T(8,128)(2,1)} %get-tuple-element.524), channel_id=1, source_target_pairs={{0,1},{1,2},{4,5},{5,6},{8,9},{9,10},{12,13},{13,14},{16,17},{17,1... | collective-permute-start | bytes 2359304 | tf_op jit(solution)/shard_map/ppermute | solution.py:82
  1549.4 21.7 %collective-permute-start.137 = (bf16[256,1536]{1,0:T(8,128)(2,1)S(1)}, bf16[256,1536]{1,0:T(8,128)(2,1)S(1)}, u32[]{:S(2)}, u32[]{:S(2)}) collective-permute-start(bf16[256,1536]{1,0:T(8,128)(2,1)S(1)} %get-tuple-element.526), channel_id=1, source_target_pairs={{0,1},{1,2},{2,3},{4,5},{5,6},{6,7},{8,9},{9,10},{10,11},{12,13},{... | collective-permute-start | bytes 2359304 | tf_op jit(solution)/shard_map/ppermute | solution.py:82
  1555.5 20.5 %collective-permute-start.138 = (bf16[256,1536]{1,0:T(8,128)(2,1)S(1)}, bf16[256,1536]{1,0:T(8,128)(2,1)S(1)}, u32[]{:S(2)}, u32[]{:S(2)}) collective-permute-start(bf16[256,1536]{1,0:T(8,128)(2,1)S(1)} %get-tuple-element.527), channel_id=1, source_target_pairs={{1,0},{2,1},{3,2},{5,4},{6,5},{7,6},{9,8},{10,9},{11,10},{13,12},{... | collective-permute-start | bytes 2359304 | tf_op jit(solution)/shard_map/ppermute | solution.py:83
  (389 other events, 6526.7 us)
Sparse Core Ops, SparseCore 0:
  51.2 46.7 all-gather.8
  100.4 29.2 all-gather.10
  166.0 80.9 all-gather.12
  249.2 48.8 all-gather.14
  347.9 60.0 all-gather.16
  471.6 42.4 all-gather.18
  553.2 77.9 all-gather.22
  633.1 48.8 all-gather.20
  800.1 111.6 reduce-scatter.8
  915.1 75.1 reduce-scatter.10
  994.1 53.8 reduce-scatter.12
  1073.0 47.4 reduce-scatter.14
  1229.0 102.9 reduce-scatter.16
  1335.4 70.0 reduce-scatter.18
  1409.7 53.8 reduce-scatter.20
  1487.7 48.5 reduce-scatter.22

commit v3 on v2

--- a/solution.py
+++ b/solution.py
@@ -39,9 +39,9 @@
     return lax.optimization_barrier(values)
 
 
-def hop_both(v, x, riders=(), axis="tp"):
+def hop_both(v, x, riders=(), last=(), axis="tp"):
     n, me = lax.axis_size(axis), lax.axis_index(axis)
-    riders = tuple(riders)
+    riders, last = tuple(riders), tuple(last)
     rel = {0: v}
     ahead = right = left = None
     if v is not None:
@@ -63,12 +63,12 @@
             held += [right, left]
         if step > 1:
             count = len(held)
-            extra = riders if step == 2 else ()
-            if step == 2 and lead and scatters and not gathers:
-                extra = riders
+            extra = riders if step == 2 else last if step == n + lead - 1 else ()
             held = list(tie(*held, *extra))
-            if extra:
+            if step == 2:
                 riders = tuple(held[count:])
+            elif extra:
+                last = tuple(held[count:])
             held = held[:count]
         if gathers:
             ahead = (
@@ -95,7 +95,7 @@
         gathered = jnp.concatenate(outs, 0)
     if x is not None:
         total = piece(me).astype(f32) + right.astype(f32) + left.astype(f32)
-    return gathered, total, riders
+    return gathered, total, riders + last
 
 
 def choose(options, me):
@@ -1029,9 +1029,8 @@
             moe_out, *packs[l + 1][2:] = tie(moe_out, *packs[l + 1][2:])
             residual = mid + moe_out
 
-    def finish(r):
-        late, early, sums = r["late"], r["early"], r["sums"]
-        halves = r["up"].reshape(cut, ff_blocks, 2, FF_BLOCK)
+    def finish_up(up):
+        halves = up.reshape(cut, ff_blocks, 2, FF_BLOCK)
         halves = jnp.transpose(halves, (2, 0, 1, 3)).reshape(2, cut, ns, per_seq)
         mine_up = halves[..., : mine * ff_cut].reshape(2, cut, ns, mine, ff_cut)
         mine_up = jnp.transpose(mine_up, (3, 1, 0, 2, 4)).reshape(mine, cut, 2 * ff)
@@ -1041,11 +1040,17 @@
         shared_grad = jnp.transpose(
             shared_grad.reshape(nt, fine, 2, ns, sh_cut), (1, 2, 3, 0, 4)
         ).reshape(fine, -1)
-        common = pair_scatter(late[:, inner:])
+        return mine_up, shared_grad
+
+    def finish_in(early, late):
+        return jnp.stack([early[:, inner:], late[:, :inner]], 1), pair_scatter(late[:, inner:])
+
+    def outputs(r):
+        sums, common, down = r["sums"], r["common"], r["down"]
         small = common[:, 2 * STATE + heads :]
         return [
-            jnp.stack([early[:, inner:], late[:, :inner]], 1),
-            late[:, width : width + heads].astype(f32),
+            r["inner"],
+            r["late"][:, width : width + heads].astype(f32),
             common[:, : 2 * STATE],
             sums[:4],
             small[: 4 * tap_cut, experts + 2].reshape(4, tap_cut),
@@ -1053,13 +1058,13 @@
             sums[6, LANES : LANES + heads],
             jnp.sum(sums[5].reshape(heads, HEAD_DIM), axis=1),
             sums[4],
-            early[:, :inner].T,
+            r["early"][:, :inner].T,
             jnp.transpose(small[:, experts : experts + 2]),
             small[:, :experts],
-            mine_up,
-            r["down"][: mine * ff_cut].reshape(mine, ff_cut, depth),
-            shared_grad,
-            r["down"][mine * ff_cut :],
+            r["mine_up"],
+            down[: mine * ff_cut].reshape(mine, ff_cut, depth),
+            r["shared_up"],
+            down[mine * ff_cut :],
         ]
 
     grad = cotangent
@@ -1089,9 +1094,14 @@
             state = (first, state[1])
         d_hidden = state[0]
         up_part = mm(k["moe_in"], d_hidden, TN).astype(bf16)
-        _, d_moe, (d_gate_all, up_part) = hop_both(
-            None, mm(d_hidden, w_up[l], NT).astype(bf16), (gate_sums(), up_part)
+        _, d_moe, riders = hop_both(
+            None,
+            mm(d_hidden, w_up[l], NT).astype(bf16),
+            (gate_sums(), up_part) + (() if top else (above["up"],)),
         )
+        d_gate_all, up_part, *riders = riders
+        if not top:
+            above["mine_up"], above["shared_up"] = finish_up(riders[0])
         up_grad = lax.psum_scatter(up_part, "seq", scatter_dimension=0, tiled=True)
         down_part = mm(k["act"], gs, TN).astype(bf16)
         if top:
@@ -1118,8 +1128,13 @@
             d_mixed, moe_out, riders = hop_both(send, last_out, (cross_all, down_part))
             residual = k["mid"] + moe_out
         else:
-            d_mixed, _, riders = hop_both(send, None, (cross_all, down_part))
-        cross_all, down_part = riders
+            names = ("mine_up", "shared_up", "early", "late")
+            d_mixed, _, riders = hop_both(
+                send, None, [cross_all, down_part] + [above[name] for name in names]
+            )
+            above.update(zip(names, riders[2:]))
+            above["inner"], above["common"] = finish_in(above["early"], above["late"])
+        cross_all, down_part = riders[:2]
         down_grad = lax.psum_scatter(down_part, "seq", scatter_dimension=0, tiled=True)
         c2 = jnp.broadcast_to(cross_all[:, None], (rows, LANES))
         dg = mm(d_mixed, w_out[l])
@@ -1133,6 +1148,10 @@
         carried, early, up_grad = tie(carried, early, up_grad)
         if top:
             carried, residual = tie(carried, residual)
+        else:
+            carried, above["inner"], above["common"] = tie(
+                carried, above["inner"], above["common"]
+            )
         early = lax.psum_scatter(early, "seq", scatter_dimension=0, tiled=True)
         dp, last, back, tacc, hacc = mixer_scan_back(
             k["pu"], k["edge"], dz, k["taps"], k["head"], k["head_rows"], aux, auxr, ex,
@@ -1157,27 +1176,32 @@
         sums = jnp.concatenate(
             [tacc[:4, :inner], acc[:2], pad_rows([hacc[:2].reshape(-1)], 2, inner)], 0
         )
-        names = ("up", "down", "early", "sums")
-        now = dict(up=up_grad, down=down_grad, early=early, sums=sums)
-        held = [late]
+        if top:
+            _, d_own, riders = hop_both(None, d_normed.astype(bf16), (late, sums))
+            late, sums = riders
+        else:
+            _, d_own, riders = hop_both(
+                None,
+                d_normed.astype(bf16),
+                (late, early),
+                (sums, above["sums"], up_grad),
+            )
+            late, early, sums = riders[:3]
+        late = lax.psum_scatter(late, "seq", scatter_dimension=0, tiled=True)
+        if top:
+            d_own, early = tie(d_own, early)
+        else:
+            both = pair_total(jnp.concatenate([sums, riders[3]], 0), "seq")
+            sums, above["sums"] = both[: sums.shape[0]], both[sums.shape[0] :]
+            finished[l + 1] = outputs(above)
+            d_own, down_grad = tie(d_own, down_grad)
+        grad = grad_mid + norm_back(k["residual"], k["inv1"], k["gain1"], d_own)
+        above = dict(up=up_grad, down=down_grad, early=early, late=late, sums=sums)
         if not top:
-            held += [now[name] for name in names] + [above[name] for name in names]
-            held += [above["late"]]
-        _, d_own, riders = hop_both(None, d_normed.astype(bf16), held)
-        late = lax.psum_scatter(riders[0], "seq", scatter_dimension=0, tiled=True)
-        if top:
-            d_own, now["early"] = tie(d_own, early)
-        else:
-            now.update(zip(names, riders[1:5]))
-            above.update(zip(names, riders[5:9]))
-            above["late"] = riders[9]
-            both = pair_total(jnp.concatenate([now["sums"], above["sums"]], 0), "seq")
-            now["sums"], above["sums"] = both[: sums.shape[0]], both[sums.shape[0] :]
-            finished[l + 1] = finish(above)
-        grad = grad_mid + norm_back(k["residual"], k["inv1"], k["gain1"], d_own)
-        above = dict(now, late=late)
-
-    finished[0] = finish(above)
+            above["mine_up"], above["shared_up"] = finish_up(riders[4])
+
+    above["inner"], above["common"] = finish_in(above["early"], above["late"])
+    finished[0] = outputs(above)
     stacked = [jnp.stack([part[i] for part in finished], 0).astype(f32) for i in range(16)]
     return (residual, grad, *stacked)
 

time: 1620 us -> 1610 us (level)
  waiting for transfers between devices: 434 us -> 395 us
  local copies, waits for them, and re-layouts: 173 us -> 197 us
    ppermute x24, waiting for transfers between devices: 135 us -> 114 us  [hop_both(): right = lax.ppermute(held[0], axis, [(i, i + 1) for i in range(0, s)])]
    reduce_scatter x2, waiting for transfers between devices: 16.9 us -> 0.01 us  [local(): early = lax.psum_scatter(early, 'seq', scatter_dimension=0, tiled=True)]
    unnamed x587 -> x577, local copies, waits for them, and re-layouts: 58 us -> 57 us
  transfers between devices with their start and end apart: 168 -> 168, of which waited for: 62 -> 60; matrix products, arithmetic and copies ran while one was open for 29% -> 32% of each run, Pallas kernels for 15% -> 15%
where the time goes in v3:
time: 1610 us; the launch traced here: 1600 us
  waiting for transfers between devices  395 us (25%)
  starting transfers between devices  345 us (21%)
  Pallas kernels  260 us (16%)
  matrix products  219 us (14%)
  local copies, waits for them, and re-layouts  197 us (12%)
  other arithmetic  161 us (10%)
  between operations  20.1 us (1%)
    dot_general x28, matrix products, mm(): lax.dot_general(a, b, dims, precision=precision, preferred_element_type=f32)  219 us
    ppermute x15, waiting for transfers between devices, hop_both(): lax.ppermute(held[1], axis, [(i, i - 1) for i in range(1, n - step + 1)])  127 us
    ppermute x24, starting transfers between devices, hop_both(): right = lax.ppermute(held[0], axis, [(i, i + 1) for i in range(0, s)])  115 us
    ppermute x24, waiting for transfers between devices, hop_both(): right = lax.ppermute(held[0], axis, [(i, i + 1) for i in range(0, s)])  114 us
    pallas_call x8, Pallas kernels, experts_up(): pl.pallas_call(up_kernel, grid_spec=pltpu.PrefetchScalarGridSpec(num_scal...  102 us
    pallas_call x5, Pallas kernels, experts_down_back(): pl.pallas_call(down_back_kernel, grid_spec=pltpu.PrefetchScalarGridSpec(n...  65.4 us
    ppermute x24, starting transfers between devices, shift_seq(): return lax.ppermute(v, 'seq', [(i, i + steps) for i in range(first, last)])  60.7 us
    unnamed x577, local copies, waits for them, and re-layouts  57 us
  transfers between devices with their start and end apart: 168, of which 60 were waited for; matrix products, arithmetic and copies ran while one was open for 32% of the time, Pallas kernels for 15%

profile of v3, /device:TPU:0, one launch (start us, length us, event | category | flops | bytes accessed | tf_op | source)
XLA Modules:
  0.0 1597.7 jit_solution(6402765418101743647)
XLA Ops:
  12.7 6.4 collective-permute-start
  26.0 8.2 collective-permute-done.1
  76.3 7.6 collective-permute-done.3
  112.9 7.2 fusion.6.u_ref.bc_ref.dt_ref.uh_ref.bch_ref
  122.3 6.6 mixer_states.2
  141.5 6.1 fusion.31.z_ref
  171.1 6.7 collective-permute-start.17
  209.3 10.7 collective-permute-done.33
  247.4 6.1 collective-permute-start.27
  264.1 7.0 collective-permute-done.28
  282.6 12.7 experts_up.8
  299.7 12.6 experts_up.9
  317.9 12.6 experts_up.10
  335.0 12.7 experts_up.11
  347.8 11.1 convolution_convert_fusion.10
  364.8 12.6 collective-permute-done.39
  383.1 9.8 collective-permute-done.41
  394.5 7.3 collective-permute-start.43
  427.7 8.0 collective-permute-done.46
  439.2 29.1 %collective-permute-done.48 = bf16[256,1536]{1,0:T(8,128)(2,1)} collective-permute-done((bf16[256,1536]{1,0:T(8,128)(2,1)S(1)}, bf16[256,1536]{1,0:T(8,128)(2,1)}, u32[]{:S(2)}, u32[]{:S(2)}) %collective-permute-start.48) | collective-permute-done | bytes 786464 | tf_op jit(solution)/shard_map/ppermute | solution.py:76
  471.5 12.5 collective-permute-done.50
  490.2 8.3 fusion.4.u_ref.bc_ref.dt_ref.uh_ref.bch_ref
  500.7 6.6 mixer_states.3
  507.7 17.3 %collective-permute-start.54 = (bf16[144,768]{1,0:T(8,128)(2,1)S(1)}, bf16[144,768]{1,0:T(8,128)(2,1)S(1)}, u32[]{:S(2)}, u32[]{:S(2)}) collective-permute-start(bf16[144,768]{1,0:T(8,128)(2,1)S(1)} %fusion.52), channel_id=1, source_target_pairs={{0,12},{4,16},{8,20},{12,24},{16,28},{1,13},{5,17},{9,21},{13,25},... | collective-permute-start | bytes 663560 | tf_op jit(solution)/shard_map/ppermute | solution.py:226
  580.6 15.9 collective-permute-done.59
  606.8 13.4 collective-permute-done.61
  620.7 6.4 collective-permute-start.63
  628.4 12.0 collective-permute-done.63
  653.2 13.2 experts_up.12
  670.6 12.8 experts_up.13
  686.9 12.7 experts_up.14
  703.6 12.8 experts_up.15
  722.3 23.0 %experts_down_back.5 = (bf16[1024,4608]{1,0:T(8,128)(2,1)S(1)}, f32[1024,128]{1,0:T(8,128)S(1)}) custom-call(s32[1]{0:T(128)} %constant.179.clone.1.at_ref, bf16[1024,1536]{1,0:T(8,128)(2,1)S(1)} %copy-done.11, bf16[2304,1536]{1,0:T(8,128)(2,1)S(1)} %copy-done.25, bf16[1024,4608]{1,0:T(8,128)(2,1)} %get-tuple-element.416.h_ref, f32[1024,128]{1,0:T(8,128)S(1)} %copy-done.19, ...), custom_call_target="tpu_custom_call" | custom-call | tf_op jit(solution)/shard_map/experts_down_back/pallas_call | solution.py:791
  751.5 21.4 %convolution_convert_fusion.7 = bf16[1024,1536]{1,0:T(8,128)(2,1)S(1)} fusion(bf16[1024,4608]{1,0:T(8,128)(2,1)} %copy-done.79, bf16[1536,4608]{1,0:T(8,128)(2,1)} %all-gather.23.cloned.1.call-done.w_ref), kind=kOutput, calls=%fused_computation.17 | convolution fusion | flops 14497087488 | bytes 26738688 | tf_op jit(solution)/shard_map/dot_general | solution.py:31
  778.5 17.7 %convolution_convert_fusion.1 = bf16[1536,4608]{1,0:T(8,128)(2,1)} fusion(bf16[1024,4608]{1,0:T(8,128)(2,1)S(1)} %copy-done.80, bf16[256,1536]{1,0:T(8,128)(2,1)S(1)} %copy-done.164, bf16[256,1536]{1,0:T(8,128)(2,1)S(1)} %copy-done.163, bf16[256,1536]{1,0:T(8,128)(2,1)S(1)} %copy-done.162, bf16[256,1536]{1,0:T(8,128)(2,1)S(1)} %copy-done.161), kind=kOutput, calls=%fused_computation.1 | convolution fusion | flops 14515175424 | bytes 26738688 | tf_op jit(solution)/shard_map/dot_general | solution.py:31
  799.4 6.8 collective-permute-start.75
  807.7 11.7 convolution_convert_fusion.3
  828.4 13.1 convolution_convert_fusion.8
  859.9 9.5 collective-permute-done.82
  877.7 7.2 collective-permute-done.85
  886.6 12.7 collective-permute-done.84
  907.2 6.7 collective-permute-done.88
  947.4 17.6 %collective-permute-done.92 = bf16[144,768]{1,0:T(8,128)(2,1)S(1)} collective-permute-done((bf16[144,768]{1,0:T(8,128)(2,1)S(1)}, bf16[144,768]{1,0:T(8,128)(2,1)S(1)}, u32[]{:S(2)}, u32[]{:S(2)}) %collective-permute-start.92) | collective-permute-done | bytes 221216 | tf_op jit(solution)/shard_map/ppermute | solution.py:226
  972.9 27.0 %mixer_scan_back.2 = (bf16[1024,2048]{1,0:T(8,128)(2,1)}, f32[8,1024]{1,0:T(8,128)S(1)}, f32[8,1024]{1,0:T(8,128)S(1)}, f32[8,1024]{1,0:T(8,128)S(1)}, f32[8,128]{1,0:T(8,128)S(1)}) custom-call(f32[1024,1152]{1,0:T(8,128)} %copy-done.1, f32[1024,1152]{1,0:T(8,128)} %copy-done.1, f32[1024,1152]{1,0:T(8,128)} %copy-done.1, f32[1024,1152]{1,0:T(8,128)} %copy-done.1, ...), custom_call_target="tpu_custom_call" | custom-call | tf_op jit(solution)/shard_map/mixer_scan_back/pallas_call | solution.py:666
  1003.7 11.6 fusion.3
  1030.2 9.8 collective-permute-done.99
  1046.8 16.1 %collective-permute-done.101 = bf16[256,1536]{1,0:T(8,128)(2,1)S(1)} collective-permute-done((bf16[256,1536]{1,0:T(8,128)(2,1)S(1)}, bf16[256,1536]{1,0:T(8,128)(2,1)S(1)}, u32[]{:S(2)}, u32[]{:S(2)}) %collective-permute-start.101) | collective-permute-done | bytes 786464 | tf_op jit(solution)/shard_map/ppermute | solution.py:82
  1064.3 7.4 collective-permute-start.103
  1073.1 13.9 collective-permute-done.103
  1105.2 10.7 experts_down_back.6
  1122.4 10.5 experts_down_back.7
  1133.0 7.2 collective-permute-done.108
  1144.2 10.6 experts_down_back.8
  1162.4 10.5 experts_down_back.9
  1174.3 20.5 %convolution_convert_fusion.6 = bf16[1024,1536]{1,0:T(8,128)(2,1)S(1)} fusion(bf16[1024,4608]{1,0:T(8,128)(2,1)} %get-tuple-element.490, bf16[1536,4608]{1,0:T(8,128)(2,1)} %all-gather.13.cloned.1.call-done.w_ref), kind=kOutput, calls=%fused_computation.16 | convolution fusion | flops 14497087488 | bytes 26738688 | tf_op jit(solution)/shard_map/dot_general | solution.py:31
  1205.5 17.7 %convolution_convert_fusion = bf16[1536,4608]{1,0:T(8,128)(2,1)} fusion(bf16[1024,4608]{1,0:T(8,128)(2,1)S(1)} %copy-done.85, bf16[256,1536]{1,0:T(8,128)(2,1)S(1)} %copy-done.155, bf16[256,1536]{1,0:T(8,128)(2,1)S(1)} %copy-done.154, bf16[256,1536]{1,0:T(8,128)(2,1)S(1)} %copy-done.153, bf16[256,1536]{1,0:T(8,128)(2,1)S(1)} %copy-done.152), kind=kOutput, calls=%fused_computation | convolution fusion | flops 14515175424 | bytes 26738688 | tf_op jit(solution)/shard_map/dot_general | solution.py:31
  1231.6 12.7 convolution_convert_fusion.2
  1306.5 28.7 %collective-permute-done.127 = bf16[256,1536]{1,0:T(8,128)(2,1)S(1)} collective-permute-done((bf16[256,1536]{1,0:T(8,128)(2,1)}, bf16[256,1536]{1,0:T(8,128)(2,1)S(1)}, u32[]{:S(2)}, u32[]{:S(2)}) %collective-permute-start.127) | collective-permute-done | bytes 786464 | tf_op jit(solution)/shard_map/ppermute | solution.py:76
  1338.9 10.9 collective-permute-done.129
  1384.8 12.2 collective-permute-done.133
  1417.5 27.0 %mixer_scan_back.3 = (bf16[1024,2048]{1,0:T(8,128)(2,1)}, f32[8,1024]{1,0:T(8,128)S(1)}, f32[8,1024]{1,0:T(8,128)S(1)}, f32[8,1024]{1,0:T(8,128)S(1)}, f32[8,128]{1,0:T(8,128)S(1)}) custom-call(f32[1024,1152]{1,0:T(8,128)} %copy-done, f32[1024,1152]{1,0:T(8,128)} %copy-done, f32[1024,1152]{1,0:T(8,128)} %copy-done, f32[1024,1152]{1,0:T(8,128)} %copy-done, ...), custom_call_target="tpu_custom_call" | custom-call | tf_op jit(solution)/shard_map/mixer_scan_back/pallas_call | solution.py:666
  1448.7 10.8 fusion.1
  1500.2 7.2 collective-permute-done.140
  1511.5 6.9 collective-permute-start.142
  (1316 shorter events, 795.4 us)
Async XLA Ops:
  7.2 103.9 %all-gather.9.cloned.1.call-start = ((), (), s32[]{:S(2)}) async-start(), calls=%async_computation.8 | async-start | bytes 7077888 | tf_op jit(solution)/shard_map/all_gather | solution.py:928
  11.4 22.8 %collective-permute-start.1 = (bf16[256,1536]{1,0:T(8,128)(2,1)}, bf16[256,1536]{1,0:T(8,128)(2,1)}, u32[]{:S(2)}, u32[]{:S(2)}) collective-permute-start(bf16[256,1536]{1,0:T(8,128)(2,1)} %multiply_convert_fusion.5), channel_id=1, source_target_pairs={{1,0},{2,1},{3,2},{5,4},{6,5},{7,6},{9,8},{10,9},{11,10},{13,12},{... | collective-permute-start | bytes 2359304 | tf_op jit(solution)/shard_map/ppermute | solution.py:76
  12.7 22.7 %collective-permute-start = (bf16[256,1536]{1,0:T(8,128)(2,1)}, bf16[256,1536]{1,0:T(8,128)(2,1)}, u32[]{:S(2)}, u32[]{:S(2)}) collective-permute-start(bf16[256,1536]{1,0:T(8,128)(2,1)} %multiply_convert_fusion.5), channel_id=1, source_target_pairs={{0,1},{1,2},{2,3},{4,5},{5,6},{6,7},{8,9},{9,10},{10,11},{12,13},{... | collective-permute-start | bytes 2359304 | tf_op jit(solution)/shard_map/ppermute | solution.py:75
  51.1 142.1 %all-gather.11.cloned.1.call-start = ((), (), s32[]{:S(2)}) async-start(), calls=%async_computation.9 | async-start | bytes 2654208 | tf_op jit(solution)/shard_map/all_gather | solution.py:928
  53.1 229.5 %all-gather.13.cloned.1.call-start = ((), (), s32[]{:S(2)}) async-start(), calls=%async_computation.10 | async-start | bytes 15925248 | tf_op jit(solution)/shard_map/all_gather | solution.py:928
  57.4 32.3 %collective-permute-start.6 = (bf16[2,48,512]{2,1,0:T(8,128)(2,1)}, bf16[2,48,512]{2,1,0:T(8,128)(2,1)S(1)}, u32[]{:S(2)}, u32[]{:S(2)}) collective-permute-start(bf16[2,48,512]{2,1,0:T(8,128)(2,1)} %get-tuple-element.816), channel_id=1, source_target_pairs={{0,3},{1,2},{2,1},{3,0},{4,7},{5,6},{6,5},{7,4},{8,11},{9,10},{10,... | collective-permute-start | bytes 294920 | tf_op jit(solution)/shard_map/ppermute | solution.py:177
  61.0 28.8 %collective-permute-start.8 = (bf16[2,48,512]{2,1,0:T(8,128)(2,1)}, bf16[2,48,512]{2,1,0:T(8,128)(2,1)}, u32[]{:S(2)}, u32[]{:S(2)}) collective-permute-start(bf16[2,48,512]{2,1,0:T(8,128)(2,1)} %get-tuple-element.817), channel_id=1, source_target_pairs={{0,1},{1,0},{2,3},{3,2},{4,5},{5,4},{6,7},{7,6},{8,9},{9,8},{10,11... | collective-permute-start | bytes 294920 | tf_op jit(solution)/shard_map/ppermute | solution.py:177
  61.0 29.4 %collective-permute-start.7 = (bf16[2,48,512]{2,1,0:T(8,128)(2,1)}, bf16[2,48,512]{2,1,0:T(8,128)(2,1)}, u32[]{:S(2)}, u32[]{:S(2)}) collective-permute-start(bf16[2,48,512]{2,1,0:T(8,128)(2,1)} %get-tuple-element.818), channel_id=1, source_target_pairs={{0,2},{1,3},{2,0},{3,1},{4,6},{5,7},{6,4},{7,5},{8,10},{9,11},{10,... | collective-permute-start | bytes 294920 | tf_op jit(solution)/shard_map/ppermute | solution.py:177
  63.4 20.5 %collective-permute-start.3 = (bf16[256,1536]{1,0:T(8,128)(2,1)}, bf16[256,1536]{1,0:T(8,128)(2,1)}, u32[]{:S(2)}, u32[]{:S(2)}) collective-permute-start(bf16[256,1536]{1,0:T(8,128)(2,1)} %collective-permute-done.1), channel_id=1, source_target_pairs={{1,0},{2,1},{5,4},{6,5},{9,8},{10,9},{13,12},{14,13},{17,16},{18,1... | collective-permute-start | bytes 2359304 | tf_op jit(solution)/shard_map/ppermute | solution.py:76
  83.9 22.7 %collective-permute-start.4 = (bf16[256,1536]{1,0:T(8,128)(2,1)}, bf16[256,1536]{1,0:T(8,128)(2,1)}, u32[]{:S(2)}, u32[]{:S(2)}) collective-permute-start(bf16[256,1536]{1,0:T(8,128)(2,1)} %collective-permute-done.2), channel_id=1, source_target_pairs={{2,3},{6,7},{10,11},{14,15},{18,19},{22,23},{26,27},{30,31}} | collective-permute-start | bytes 2359304 | tf_op jit(solution)/shard_map/ppermute | solution.py:75
  85.4 21.2 %collective-permute-start.5 = (bf16[256,1536]{1,0:T(8,128)(2,1)}, bf16[256,1536]{1,0:T(8,128)(2,1)}, u32[]{:S(2)}, u32[]{:S(2)}) collective-permute-start(bf16[256,1536]{1,0:T(8,128)(2,1)} %collective-permute-done.3), channel_id=1, source_target_pairs={{1,0},{5,4},{9,8},{13,12},{17,16},{21,20},{25,24},{29,28}} | collective-permute-start | bytes 2359304 | tf_op jit(solution)/shard_map/ppermute | solution.py:76
  129.2 24.4 %collective-permute-start.14 = (bf16[144,768]{1,0:T(8,128)(2,1)S(1)}, bf16[144,768]{1,0:T(8,128)(2,1)S(1)}, u32[]{:S(2)}, u32[]{:S(2)}) collective-permute-start(bf16[144,768]{1,0:T(8,128)(2,1)S(1)} %fusion.54), channel_id=1, source_target_pairs={{0,12},{4,16},{8,20},{12,24},{16,28},{1,13},{5,17},{9,21},{13,25},... | collective-permute-start | bytes 663560 | tf_op jit(solution)/shard_map/ppermute | solution.py:226
  165.8 182.0 %all-gather.15.cloned.1.call-start = ((), (), s32[]{:S(2)}) async-start(), calls=%async_computation.11 | async-start | bytes 7962624 | tf_op jit(solution)/shard_map/all_gather | solution.py:928
  166.4 321.8 %all-gather.17.cloned.1.call-start = ((), (), s32[]{:S(2)}) async-start(), calls=%async_computation.12 | async-start | bytes 7077888 | tf_op jit(solution)/shard_map/all_gather | solution.py:928
  169.8 32.8 %collective-permute-start.18 = (bf16[256,1536]{1,0:T(8,128)(2,1)}, bf16[256,1536]{1,0:T(8,128)(2,1)}, u32[]{:S(2)}, u32[]{:S(2)}) collective-permute-start(bf16[256,1536]{1,0:T(8,128)(2,1)} %convert_element_type.996), channel_id=1, source_target_pairs={{1,0},{2,1},{3,2},{5,4},{6,5},{7,6},{9,8},{10,9},{11,10},{13,12},{... | collective-permute-start | bytes 2359304 | tf_op jit(solution)/shard_map/ppermute | solution.py:76
  171.1 31.5 %collective-permute-start.17 = (bf16[256,1536]{1,0:T(8,128)(2,1)}, bf16[256,1536]{1,0:T(8,128)(2,1)}, u32[]{:S(2)}, u32[]{:S(2)}) collective-permute-start(bf16[256,1536]{1,0:T(8,128)(2,1)} %convert_element_type.996), channel_id=1, source_target_pairs={{0,1},{1,2},{2,3},{4,5},{5,6},{6,7},{8,9},{9,10},{10,11},{12,13},{... | collective-permute-start | bytes 2359304 | tf_op jit(solution)/shard_map/ppermute | solution.py:75
  202.6 21.8 %collective-permute-start.23 = (bf16[256,1536]{1,0:T(8,128)(2,1)}, bf16[256,1536]{1,0:T(8,128)(2,1)S(1)}, u32[]{:S(2)}, u32[]{:S(2)}) collective-permute-start(bf16[256,1536]{1,0:T(8,128)(2,1)} %get-tuple-element.317), channel_id=1, source_target_pairs={{0,1},{4,5},{8,9},{12,13},{16,17},{20,21},{24,25},{28,29}} | collective-permute-start | bytes 2359304 | tf_op jit(solution)/shard_map/ppermute | solution.py:82
  207.3 21.2 %collective-permute-start.21 = (bf16[256,1536]{1,0:T(8,128)(2,1)}, bf16[256,1536]{1,0:T(8,128)(2,1)S(1)}, u32[]{:S(2)}, u32[]{:S(2)}) collective-permute-start(bf16[256,1536]{1,0:T(8,128)(2,1)} %collective-permute-done.17), channel_id=1, source_target_pairs={{1,2},{2,3},{5,6},{6,7},{9,10},{10,11},{13,14},{14,15},{17,18},{18... | collective-permute-start | bytes 2359304 | tf_op jit(solution)/shard_map/ppermute | solution.py:75
  208.0 20.9 %collective-permute-start.22 = (bf16[256,1536]{1,0:T(8,128)(2,1)}, bf16[256,1536]{1,0:T(8,128)(2,1)S(1)}, u32[]{:S(2)}, u32[]{:S(2)}) collective-permute-start(bf16[256,1536]{1,0:T(8,128)(2,1)} %collective-permute-done.18), channel_id=1, source_target_pairs={{1,0},{2,1},{5,4},{6,5},{9,8},{10,9},{13,12},{14,13},{17,16},{18,1... | collective-permute-start | bytes 2359304 | tf_op jit(solution)/shard_map/ppermute | solution.py:76
  273.8 21.6 %collective-permute-start.32 = (bf16[256,1536]{1,0:T(8,128)(2,1)S(1)}, bf16[256,1536]{1,0:T(8,128)(2,1)}, u32[]{:S(2)}, u32[]{:S(2)}) collective-permute-start(bf16[256,1536]{1,0:T(8,128)(2,1)S(1)} %multiply_convert_fusion.4.x_ref), channel_id=1, source_target_pairs={{1,0},{2,1},{3,2},{5,4},{6,5},{7,6},{9,8},{10,9},{11,10},{13,12},{... | collective-permute-start | bytes 2359304 | tf_op jit(solution)/shard_map/ppermute | solution.py:115
  275.2 20.1 %collective-permute-start.31 = (bf16[256,1536]{1,0:T(8,128)(2,1)S(1)}, bf16[256,1536]{1,0:T(8,128)(2,1)}, u32[]{:S(2)}, u32[]{:S(2)}) collective-permute-start(bf16[256,1536]{1,0:T(8,128)(2,1)S(1)} %multiply_convert_fusion.4.x_ref), channel_id=1, source_target_pairs={{0,1},{1,2},{2,3},{4,5},{5,6},{6,7},{8,9},{9,10},{10,11},{12,13},{... | collective-permute-start | bytes 2359304 | tf_op jit(solution)/shard_map/ppermute | solution.py:114
  347.7 225.5 %all-gather.19.cloned.1.call-start = ((), (), s32[]{:S(2)}) async-start(), calls=%async_computation.13 | async-start | bytes 2654208 | tf_op jit(solution)/shard_map/all_gather | solution.py:928
  394.5 24.4 %collective-permute-start.43 = (bf16[256,1536]{1,0:T(8,128)(2,1)}, bf16[256,1536]{1,0:T(8,128)(2,1)}, u32[]{:S(2)}, u32[]{:S(2)}) collective-permute-start(bf16[256,1536]{1,0:T(8,128)(2,1)} %get-tuple-element.357), channel_id=1, source_target_pairs={{0,1},{1,2},{2,3},{4,5},{5,6},{6,7},{8,9},{9,10},{10,11},{12,13},{... | collective-permute-start | bytes 2359304 | tf_op jit(solution)/shard_map/ppermute | solution.py:82
  437.9 30.4 %collective-permute-start.48 = (bf16[256,1536]{1,0:T(8,128)(2,1)S(1)}, bf16[256,1536]{1,0:T(8,128)(2,1)}, u32[]{:S(2)}, u32[]{:S(2)}) collective-permute-start(bf16[256,1536]{1,0:T(8,128)(2,1)S(1)} %collective-permute-done.46), channel_id=1, source_target_pairs={{1,0},{2,1},{5,4},{6,5},{9,8},{10,9},{13,12},{14,13},{17,16},{18,1... | collective-permute-start | bytes 2359304 | tf_op jit(solution)/shard_map/ppermute | solution.py:76
  471.2 182.1 %all-gather.23.cloned.1.call-start = ((), (), s32[]{:S(2)}) async-start(), calls=%async_computation.15 | async-start | bytes 15925248 | tf_op jit(solution)/shard_map/all_gather | solution.py:928
  507.7 34.4 %collective-permute-start.54 = (bf16[144,768]{1,0:T(8,128)(2,1)S(1)}, bf16[144,768]{1,0:T(8,128)(2,1)S(1)}, u32[]{:S(2)}, u32[]{:S(2)}) collective-permute-start(bf16[144,768]{1,0:T(8,128)(2,1)S(1)} %fusion.52), channel_id=1, source_target_pairs={{0,12},{4,16},{8,20},{12,24},{16,28},{1,13},{5,17},{9,21},{13,25},... | collective-permute-start | bytes 663560 | tf_op jit(solution)/shard_map/ppermute | solution.py:226
  552.8 163.6 %all-gather.21.cloned.1.call-start = ((), (), s32[]{:S(2)}) async-start(), calls=%async_computation.14 | async-start | bytes 7962624 | tf_op jit(solution)/shard_map/all_gather | solution.py:928
  553.5 415.4 %reduce-scatter.9.cloned.1.call-start = ((), (), s32[]{:S(2)}) async-start(), calls=%async_computation.16 | async-start | bytes 15925248 | tf_op jit(solution)/shard_map/reduce_scatter | solution.py:1105
  578.1 23.0 %collective-permute-start.58 = (bf16[256,1536]{1,0:T(8,128)(2,1)S(1)}, bf16[256,1536]{1,0:T(8,128)(2,1)S(1)}, u32[]{:S(2)}, u32[]{:S(2)}) collective-permute-start(bf16[256,1536]{1,0:T(8,128)(2,1)S(1)} %get-tuple-element.739), channel_id=1, source_target_pairs={{3,2},{7,6},{11,10},{15,14},{19,18},{23,22},{27,26},{31,30}} | collective-permute-start | bytes 2359304 | tf_op jit(solution)/shard_map/ppermute | solution.py:83
  579.0 22.1 %collective-permute-start.57 = (bf16[256,1536]{1,0:T(8,128)(2,1)S(1)}, bf16[256,1536]{1,0:T(8,128)(2,1)S(1)}, u32[]{:S(2)}, u32[]{:S(2)}) collective-permute-start(bf16[256,1536]{1,0:T(8,128)(2,1)S(1)} %get-tuple-element.740), channel_id=1, source_target_pairs={{0,1},{4,5},{8,9},{12,13},{16,17},{20,21},{24,25},{28,29}} | collective-permute-start | bytes 2359304 | tf_op jit(solution)/shard_map/ppermute | solution.py:82
  645.6 20.8 %collective-permute-start.66 = (bf16[256,1536]{1,0:T(8,128)(2,1)S(1)}, bf16[256,1536]{1,0:T(8,128)(2,1)S(1)}, u32[]{:S(2)}, u32[]{:S(2)}) collective-permute-start(bf16[256,1536]{1,0:T(8,128)(2,1)S(1)} %multiply_convert_fusion.2.x_ref), channel_id=1, source_target_pairs={{1,0},{2,1},{3,2},{5,4},{6,5},{7,6},{9,8},{10,9},{11,10},{13,12},{... | collective-permute-start | bytes 2359304 | tf_op jit(solution)/shard_map/ppermute | solution.py:115
  749.1 29.2 %collective-permute-start.73 = (f32[128,128]{1,0:T(8,128)S(1)}, f32[128,128]{1,0:T(8,128)S(1)}, u32[]{:S(2)}, u32[]{:S(2)}) collective-permute-start(f32[128,128]{1,0:T(8,128)S(1)} %reshape.657), channel_id=1, source_target_pairs={{0,1},{1,0},{2,3},{3,2},{4,5},{5,4},{6,7},{7,6},{8,9},{9,8},{10,11... | collective-permute-start | bytes 196616 | tf_op jit(solution)/shard_map/ppermute | solution.py:140
  774.2 22.0 %collective-permute-start.72 = (bf16[256,1536]{1,0:T(8,128)(2,1)}, bf16[256,1536]{1,0:T(8,128)(2,1)}, u32[]{:S(2)}, u32[]{:S(2)}) collective-permute-start(bf16[256,1536]{1,0:T(8,128)(2,1)} %get-tuple-element.733), channel_id=1, source_target_pairs={{3,2},{7,6},{11,10},{15,14},{19,18},{23,22},{27,26},{31,30}} | collective-permute-start | bytes 2359304 | tf_op jit(solution)/shard_map/ppermute | solution.py:83
  775.9 20.4 %collective-permute-start.71 = (bf16[256,1536]{1,0:T(8,128)(2,1)}, bf16[256,1536]{1,0:T(8,128)(2,1)}, u32[]{:S(2)}, u32[]{:S(2)}) collective-permute-start(bf16[256,1536]{1,0:T(8,128)(2,1)} %get-tuple-element.734), channel_id=1, source_target_pairs={{0,1},{4,5},{8,9},{12,13},{16,17},{20,21},{24,25},{28,29}} | collective-permute-start | bytes 2359304 | tf_op jit(solution)/shard_map/ppermute | solution.py:82
  799.3 204.3 %reduce-scatter.11.cloned.1.call-start = ((), (), s32[]{:S(2)}) async-start(), calls=%async_computation.17 | async-start | bytes 7962624 | tf_op jit(solution)/shard_map/reduce_scatter | solution.py:1138
  870.7 224.4 %reduce-scatter.13.cloned.1.call-start = ((), (), s32[]{:S(2)}) async-start(), calls=%async_computation.18 | async-start | bytes 5308416 | tf_op jit(solution)/shard_map/reduce_scatter | solution.py:1155
  876.4 22.9 %collective-permute-start.84 = (bf16[256,1536]{1,0:T(8,128)(2,1)}, bf16[256,1536]{1,0:T(8,128)(2,1)S(1)}, u32[]{:S(2)}, u32[]{:S(2)}) collective-permute-start(bf16[256,1536]{1,0:T(8,128)(2,1)} %copy-done.182), channel_id=1, source_target_pairs={{1,0},{2,1},{5,4},{6,5},{9,8},{10,9},{13,12},{14,13},{17,16},{18,1... | collective-permute-start | bytes 2359304 | tf_op jit(solution)/shard_map/ppermute | solution.py:76
  901.7 26.4 %collective-permute-start.94 = (bf16[256,1536]{1,0:T(8,128)(2,1)S(1)}, bf16[256,1536]{1,0:T(8,128)(2,1)S(1)}, u32[]{:S(2)}, u32[]{:S(2)}) collective-permute-start(bf16[256,1536]{1,0:T(8,128)(2,1)S(1)} %get-tuple-element.445), channel_id=1, source_target_pairs={{0,1},{1,2},{4,5},{5,6},{8,9},{9,10},{12,13},{13,14},{16,17},{17,1... | collective-permute-start | bytes 2359304 | tf_op jit(solution)/shard_map/ppermute | solution.py:82
  906.5 21.6 %collective-permute-start.95 = (bf16[256,1536]{1,0:T(8,128)(2,1)S(1)}, bf16[256,1536]{1,0:T(8,128)(2,1)S(1)}, u32[]{:S(2)}, u32[]{:S(2)}) collective-permute-start(bf16[256,1536]{1,0:T(8,128)(2,1)S(1)} %get-tuple-element.446), channel_id=1, source_target_pairs={{2,1},{3,2},{6,5},{7,6},{10,9},{11,10},{14,13},{15,14},{18,17},{19... | collective-permute-start | bytes 2359304 | tf_op jit(solution)/shard_map/ppermute | solution.py:83
  929.7 39.4 %collective-permute-start.96 = (bf16[256,1536]{1,0:T(8,128)(2,1)}, bf16[256,1536]{1,0:T(8,128)(2,1)}, u32[]{:S(2)}, u32[]{:S(2)}) collective-permute-start(bf16[256,1536]{1,0:T(8,128)(2,1)} %get-tuple-element.447), channel_id=1, source_target_pairs={{0,1},{1,2},{2,3},{4,5},{5,6},{6,7},{8,9},{9,10},{10,11},{12,13},{... | collective-permute-start | bytes 2359304 | tf_op jit(solution)/shard_map/ppermute | solution.py:82
  932.4 36.7 %collective-permute-start.97 = (bf16[256,1536]{1,0:T(8,128)(2,1)}, bf16[256,1536]{1,0:T(8,128)(2,1)}, u32[]{:S(2)}, u32[]{:S(2)}) collective-permute-start(bf16[256,1536]{1,0:T(8,128)(2,1)} %get-tuple-element.448), channel_id=1, source_target_pairs={{1,0},{2,1},{3,2},{5,4},{6,5},{7,6},{9,8},{10,9},{11,10},{13,12},{... | collective-permute-start | bytes 2359304 | tf_op jit(solution)/shard_map/ppermute | solution.py:83
  942.0 25.2 %collective-permute-start.93 = (bf16[144,768]{1,0:T(8,128)(2,1)S(1)}, bf16[144,768]{1,0:T(8,128)(2,1)S(1)}, u32[]{:S(2)}, u32[]{:S(2)}) collective-permute-start(bf16[144,768]{1,0:T(8,128)(2,1)S(1)} %maximum_maximum_fusion.2), channel_id=1, source_target_pairs={{24,0},{28,4},{25,1},{29,5},{26,2},{30,6},{27,3},{31,7}} | collective-permute-start | bytes 663560 | tf_op jit(solution)/shard_map/ppermute | solution.py:226
  943.3 21.7 %collective-permute-start.92 = (bf16[144,768]{1,0:T(8,128)(2,1)S(1)}, bf16[144,768]{1,0:T(8,128)(2,1)S(1)}, u32[]{:S(2)}, u32[]{:S(2)}) collective-permute-start(bf16[144,768]{1,0:T(8,128)(2,1)S(1)} %maximum_maximum_fusion.2), channel_id=1, source_target_pairs={{12,0},{16,4},{20,8},{24,12},{28,16},{13,1},{17,5},{21,9},{25,13},... | collective-permute-start | bytes 663560 | tf_op jit(solution)/shard_map/ppermute | solution.py:226
  969.1 205.1 %reduce-scatter.15.cloned.1.call-start = ((), (), s32[]{:S(2)}) async-start(), calls=%async_computation.19 | async-start | bytes 3981312 | tf_op jit(solution)/shard_map/reduce_scatter | solution.py:1190
  1017.4 22.6 %collective-permute-start.99 = (bf16[256,1536]{1,0:T(8,128)(2,1)}, bf16[256,1536]{1,0:T(8,128)(2,1)S(1)}, u32[]{:S(2)}, u32[]{:S(2)}) collective-permute-start(bf16[256,1536]{1,0:T(8,128)(2,1)} %get-tuple-element.722), channel_id=1, source_target_pairs={{0,1},{4,5},{8,9},{12,13},{16,17},{20,21},{24,25},{28,29}} | collective-permute-start | bytes 2359304 | tf_op jit(solution)/shard_map/ppermute | solution.py:82
  1041.7 21.1 %collective-permute-start.101 = (bf16[256,1536]{1,0:T(8,128)(2,1)S(1)}, bf16[256,1536]{1,0:T(8,128)(2,1)S(1)}, u32[]{:S(2)}, u32[]{:S(2)}) collective-permute-start(bf16[256,1536]{1,0:T(8,128)(2,1)S(1)} %get-tuple-element.462), channel_id=1, source_target_pairs={{0,1},{1,2},{4,5},{5,6},{8,9},{9,10},{12,13},{13,14},{16,17},{17,1... | collective-permute-start | bytes 2359304 | tf_op jit(solution)/shard_map/ppermute | solution.py:82
  1064.3 22.7 %collective-permute-start.103 = (bf16[256,1536]{1,0:T(8,128)(2,1)}, bf16[256,1536]{1,0:T(8,128)(2,1)}, u32[]{:S(2)}, u32[]{:S(2)}) collective-permute-start(bf16[256,1536]{1,0:T(8,128)(2,1)} %get-tuple-element.464), channel_id=1, source_target_pairs={{0,1},{1,2},{2,3},{4,5},{5,6},{6,7},{8,9},{9,10},{10,11},{12,13},{... | collective-permute-start | bytes 2359304 | tf_op jit(solution)/shard_map/ppermute | solution.py:82
  1071.7 20.4 %collective-permute-start.104 = (bf16[256,1536]{1,0:T(8,128)(2,1)}, bf16[256,1536]{1,0:T(8,128)(2,1)}, u32[]{:S(2)}, u32[]{:S(2)}) collective-permute-start(bf16[256,1536]{1,0:T(8,128)(2,1)} %get-tuple-element.465), channel_id=1, source_target_pairs={{1,0},{2,1},{3,2},{5,4},{6,5},{7,6},{9,8},{10,9},{11,10},{13,12},{... | collective-permute-start | bytes 2359304 | tf_op jit(solution)/shard_map/ppermute | solution.py:83
  1073.1 325.8 %reduce-scatter.17.cloned.1.call-start = ((), (), s32[]{:S(2)}) async-start(), calls=%async_computation.20 | async-start | bytes 15925248 | tf_op jit(solution)/shard_map/reduce_scatter | solution.py:1105
  1174.2 31.1 %collective-permute-start.113 = (f32[128,128]{1,0:T(8,128)S(1)}, f32[128,128]{1,0:T(8,128)S(1)}, u32[]{:S(2)}, u32[]{:S(2)}) collective-permute-start(f32[128,128]{1,0:T(8,128)S(1)} %reshape.664), channel_id=1, source_target_pairs={{0,1},{1,0},{2,3},{3,2},{4,5},{5,4},{6,7},{7,6},{8,9},{9,8},{10,11... | collective-permute-start | bytes 196616 | tf_op jit(solution)/shard_map/ppermute | solution.py:140
  1197.7 25.5 %collective-permute-start.112 = (bf16[256,1536]{1,0:T(8,128)(2,1)}, bf16[256,1536]{1,0:T(8,128)(2,1)}, u32[]{:S(2)}, u32[]{:S(2)}) collective-permute-start(bf16[256,1536]{1,0:T(8,128)(2,1)} %get-tuple-element.715), channel_id=1, source_target_pairs={{3,2},{7,6},{11,10},{15,14},{19,18},{23,22},{27,26},{31,30}} | collective-permute-start | bytes 2359304 | tf_op jit(solution)/shard_map/ppermute | solution.py:83
  1199.4 23.8 %collective-permute-start.111 = (bf16[256,1536]{1,0:T(8,128)(2,1)}, bf16[256,1536]{1,0:T(8,128)(2,1)}, u32[]{:S(2)}, u32[]{:S(2)}) collective-permute-start(bf16[256,1536]{1,0:T(8,128)(2,1)} %get-tuple-element.716), channel_id=1, source_target_pairs={{0,1},{4,5},{8,9},{12,13},{16,17},{20,21},{24,25},{28,29}} | collective-permute-start | bytes 2359304 | tf_op jit(solution)/shard_map/ppermute | solution.py:82
  1226.6 222.1 %reduce-scatter.19.cloned.1.call-start = ((), (), s32[]{:S(2)}) async-start(), calls=%async_computation.21 | async-start | bytes 7962624 | tf_op jit(solution)/shard_map/reduce_scatter | solution.py:1138
  1226.7 24.3 %collective-permute-start.115 = (bf16[256,1536]{1,0:T(8,128)(2,1)}, bf16[256,1536]{1,0:T(8,128)(2,1)}, u32[]{:S(2)}, u32[]{:S(2)}) collective-permute-start(bf16[256,1536]{1,0:T(8,128)(2,1)} %get-tuple-element.493), channel_id=1, source_target_pairs={{0,1},{1,2},{4,5},{5,6},{8,9},{9,10},{12,13},{13,14},{16,17},{17,1... | collective-permute-start | bytes 2359304 | tf_op jit(solution)/shard_map/ppermute | solution.py:82
  1229.7 21.3 %collective-permute-start.116 = (bf16[256,1536]{1,0:T(8,128)(2,1)}, bf16[256,1536]{1,0:T(8,128)(2,1)}, u32[]{:S(2)}, u32[]{:S(2)}) collective-permute-start(bf16[256,1536]{1,0:T(8,128)(2,1)} %get-tuple-element.494), channel_id=1, source_target_pairs={{2,1},{3,2},{6,5},{7,6},{10,9},{11,10},{14,13},{15,14},{18,17},{19... | collective-permute-start | bytes 2359304 | tf_op jit(solution)/shard_map/ppermute | solution.py:83
  1255.1 29.1 %collective-permute-start.117 = (bf16[256,1536]{1,0:T(8,128)(2,1)}, bf16[256,1536]{1,0:T(8,128)(2,1)}, u32[]{:S(2)}, u32[]{:S(2)}) collective-permute-start(bf16[256,1536]{1,0:T(8,128)(2,1)} %get-tuple-element.495), channel_id=1, source_target_pairs={{0,1},{1,2},{2,3},{4,5},{5,6},{6,7},{8,9},{9,10},{10,11},{12,13},{... | collective-permute-start | bytes 2359304 | tf_op jit(solution)/shard_map/ppermute | solution.py:82
  1260.1 24.1 %collective-permute-start.118 = (bf16[256,1536]{1,0:T(8,128)(2,1)}, bf16[256,1536]{1,0:T(8,128)(2,1)}, u32[]{:S(2)}, u32[]{:S(2)}) collective-permute-start(bf16[256,1536]{1,0:T(8,128)(2,1)} %get-tuple-element.496), channel_id=1, source_target_pairs={{1,0},{2,1},{3,2},{5,4},{6,5},{7,6},{9,8},{10,9},{11,10},{13,12},{... | collective-permute-start | bytes 2359304 | tf_op jit(solution)/shard_map/ppermute | solution.py:83
  1304.3 181.2 %reduce-scatter.21.cloned.1.call-start = ((), (), s32[]{:S(2)}) async-start(), calls=%async_computation.22 | async-start | bytes 5308416 | tf_op jit(solution)/shard_map/reduce_scatter | solution.py:1155
  1305.2 30.0 %collective-permute-start.127 = (bf16[256,1536]{1,0:T(8,128)(2,1)}, bf16[256,1536]{1,0:T(8,128)(2,1)S(1)}, u32[]{:S(2)}, u32[]{:S(2)}) collective-permute-start(bf16[256,1536]{1,0:T(8,128)(2,1)} %collective-permute-done.120), channel_id=1, source_target_pairs={{1,0},{2,1},{5,4},{6,5},{9,8},{10,9},{13,12},{14,13},{17,16},{18,1... | collective-permute-start | bytes 2359304 | tf_op jit(solution)/shard_map/ppermute | solution.py:76
  1398.9 177.4 %reduce-scatter.23.cloned.1.call-start = ((), (), s32[]{:S(2)}) async-start(), calls=%async_computation.23 | async-start | bytes 3981312 | tf_op jit(solution)/shard_map/reduce_scatter | solution.py:1190
  1485.5 21.9 %collective-permute-start.140 = (bf16[256,1536]{1,0:T(8,128)(2,1)}, bf16[256,1536]{1,0:T(8,128)(2,1)}, u32[]{:S(2)}, u32[]{:S(2)}) collective-permute-start(bf16[256,1536]{1,0:T(8,128)(2,1)} %get-tuple-element.529), channel_id=1, source_target_pairs={{0,1},{1,2},{4,5},{5,6},{8,9},{9,10},{12,13},{13,14},{16,17},{17,1... | collective-permute-start | bytes 2359304 | tf_op jit(solution)/shard_map/ppermute | solution.py:82
  1510.4 38.6 %collective-permute-start.146 = (f32[16,768]{1,0:T(8,128)S(1)}, f32[16,768]{1,0:T(8,128)}, u32[]{:S(2)}, u32[]{:S(2)}) collective-permute-start(f32[16,768]{1,0:T(8,128)S(1)} %constant_dynamic-update-slice_fusion), channel_id=1, source_target_pairs={{0,4},{4,0},{8,12},{12,8},{16,20},{20,16},{24,28},{28,24},{1,5},{5... | collective-permute-start | bytes 147464 | tf_op jit(solution)/shard_map/ppermute | solution.py:140
  1511.5 54.1 %collective-permute-start.142 = (bf16[256,1536]{1,0:T(8,128)(2,1)}, bf16[256,1536]{1,0:T(8,128)(2,1)}, u32[]{:S(2)}, u32[]{:S(2)}) collective-permute-start(bf16[256,1536]{1,0:T(8,128)(2,1)} %get-tuple-element.535), channel_id=1, source_target_pairs={{0,1},{1,2},{2,3},{4,5},{5,6},{6,7},{8,9},{9,10},{10,11},{12,13},{... | collective-permute-start | bytes 2359304 | tf_op jit(solution)/shard_map/ppermute | solution.py:82
  1549.0 20.4 %collective-permute-start.143 = (bf16[256,1536]{1,0:T(8,128)(2,1)}, bf16[256,1536]{1,0:T(8,128)(2,1)S(1)}, u32[]{:S(2)}, u32[]{:S(2)}) collective-permute-start(bf16[256,1536]{1,0:T(8,128)(2,1)} %get-tuple-element.536), channel_id=1, source_target_pairs={{1,0},{2,1},{3,2},{5,4},{6,5},{7,6},{9,8},{10,9},{11,10},{13,12},{... | collective-permute-start | bytes 2359304 | tf_op jit(solution)/shard_map/ppermute | solution.py:83
  (384 other events, 6360.0 us)
Sparse Core Ops, SparseCore 0:
  51.2 46.7 all-gather.8
  100.4 29.2 all-gather.10
  165.9 80.9 all-gather.12
  249.2 48.8 all-gather.14
  347.9 59.9 all-gather.16
  471.3 42.5 all-gather.18
  552.9 77.9 all-gather.22
  632.7 48.8 all-gather.20
  799.4 112.0 reduce-scatter.8
  914.9 75.0 reduce-scatter.10
  993.8 53.8 reduce-scatter.12
  1073.2 48.4 reduce-scatter.14
  1226.7 107.5 reduce-scatter.16
  1337.7 78.0 reduce-scatter.18
  1420.1 54.1 reduce-scatter.20
  1497.4 49.2 reduce-scatter.22

commit v4 on v3

--- a/solution.py
+++ b/solution.py
@@ -1148,10 +1148,6 @@
         carried, early, up_grad = tie(carried, early, up_grad)
         if top:
             carried, residual = tie(carried, residual)
-        else:
-            carried, above["inner"], above["common"] = tie(
-                carried, above["inner"], above["common"]
-            )
         early = lax.psum_scatter(early, "seq", scatter_dimension=0, tiled=True)
         dp, last, back, tacc, hacc = mixer_scan_back(
             k["pu"], k["edge"], dz, k["taps"], k["head"], k["head_rows"], aux, auxr, ex,
@@ -1183,9 +1179,11 @@
             _, d_own, riders = hop_both(
                 None,
                 d_normed.astype(bf16),
-                (late, early),
+                (late, early, above["inner"], above["common"]),
                 (sums, above["sums"], up_grad),
             )
+            above["inner"], above["common"] = riders[2:4]
+            riders = riders[:2] + riders[4:]
             late, early, sums = riders[:3]
         late = lax.psum_scatter(late, "seq", scatter_dimension=0, tiled=True)
         if top:

time: 1610 us -> 1610 us (level)
    unnamed x577 -> x573, local copies, waits for them, and re-layouts: 57 us -> 56.8 us
  transfers between devices with their start and end apart: 168 -> 168, of which waited for: 60 -> 62; matrix products, arithmetic and copies ran while one was open for 32% -> 31% of each run, Pallas kernels for 15% -> 15%
where the time goes in v4:
time: 1610 us; the launch traced here: 1600 us
  waiting for transfers between devices  402 us (25%)
  starting transfers between devices  345 us (21%)
  Pallas kernels  260 us (16%)
  matrix products  219 us (14%)
  local copies, waits for them, and re-layouts  192 us (12%)
  other arithmetic  160 us (10%)
  between operations  20.1 us (1%)
    dot_general x28, matrix products, mm(): lax.dot_general(a, b, dims, precision=precision, preferred_element_type=f32)  219 us
    ppermute x15, waiting for transfers between devices, hop_both(): lax.ppermute(held[1], axis, [(i, i - 1) for i in range(1, n - step + 1)])  125 us
    ppermute x24, waiting for transfers between devices, hop_both(): right = lax.ppermute(held[0], axis, [(i, i + 1) for i in range(0, s)])  117 us
    ppermute x24, starting transfers between devices, hop_both(): right = lax.ppermute(held[0], axis, [(i, i + 1) for i in range(0, s)])  116 us
    pallas_call x8, Pallas kernels, experts_up(): pl.pallas_call(up_kernel, grid_spec=pltpu.PrefetchScalarGridSpec(num_scal...  102 us
    pallas_call x5, Pallas kernels, experts_down_back(): pl.pallas_call(down_back_kernel, grid_spec=pltpu.PrefetchScalarGridSpec(n...  65.3 us
    ppermute x24, starting transfers between devices, shift_seq(): return lax.ppermute(v, 'seq', [(i, i + steps) for i in range(first, last)])  60.5 us
    unnamed x573, local copies, waits for them, and re-layouts  56.8 us
  transfers between devices with their start and end apart: 168, of which 62 were waited for; matrix products, arithmetic and copies ran while one was open for 31% of the time, Pallas kernels for 15%

profile of v4, /device:TPU:0, one launch (start us, length us, event | category | flops | bytes accessed | tf_op | source)
XLA Modules:
  0.0 1598.6 jit_solution(9700948663978573623)
XLA Ops:
  12.7 6.4 collective-permute-start
  26.0 8.2 collective-permute-done.1
  76.4 7.6 collective-permute-done.3
  113.0 7.2 fusion.6.u_ref.bc_ref.dt_ref.uh_ref.bch_ref
  122.3 6.6 mixer_states.2
  171.2 6.6 collective-permute-start.17
  209.4 10.8 collective-permute-done.33
  264.2 7.0 collective-permute-done.28
  282.7 12.7 experts_up.8
  299.8 12.6 experts_up.9
  318.0 12.6 experts_up.10
  335.1 12.7 experts_up.11
  347.9 11.1 convolution_convert_fusion.10
  364.8 12.6 collective-permute-done.39
  383.1 9.8 collective-permute-done.41
  394.5 7.3 collective-permute-start.43
  427.8 8.0 collective-permute-done.46
  439.2 29.3 %collective-permute-done.48 = bf16[256,1536]{1,0:T(8,128)(2,1)} collective-permute-done((bf16[256,1536]{1,0:T(8,128)(2,1)S(1)}, bf16[256,1536]{1,0:T(8,128)(2,1)}, u32[]{:S(2)}, u32[]{:S(2)}) %collective-permute-start.48) | collective-permute-done | bytes 786464 | tf_op jit(solution)/shard_map/ppermute | solution.py:76
  471.7 12.5 collective-permute-done.50
  490.4 8.3 fusion.4.u_ref.bc_ref.dt_ref.uh_ref.bch_ref
  500.9 6.6 mixer_states.3
  507.9 17.1 %collective-permute-start.54 = (bf16[144,768]{1,0:T(8,128)(2,1)S(1)}, bf16[144,768]{1,0:T(8,128)(2,1)S(1)}, u32[]{:S(2)}, u32[]{:S(2)}) collective-permute-start(bf16[144,768]{1,0:T(8,128)(2,1)S(1)} %fusion.52), channel_id=1, source_target_pairs={{0,12},{4,16},{8,20},{12,24},{16,28},{1,13},{5,17},{9,21},{13,25},... | collective-permute-start | bytes 663560 | tf_op jit(solution)/shard_map/ppermute | solution.py:226
  580.8 16.0 collective-permute-done.59
  607.0 13.5 collective-permute-done.61
  620.9 6.4 collective-permute-start.63
  628.6 12.0 collective-permute-done.63
  653.5 13.1 experts_up.12
  670.7 12.7 experts_up.13
  687.0 12.7 experts_up.14
  703.7 12.8 experts_up.15
  722.5 23.0 %experts_down_back.5 = (bf16[1024,4608]{1,0:T(8,128)(2,1)S(1)}, f32[1024,128]{1,0:T(8,128)S(1)}) custom-call(s32[1]{0:T(128)} %constant.179.clone.1.at_ref, bf16[1024,1536]{1,0:T(8,128)(2,1)S(1)} %copy-done.11, bf16[2304,1536]{1,0:T(8,128)(2,1)S(1)} %copy-done.25, bf16[1024,4608]{1,0:T(8,128)(2,1)} %get-tuple-element.415.h_ref, f32[1024,128]{1,0:T(8,128)S(1)} %copy-done.19, ...), custom_call_target="tpu_custom_call" | custom-call | tf_op jit(solution)/shard_map/experts_down_back/pallas_call | solution.py:791
  751.7 21.5 %convolution_convert_fusion.7 = bf16[1024,1536]{1,0:T(8,128)(2,1)S(1)} fusion(bf16[1024,4608]{1,0:T(8,128)(2,1)} %copy-done.79, bf16[1536,4608]{1,0:T(8,128)(2,1)} %all-gather.23.cloned.1.call-done.w_ref), kind=kOutput, calls=%fused_computation.17 | convolution fusion | flops 14497087488 | bytes 26738688 | tf_op jit(solution)/shard_map/dot_general | solution.py:31
  778.7 17.7 %convolution_convert_fusion.1 = bf16[1536,4608]{1,0:T(8,128)(2,1)} fusion(bf16[1024,4608]{1,0:T(8,128)(2,1)S(1)} %copy-done.80, bf16[256,1536]{1,0:T(8,128)(2,1)S(1)} %copy-done.164, bf16[256,1536]{1,0:T(8,128)(2,1)S(1)} %copy-done.163, bf16[256,1536]{1,0:T(8,128)(2,1)S(1)} %copy-done.162, bf16[256,1536]{1,0:T(8,128)(2,1)S(1)} %copy-done.161), kind=kOutput, calls=%fused_computation.1 | convolution fusion | flops 14515175424 | bytes 26738688 | tf_op jit(solution)/shard_map/dot_general | solution.py:31
  799.5 6.7 collective-permute-start.75
  807.8 11.7 convolution_convert_fusion.3
  828.5 13.1 convolution_convert_fusion.8
  859.8 9.1 collective-permute-done.82
  877.3 7.0 collective-permute-done.85
  886.0 11.9 collective-permute-done.84
  905.9 6.7 collective-permute-done.88
  916.1 6.1 mixer_gate_back.2
  948.1 17.0 %collective-permute-done.92 = bf16[144,768]{1,0:T(8,128)(2,1)S(1)} collective-permute-done((bf16[144,768]{1,0:T(8,128)(2,1)S(1)}, bf16[144,768]{1,0:T(8,128)(2,1)S(1)}, u32[]{:S(2)}, u32[]{:S(2)}) %collective-permute-start.92) | collective-permute-done | bytes 221216 | tf_op jit(solution)/shard_map/ppermute | solution.py:226
  973.0 27.0 %mixer_scan_back.2 = (bf16[1024,2048]{1,0:T(8,128)(2,1)}, f32[8,1024]{1,0:T(8,128)S(1)}, f32[8,1024]{1,0:T(8,128)S(1)}, f32[8,1024]{1,0:T(8,128)S(1)}, f32[8,128]{1,0:T(8,128)S(1)}) custom-call(f32[1024,1152]{1,0:T(8,128)} %copy-done.1, f32[1024,1152]{1,0:T(8,128)} %copy-done.1, f32[1024,1152]{1,0:T(8,128)} %copy-done.1, f32[1024,1152]{1,0:T(8,128)} %copy-done.1, ...), custom_call_target="tpu_custom_call" | custom-call | tf_op jit(solution)/shard_map/mixer_scan_back/pallas_call | solution.py:666
  1003.7 11.6 fusion.3
  1030.2 9.6 collective-permute-done.99
  1046.6 16.0 collective-permute-done.101
  1064.1 7.7 collective-permute-start.103
  1073.1 14.1 collective-permute-done.103
  1105.1 10.6 experts_down_back.6
  1123.2 10.5 experts_down_back.7
  1133.8 8.0 collective-permute-done.108
  1145.9 10.6 experts_down_back.8
  1164.9 10.6 experts_down_back.9
  1176.8 20.5 %convolution_convert_fusion.6 = bf16[1024,1536]{1,0:T(8,128)(2,1)S(1)} fusion(bf16[1024,4608]{1,0:T(8,128)(2,1)} %get-tuple-element.489, bf16[1536,4608]{1,0:T(8,128)(2,1)} %all-gather.13.cloned.1.call-done.w_ref), kind=kOutput, calls=%fused_computation.16 | convolution fusion | flops 14497087488 | bytes 26738688 | tf_op jit(solution)/shard_map/dot_general | solution.py:31
  1208.0 17.8 %convolution_convert_fusion = bf16[1536,4608]{1,0:T(8,128)(2,1)} fusion(bf16[1024,4608]{1,0:T(8,128)(2,1)S(1)} %copy-done.85, bf16[256,1536]{1,0:T(8,128)(2,1)S(1)} %copy-done.155, bf16[256,1536]{1,0:T(8,128)(2,1)S(1)} %copy-done.154, bf16[256,1536]{1,0:T(8,128)(2,1)S(1)} %copy-done.153, bf16[256,1536]{1,0:T(8,128)(2,1)S(1)} %copy-done.152), kind=kOutput, calls=%fused_computation | convolution fusion | flops 14515175424 | bytes 26738688 | tf_op jit(solution)/shard_map/dot_general | solution.py:31
  1233.5 12.5 convolution_convert_fusion.2
  1256.1 6.1 collective-permute-start.117
  1310.2 26.0 %collective-permute-done.127 = bf16[256,1536]{1,0:T(8,128)(2,1)S(1)} collective-permute-done((bf16[256,1536]{1,0:T(8,128)(2,1)}, bf16[256,1536]{1,0:T(8,128)(2,1)S(1)}, u32[]{:S(2)}, u32[]{:S(2)}) %collective-permute-start.127) | collective-permute-done | bytes 786464 | tf_op jit(solution)/shard_map/ppermute | solution.py:76
  1338.4 12.4 collective-permute-done.129
  1384.2 12.1 collective-permute-done.133
  1418.1 27.0 %mixer_scan_back.3 = (bf16[1024,2048]{1,0:T(8,128)(2,1)}, f32[8,1024]{1,0:T(8,128)S(1)}, f32[8,1024]{1,0:T(8,128)S(1)}, f32[8,1024]{1,0:T(8,128)S(1)}, f32[8,128]{1,0:T(8,128)S(1)}) custom-call(f32[1024,1152]{1,0:T(8,128)} %copy-done, f32[1024,1152]{1,0:T(8,128)} %copy-done, f32[1024,1152]{1,0:T(8,128)} %copy-done, f32[1024,1152]{1,0:T(8,128)} %copy-done, ...), custom_call_target="tpu_custom_call" | custom-call | tf_op jit(solution)/shard_map/mixer_scan_back/pallas_call | solution.py:666
  1448.8 10.8 fusion.1
  1497.1 11.1 collective-permute-done.140
  1512.8 6.4 collective-permute-start.142
  (1312 shorter events, 795.2 us)
Async XLA Ops:
  7.2 104.0 %all-gather.9.cloned.1.call-start = ((), (), s32[]{:S(2)}) async-start(), calls=%async_computation.8 | async-start | bytes 7077888 | tf_op jit(solution)/shard_map/all_gather | solution.py:928
  11.4 22.8 %collective-permute-start.1 = (bf16[256,1536]{1,0:T(8,128)(2,1)}, bf16[256,1536]{1,0:T(8,128)(2,1)}, u32[]{:S(2)}, u32[]{:S(2)}) collective-permute-start(bf16[256,1536]{1,0:T(8,128)(2,1)} %multiply_convert_fusion.5), channel_id=1, source_target_pairs={{1,0},{2,1},{3,2},{5,4},{6,5},{7,6},{9,8},{10,9},{11,10},{13,12},{... | collective-permute-start | bytes 2359304 | tf_op jit(solution)/shard_map/ppermute | solution.py:76
  12.7 22.7 %collective-permute-start = (bf16[256,1536]{1,0:T(8,128)(2,1)}, bf16[256,1536]{1,0:T(8,128)(2,1)}, u32[]{:S(2)}, u32[]{:S(2)}) collective-permute-start(bf16[256,1536]{1,0:T(8,128)(2,1)} %multiply_convert_fusion.5), channel_id=1, source_target_pairs={{0,1},{1,2},{2,3},{4,5},{5,6},{6,7},{8,9},{9,10},{10,11},{12,13},{... | collective-permute-start | bytes 2359304 | tf_op jit(solution)/shard_map/ppermute | solution.py:75
  51.1 142.1 %all-gather.11.cloned.1.call-start = ((), (), s32[]{:S(2)}) async-start(), calls=%async_computation.9 | async-start | bytes 2654208 | tf_op jit(solution)/shard_map/all_gather | solution.py:928
  53.1 229.6 %all-gather.13.cloned.1.call-start = ((), (), s32[]{:S(2)}) async-start(), calls=%async_computation.10 | async-start | bytes 15925248 | tf_op jit(solution)/shard_map/all_gather | solution.py:928
  57.5 32.3 %collective-permute-start.6 = (bf16[2,48,512]{2,1,0:T(8,128)(2,1)}, bf16[2,48,512]{2,1,0:T(8,128)(2,1)S(1)}, u32[]{:S(2)}, u32[]{:S(2)}) collective-permute-start(bf16[2,48,512]{2,1,0:T(8,128)(2,1)} %get-tuple-element.814), channel_id=1, source_target_pairs={{0,3},{1,2},{2,1},{3,0},{4,7},{5,6},{6,5},{7,4},{8,11},{9,10},{10,... | collective-permute-start | bytes 294920 | tf_op jit(solution)/shard_map/ppermute | solution.py:177
  61.1 28.8 %collective-permute-start.8 = (bf16[2,48,512]{2,1,0:T(8,128)(2,1)}, bf16[2,48,512]{2,1,0:T(8,128)(2,1)}, u32[]{:S(2)}, u32[]{:S(2)}) collective-permute-start(bf16[2,48,512]{2,1,0:T(8,128)(2,1)} %get-tuple-element.815), channel_id=1, source_target_pairs={{0,1},{1,0},{2,3},{3,2},{4,5},{5,4},{6,7},{7,6},{8,9},{9,8},{10,11... | collective-permute-start | bytes 294920 | tf_op jit(solution)/shard_map/ppermute | solution.py:177
  61.1 29.4 %collective-permute-start.7 = (bf16[2,48,512]{2,1,0:T(8,128)(2,1)}, bf16[2,48,512]{2,1,0:T(8,128)(2,1)}, u32[]{:S(2)}, u32[]{:S(2)}) collective-permute-start(bf16[2,48,512]{2,1,0:T(8,128)(2,1)} %get-tuple-element.816), channel_id=1, source_target_pairs={{0,2},{1,3},{2,0},{3,1},{4,6},{5,7},{6,4},{7,5},{8,10},{9,11},{10,... | collective-permute-start | bytes 294920 | tf_op jit(solution)/shard_map/ppermute | solution.py:177
  63.4 20.5 %collective-permute-start.3 = (bf16[256,1536]{1,0:T(8,128)(2,1)}, bf16[256,1536]{1,0:T(8,128)(2,1)}, u32[]{:S(2)}, u32[]{:S(2)}) collective-permute-start(bf16[256,1536]{1,0:T(8,128)(2,1)} %collective-permute-done.1), channel_id=1, source_target_pairs={{1,0},{2,1},{5,4},{6,5},{9,8},{10,9},{13,12},{14,13},{17,16},{18,1... | collective-permute-start | bytes 2359304 | tf_op jit(solution)/shard_map/ppermute | solution.py:76
  84.0 22.7 %collective-permute-start.4 = (bf16[256,1536]{1,0:T(8,128)(2,1)}, bf16[256,1536]{1,0:T(8,128)(2,1)}, u32[]{:S(2)}, u32[]{:S(2)}) collective-permute-start(bf16[256,1536]{1,0:T(8,128)(2,1)} %collective-permute-done.2), channel_id=1, source_target_pairs={{2,3},{6,7},{10,11},{14,15},{18,19},{22,23},{26,27},{30,31}} | collective-permute-start | bytes 2359304 | tf_op jit(solution)/shard_map/ppermute | solution.py:75
  85.5 21.2 %collective-permute-start.5 = (bf16[256,1536]{1,0:T(8,128)(2,1)}, bf16[256,1536]{1,0:T(8,128)(2,1)}, u32[]{:S(2)}, u32[]{:S(2)}) collective-permute-start(bf16[256,1536]{1,0:T(8,128)(2,1)} %collective-permute-done.3), channel_id=1, source_target_pairs={{1,0},{5,4},{9,8},{13,12},{17,16},{21,20},{25,24},{29,28}} | collective-permute-start | bytes 2359304 | tf_op jit(solution)/shard_map/ppermute | solution.py:76
  129.3 24.4 %collective-permute-start.14 = (bf16[144,768]{1,0:T(8,128)(2,1)S(1)}, bf16[144,768]{1,0:T(8,128)(2,1)S(1)}, u32[]{:S(2)}, u32[]{:S(2)}) collective-permute-start(bf16[144,768]{1,0:T(8,128)(2,1)S(1)} %fusion.54), channel_id=1, source_target_pairs={{0,12},{4,16},{8,20},{12,24},{16,28},{1,13},{5,17},{9,21},{13,25},... | collective-permute-start | bytes 663560 | tf_op jit(solution)/shard_map/ppermute | solution.py:226
  165.8 182.0 %all-gather.15.cloned.1.call-start = ((), (), s32[]{:S(2)}) async-start(), calls=%async_computation.11 | async-start | bytes 7962624 | tf_op jit(solution)/shard_map/all_gather | solution.py:928
  166.4 322.0 %all-gather.17.cloned.1.call-start = ((), (), s32[]{:S(2)}) async-start(), calls=%async_computation.12 | async-start | bytes 7077888 | tf_op jit(solution)/shard_map/all_gather | solution.py:928
  169.9 32.8 %collective-permute-start.18 = (bf16[256,1536]{1,0:T(8,128)(2,1)}, bf16[256,1536]{1,0:T(8,128)(2,1)}, u32[]{:S(2)}, u32[]{:S(2)}) collective-permute-start(bf16[256,1536]{1,0:T(8,128)(2,1)} %convert_element_type.996), channel_id=1, source_target_pairs={{1,0},{2,1},{3,2},{5,4},{6,5},{7,6},{9,8},{10,9},{11,10},{13,12},{... | collective-permute-start | bytes 2359304 | tf_op jit(solution)/shard_map/ppermute | solution.py:76
  171.2 31.5 %collective-permute-start.17 = (bf16[256,1536]{1,0:T(8,128)(2,1)}, bf16[256,1536]{1,0:T(8,128)(2,1)}, u32[]{:S(2)}, u32[]{:S(2)}) collective-permute-start(bf16[256,1536]{1,0:T(8,128)(2,1)} %convert_element_type.996), channel_id=1, source_target_pairs={{0,1},{1,2},{2,3},{4,5},{5,6},{6,7},{8,9},{9,10},{10,11},{12,13},{... | collective-permute-start | bytes 2359304 | tf_op jit(solution)/shard_map/ppermute | solution.py:75
  202.6 21.9 %collective-permute-start.23 = (bf16[256,1536]{1,0:T(8,128)(2,1)}, bf16[256,1536]{1,0:T(8,128)(2,1)S(1)}, u32[]{:S(2)}, u32[]{:S(2)}) collective-permute-start(bf16[256,1536]{1,0:T(8,128)(2,1)} %get-tuple-element.316), channel_id=1, source_target_pairs={{0,1},{4,5},{8,9},{12,13},{16,17},{20,21},{24,25},{28,29}} | collective-permute-start | bytes 2359304 | tf_op jit(solution)/shard_map/ppermute | solution.py:82
  207.3 21.3 %collective-permute-start.21 = (bf16[256,1536]{1,0:T(8,128)(2,1)}, bf16[256,1536]{1,0:T(8,128)(2,1)S(1)}, u32[]{:S(2)}, u32[]{:S(2)}) collective-permute-start(bf16[256,1536]{1,0:T(8,128)(2,1)} %collective-permute-done.17), channel_id=1, source_target_pairs={{1,2},{2,3},{5,6},{6,7},{9,10},{10,11},{13,14},{14,15},{17,18},{18... | collective-permute-start | bytes 2359304 | tf_op jit(solution)/shard_map/ppermute | solution.py:75
  208.1 20.9 %collective-permute-start.22 = (bf16[256,1536]{1,0:T(8,128)(2,1)}, bf16[256,1536]{1,0:T(8,128)(2,1)S(1)}, u32[]{:S(2)}, u32[]{:S(2)}) collective-permute-start(bf16[256,1536]{1,0:T(8,128)(2,1)} %collective-permute-done.18), channel_id=1, source_target_pairs={{1,0},{2,1},{5,4},{6,5},{9,8},{10,9},{13,12},{14,13},{17,16},{18,1... | collective-permute-start | bytes 2359304 | tf_op jit(solution)/shard_map/ppermute | solution.py:76
  273.8 21.5 %collective-permute-start.32 = (bf16[256,1536]{1,0:T(8,128)(2,1)S(1)}, bf16[256,1536]{1,0:T(8,128)(2,1)}, u32[]{:S(2)}, u32[]{:S(2)}) collective-permute-start(bf16[256,1536]{1,0:T(8,128)(2,1)S(1)} %multiply_convert_fusion.4.x_ref), channel_id=1, source_target_pairs={{1,0},{2,1},{3,2},{5,4},{6,5},{7,6},{9,8},{10,9},{11,10},{13,12},{... | collective-permute-start | bytes 2359304 | tf_op jit(solution)/shard_map/ppermute | solution.py:115
  347.8 225.5 %all-gather.19.cloned.1.call-start = ((), (), s32[]{:S(2)}) async-start(), calls=%async_computation.13 | async-start | bytes 2654208 | tf_op jit(solution)/shard_map/all_gather | solution.py:928
  394.5 24.4 %collective-permute-start.43 = (bf16[256,1536]{1,0:T(8,128)(2,1)}, bf16[256,1536]{1,0:T(8,128)(2,1)}, u32[]{:S(2)}, u32[]{:S(2)}) collective-permute-start(bf16[256,1536]{1,0:T(8,128)(2,1)} %get-tuple-element.356), channel_id=1, source_target_pairs={{0,1},{1,2},{2,3},{4,5},{5,6},{6,7},{8,9},{9,10},{10,11},{12,13},{... | collective-permute-start | bytes 2359304 | tf_op jit(solution)/shard_map/ppermute | solution.py:82
  437.9 30.6 %collective-permute-start.48 = (bf16[256,1536]{1,0:T(8,128)(2,1)S(1)}, bf16[256,1536]{1,0:T(8,128)(2,1)}, u32[]{:S(2)}, u32[]{:S(2)}) collective-permute-start(bf16[256,1536]{1,0:T(8,128)(2,1)S(1)} %collective-permute-done.46), channel_id=1, source_target_pairs={{1,0},{2,1},{5,4},{6,5},{9,8},{10,9},{13,12},{14,13},{17,16},{18,1... | collective-permute-start | bytes 2359304 | tf_op jit(solution)/shard_map/ppermute | solution.py:76
  471.4 182.1 %all-gather.23.cloned.1.call-start = ((), (), s32[]{:S(2)}) async-start(), calls=%async_computation.15 | async-start | bytes 15925248 | tf_op jit(solution)/shard_map/all_gather | solution.py:928
  507.9 34.2 %collective-permute-start.54 = (bf16[144,768]{1,0:T(8,128)(2,1)S(1)}, bf16[144,768]{1,0:T(8,128)(2,1)S(1)}, u32[]{:S(2)}, u32[]{:S(2)}) collective-permute-start(bf16[144,768]{1,0:T(8,128)(2,1)S(1)} %fusion.52), channel_id=1, source_target_pairs={{0,12},{4,16},{8,20},{12,24},{16,28},{1,13},{5,17},{9,21},{13,25},... | collective-permute-start | bytes 663560 | tf_op jit(solution)/shard_map/ppermute | solution.py:226
  552.9 163.6 %all-gather.21.cloned.1.call-start = ((), (), s32[]{:S(2)}) async-start(), calls=%async_computation.14 | async-start | bytes 7962624 | tf_op jit(solution)/shard_map/all_gather | solution.py:928
  553.6 415.4 %reduce-scatter.9.cloned.1.call-start = ((), (), s32[]{:S(2)}) async-start(), calls=%async_computation.16 | async-start | bytes 15925248 | tf_op jit(solution)/shard_map/reduce_scatter | solution.py:1105
  578.3 23.0 %collective-permute-start.58 = (bf16[256,1536]{1,0:T(8,128)(2,1)S(1)}, bf16[256,1536]{1,0:T(8,128)(2,1)S(1)}, u32[]{:S(2)}, u32[]{:S(2)}) collective-permute-start(bf16[256,1536]{1,0:T(8,128)(2,1)S(1)} %get-tuple-element.737), channel_id=1, source_target_pairs={{3,2},{7,6},{11,10},{15,14},{19,18},{23,22},{27,26},{31,30}} | collective-permute-start | bytes 2359304 | tf_op jit(solution)/shard_map/ppermute | solution.py:83
  579.1 22.2 %collective-permute-start.57 = (bf16[256,1536]{1,0:T(8,128)(2,1)S(1)}, bf16[256,1536]{1,0:T(8,128)(2,1)S(1)}, u32[]{:S(2)}, u32[]{:S(2)}) collective-permute-start(bf16[256,1536]{1,0:T(8,128)(2,1)S(1)} %get-tuple-element.738), channel_id=1, source_target_pairs={{0,1},{4,5},{8,9},{12,13},{16,17},{20,21},{24,25},{28,29}} | collective-permute-start | bytes 2359304 | tf_op jit(solution)/shard_map/ppermute | solution.py:82
  645.8 20.7 %collective-permute-start.66 = (bf16[256,1536]{1,0:T(8,128)(2,1)S(1)}, bf16[256,1536]{1,0:T(8,128)(2,1)S(1)}, u32[]{:S(2)}, u32[]{:S(2)}) collective-permute-start(bf16[256,1536]{1,0:T(8,128)(2,1)S(1)} %multiply_convert_fusion.2.x_ref), channel_id=1, source_target_pairs={{1,0},{2,1},{3,2},{5,4},{6,5},{7,6},{9,8},{10,9},{11,10},{13,12},{... | collective-permute-start | bytes 2359304 | tf_op jit(solution)/shard_map/ppermute | solution.py:115
  749.3 29.2 %collective-permute-start.73 = (f32[128,128]{1,0:T(8,128)S(1)}, f32[128,128]{1,0:T(8,128)S(1)}, u32[]{:S(2)}, u32[]{:S(2)}) collective-permute-start(f32[128,128]{1,0:T(8,128)S(1)} %reshape.657), channel_id=1, source_target_pairs={{0,1},{1,0},{2,3},{3,2},{4,5},{5,4},{6,7},{7,6},{8,9},{9,8},{10,11... | collective-permute-start | bytes 196616 | tf_op jit(solution)/shard_map/ppermute | solution.py:140
  774.4 22.0 %collective-permute-start.72 = (bf16[256,1536]{1,0:T(8,128)(2,1)}, bf16[256,1536]{1,0:T(8,128)(2,1)}, u32[]{:S(2)}, u32[]{:S(2)}) collective-permute-start(bf16[256,1536]{1,0:T(8,128)(2,1)} %get-tuple-element.731), channel_id=1, source_target_pairs={{3,2},{7,6},{11,10},{15,14},{19,18},{23,22},{27,26},{31,30}} | collective-permute-start | bytes 2359304 | tf_op jit(solution)/shard_map/ppermute | solution.py:83
  776.1 20.4 %collective-permute-start.71 = (bf16[256,1536]{1,0:T(8,128)(2,1)}, bf16[256,1536]{1,0:T(8,128)(2,1)}, u32[]{:S(2)}, u32[]{:S(2)}) collective-permute-start(bf16[256,1536]{1,0:T(8,128)(2,1)} %get-tuple-element.732), channel_id=1, source_target_pairs={{0,1},{4,5},{8,9},{12,13},{16,17},{20,21},{24,25},{28,29}} | collective-permute-start | bytes 2359304 | tf_op jit(solution)/shard_map/ppermute | solution.py:82
  799.5 204.2 %reduce-scatter.11.cloned.1.call-start = ((), (), s32[]{:S(2)}) async-start(), calls=%async_computation.17 | async-start | bytes 7962624 | tf_op jit(solution)/shard_map/reduce_scatter | solution.py:1138
  870.2 225.0 %reduce-scatter.13.cloned.1.call-start = ((), (), s32[]{:S(2)}) async-start(), calls=%async_computation.18 | async-start | bytes 5308416 | tf_op jit(solution)/shard_map/reduce_scatter | solution.py:1151
  876.0 22.0 %collective-permute-start.84 = (bf16[256,1536]{1,0:T(8,128)(2,1)}, bf16[256,1536]{1,0:T(8,128)(2,1)S(1)}, u32[]{:S(2)}, u32[]{:S(2)}) collective-permute-start(bf16[256,1536]{1,0:T(8,128)(2,1)} %copy-done.182), channel_id=1, source_target_pairs={{1,0},{2,1},{5,4},{6,5},{9,8},{10,9},{13,12},{14,13},{17,16},{18,1... | collective-permute-start | bytes 2359304 | tf_op jit(solution)/shard_map/ppermute | solution.py:76
  900.4 26.6 %collective-permute-start.94 = (bf16[256,1536]{1,0:T(8,128)(2,1)S(1)}, bf16[256,1536]{1,0:T(8,128)(2,1)S(1)}, u32[]{:S(2)}, u32[]{:S(2)}) collective-permute-start(bf16[256,1536]{1,0:T(8,128)(2,1)S(1)} %get-tuple-element.444), channel_id=1, source_target_pairs={{0,1},{1,2},{4,5},{5,6},{8,9},{9,10},{12,13},{13,14},{16,17},{17,1... | collective-permute-start | bytes 2359304 | tf_op jit(solution)/shard_map/ppermute | solution.py:82
  905.1 21.8 %collective-permute-start.95 = (bf16[256,1536]{1,0:T(8,128)(2,1)S(1)}, bf16[256,1536]{1,0:T(8,128)(2,1)S(1)}, u32[]{:S(2)}, u32[]{:S(2)}) collective-permute-start(bf16[256,1536]{1,0:T(8,128)(2,1)S(1)} %get-tuple-element.445), channel_id=1, source_target_pairs={{2,1},{3,2},{6,5},{7,6},{10,9},{11,10},{14,13},{15,14},{18,17},{19... | collective-permute-start | bytes 2359304 | tf_op jit(solution)/shard_map/ppermute | solution.py:83
  928.5 40.7 %collective-permute-start.96 = (bf16[256,1536]{1,0:T(8,128)(2,1)}, bf16[256,1536]{1,0:T(8,128)(2,1)}, u32[]{:S(2)}, u32[]{:S(2)}) collective-permute-start(bf16[256,1536]{1,0:T(8,128)(2,1)} %get-tuple-element.446), channel_id=1, source_target_pairs={{0,1},{1,2},{2,3},{4,5},{5,6},{6,7},{8,9},{9,10},{10,11},{12,13},{... | collective-permute-start | bytes 2359304 | tf_op jit(solution)/shard_map/ppermute | solution.py:82
  931.0 38.1 %collective-permute-start.97 = (bf16[256,1536]{1,0:T(8,128)(2,1)}, bf16[256,1536]{1,0:T(8,128)(2,1)}, u32[]{:S(2)}, u32[]{:S(2)}) collective-permute-start(bf16[256,1536]{1,0:T(8,128)(2,1)} %get-tuple-element.447), channel_id=1, source_target_pairs={{1,0},{2,1},{3,2},{5,4},{6,5},{7,6},{9,8},{10,9},{11,10},{13,12},{... | collective-permute-start | bytes 2359304 | tf_op jit(solution)/shard_map/ppermute | solution.py:83
  942.7 24.5 %collective-permute-start.93 = (bf16[144,768]{1,0:T(8,128)(2,1)S(1)}, bf16[144,768]{1,0:T(8,128)(2,1)S(1)}, u32[]{:S(2)}, u32[]{:S(2)}) collective-permute-start(bf16[144,768]{1,0:T(8,128)(2,1)S(1)} %maximum_maximum_fusion.2), channel_id=1, source_target_pairs={{24,0},{28,4},{25,1},{29,5},{26,2},{30,6},{27,3},{31,7}} | collective-permute-start | bytes 663560 | tf_op jit(solution)/shard_map/ppermute | solution.py:226
  944.0 21.1 %collective-permute-start.92 = (bf16[144,768]{1,0:T(8,128)(2,1)S(1)}, bf16[144,768]{1,0:T(8,128)(2,1)S(1)}, u32[]{:S(2)}, u32[]{:S(2)}) collective-permute-start(bf16[144,768]{1,0:T(8,128)(2,1)S(1)} %maximum_maximum_fusion.2), channel_id=1, source_target_pairs={{12,0},{16,4},{20,8},{24,12},{28,16},{13,1},{17,5},{21,9},{25,13},... | collective-permute-start | bytes 663560 | tf_op jit(solution)/shard_map/ppermute | solution.py:226
  969.1 207.6 %reduce-scatter.15.cloned.1.call-start = ((), (), s32[]{:S(2)}) async-start(), calls=%async_computation.19 | async-start | bytes 3981312 | tf_op jit(solution)/shard_map/reduce_scatter | solution.py:1188
  1017.4 22.4 %collective-permute-start.99 = (bf16[256,1536]{1,0:T(8,128)(2,1)}, bf16[256,1536]{1,0:T(8,128)(2,1)S(1)}, u32[]{:S(2)}, u32[]{:S(2)}) collective-permute-start(bf16[256,1536]{1,0:T(8,128)(2,1)} %get-tuple-element.720), channel_id=1, source_target_pairs={{0,1},{4,5},{8,9},{12,13},{16,17},{20,21},{24,25},{28,29}} | collective-permute-start | bytes 2359304 | tf_op jit(solution)/shard_map/ppermute | solution.py:82
  1041.6 21.0 %collective-permute-start.101 = (bf16[256,1536]{1,0:T(8,128)(2,1)S(1)}, bf16[256,1536]{1,0:T(8,128)(2,1)S(1)}, u32[]{:S(2)}, u32[]{:S(2)}) collective-permute-start(bf16[256,1536]{1,0:T(8,128)(2,1)S(1)} %get-tuple-element.461), channel_id=1, source_target_pairs={{0,1},{1,2},{4,5},{5,6},{8,9},{9,10},{12,13},{13,14},{16,17},{17,1... | collective-permute-start | bytes 2359304 | tf_op jit(solution)/shard_map/ppermute | solution.py:82
  1064.1 23.1 %collective-permute-start.103 = (bf16[256,1536]{1,0:T(8,128)(2,1)}, bf16[256,1536]{1,0:T(8,128)(2,1)}, u32[]{:S(2)}, u32[]{:S(2)}) collective-permute-start(bf16[256,1536]{1,0:T(8,128)(2,1)} %get-tuple-element.463), channel_id=1, source_target_pairs={{0,1},{1,2},{2,3},{4,5},{5,6},{6,7},{8,9},{9,10},{10,11},{12,13},{... | collective-permute-start | bytes 2359304 | tf_op jit(solution)/shard_map/ppermute | solution.py:82
  1071.7 20.5 %collective-permute-start.104 = (bf16[256,1536]{1,0:T(8,128)(2,1)}, bf16[256,1536]{1,0:T(8,128)(2,1)}, u32[]{:S(2)}, u32[]{:S(2)}) collective-permute-start(bf16[256,1536]{1,0:T(8,128)(2,1)} %get-tuple-element.464), channel_id=1, source_target_pairs={{1,0},{2,1},{3,2},{5,4},{6,5},{7,6},{9,8},{10,9},{11,10},{13,12},{... | collective-permute-start | bytes 2359304 | tf_op jit(solution)/shard_map/ppermute | solution.py:83
  1073.1 325.0 %reduce-scatter.17.cloned.1.call-start = ((), (), s32[]{:S(2)}) async-start(), calls=%async_computation.20 | async-start | bytes 15925248 | tf_op jit(solution)/shard_map/reduce_scatter | solution.py:1105
  1120.9 20.9 %collective-permute-start.108 = (bf16[256,1536]{1,0:T(8,128)(2,1)S(1)}, bf16[256,1536]{1,0:T(8,128)(2,1)S(1)}, u32[]{:S(2)}, u32[]{:S(2)}) collective-permute-start(bf16[256,1536]{1,0:T(8,128)(2,1)S(1)} %collective-permute-done.106), channel_id=1, source_target_pairs={{1,0},{2,1},{5,4},{6,5},{9,8},{10,9},{13,12},{14,13},{17,16},{18,1... | collective-permute-start | bytes 2359304 | tf_op jit(solution)/shard_map/ppermute | solution.py:115
  1176.7 31.2 %collective-permute-start.113 = (f32[128,128]{1,0:T(8,128)S(1)}, f32[128,128]{1,0:T(8,128)S(1)}, u32[]{:S(2)}, u32[]{:S(2)}) collective-permute-start(f32[128,128]{1,0:T(8,128)S(1)} %reshape.664), channel_id=1, source_target_pairs={{0,1},{1,0},{2,3},{3,2},{4,5},{5,4},{6,7},{7,6},{8,9},{9,8},{10,11... | collective-permute-start | bytes 196616 | tf_op jit(solution)/shard_map/ppermute | solution.py:140
  1200.2 25.6 %collective-permute-start.112 = (bf16[256,1536]{1,0:T(8,128)(2,1)}, bf16[256,1536]{1,0:T(8,128)(2,1)}, u32[]{:S(2)}, u32[]{:S(2)}) collective-permute-start(bf16[256,1536]{1,0:T(8,128)(2,1)} %get-tuple-element.713), channel_id=1, source_target_pairs={{3,2},{7,6},{11,10},{15,14},{19,18},{23,22},{27,26},{31,30}} | collective-permute-start | bytes 2359304 | tf_op jit(solution)/shard_map/ppermute | solution.py:83
  1201.9 23.9 %collective-permute-start.111 = (bf16[256,1536]{1,0:T(8,128)(2,1)}, bf16[256,1536]{1,0:T(8,128)(2,1)}, u32[]{:S(2)}, u32[]{:S(2)}) collective-permute-start(bf16[256,1536]{1,0:T(8,128)(2,1)} %get-tuple-element.714), channel_id=1, source_target_pairs={{0,1},{4,5},{8,9},{12,13},{16,17},{20,21},{24,25},{28,29}} | collective-permute-start | bytes 2359304 | tf_op jit(solution)/shard_map/ppermute | solution.py:82
  1229.2 219.6 %reduce-scatter.19.cloned.1.call-start = ((), (), s32[]{:S(2)}) async-start(), calls=%async_computation.21 | async-start | bytes 7962624 | tf_op jit(solution)/shard_map/reduce_scatter | solution.py:1138
  1229.3 23.3 %collective-permute-start.115 = (bf16[256,1536]{1,0:T(8,128)(2,1)}, bf16[256,1536]{1,0:T(8,128)(2,1)}, u32[]{:S(2)}, u32[]{:S(2)}) collective-permute-start(bf16[256,1536]{1,0:T(8,128)(2,1)} %get-tuple-element.492), channel_id=1, source_target_pairs={{0,1},{1,2},{4,5},{5,6},{8,9},{9,10},{12,13},{13,14},{16,17},{17,1... | collective-permute-start | bytes 2359304 | tf_op jit(solution)/shard_map/ppermute | solution.py:82
  1231.6 21.0 %collective-permute-start.116 = (bf16[256,1536]{1,0:T(8,128)(2,1)}, bf16[256,1536]{1,0:T(8,128)(2,1)}, u32[]{:S(2)}, u32[]{:S(2)}) collective-permute-start(bf16[256,1536]{1,0:T(8,128)(2,1)} %get-tuple-element.493), channel_id=1, source_target_pairs={{2,1},{3,2},{6,5},{7,6},{10,9},{11,10},{14,13},{15,14},{18,17},{19... | collective-permute-start | bytes 2359304 | tf_op jit(solution)/shard_map/ppermute | solution.py:83
  1256.1 31.7 %collective-permute-start.117 = (bf16[256,1536]{1,0:T(8,128)(2,1)}, bf16[256,1536]{1,0:T(8,128)(2,1)}, u32[]{:S(2)}, u32[]{:S(2)}) collective-permute-start(bf16[256,1536]{1,0:T(8,128)(2,1)} %get-tuple-element.494), channel_id=1, source_target_pairs={{0,1},{1,2},{2,3},{4,5},{5,6},{6,7},{8,9},{9,10},{10,11},{12,13},{... | collective-permute-start | bytes 2359304 | tf_op jit(solution)/shard_map/ppermute | solution.py:82
  1262.3 25.6 %collective-permute-start.118 = (bf16[256,1536]{1,0:T(8,128)(2,1)}, bf16[256,1536]{1,0:T(8,128)(2,1)}, u32[]{:S(2)}, u32[]{:S(2)}) collective-permute-start(bf16[256,1536]{1,0:T(8,128)(2,1)} %get-tuple-element.495), channel_id=1, source_target_pairs={{1,0},{2,1},{3,2},{5,4},{6,5},{7,6},{9,8},{10,9},{11,10},{13,12},{... | collective-permute-start | bytes 2359304 | tf_op jit(solution)/shard_map/ppermute | solution.py:83
  1308.0 177.6 %reduce-scatter.21.cloned.1.call-start = ((), (), s32[]{:S(2)}) async-start(), calls=%async_computation.22 | async-start | bytes 5308416 | tf_op jit(solution)/shard_map/reduce_scatter | solution.py:1151
  1308.9 27.3 %collective-permute-start.127 = (bf16[256,1536]{1,0:T(8,128)(2,1)}, bf16[256,1536]{1,0:T(8,128)(2,1)S(1)}, u32[]{:S(2)}, u32[]{:S(2)}) collective-permute-start(bf16[256,1536]{1,0:T(8,128)(2,1)} %collective-permute-done.120), channel_id=1, source_target_pairs={{1,0},{2,1},{5,4},{6,5},{9,8},{10,9},{13,12},{14,13},{17,16},{18,1... | collective-permute-start | bytes 2359304 | tf_op jit(solution)/shard_map/ppermute | solution.py:76
  1398.2 179.1 %reduce-scatter.23.cloned.1.call-start = ((), (), s32[]{:S(2)}) async-start(), calls=%async_computation.23 | async-start | bytes 3981312 | tf_op jit(solution)/shard_map/reduce_scatter | solution.py:1188
  1486.6 21.6 %collective-permute-start.140 = (bf16[256,1536]{1,0:T(8,128)(2,1)}, bf16[256,1536]{1,0:T(8,128)(2,1)}, u32[]{:S(2)}, u32[]{:S(2)}) collective-permute-start(bf16[256,1536]{1,0:T(8,128)(2,1)} %get-tuple-element.527), channel_id=1, source_target_pairs={{0,1},{1,2},{4,5},{5,6},{8,9},{9,10},{12,13},{13,14},{16,17},{17,1... | collective-permute-start | bytes 2359304 | tf_op jit(solution)/shard_map/ppermute | solution.py:82
  1511.2 38.6 %collective-permute-start.146 = (f32[16,768]{1,0:T(8,128)S(1)}, f32[16,768]{1,0:T(8,128)}, u32[]{:S(2)}, u32[]{:S(2)}) collective-permute-start(f32[16,768]{1,0:T(8,128)S(1)} %constant_dynamic-update-slice_fusion), channel_id=1, source_target_pairs={{0,4},{4,0},{8,12},{12,8},{16,20},{20,16},{24,28},{28,24},{1,5},{5... | collective-permute-start | bytes 147464 | tf_op jit(solution)/shard_map/ppermute | solution.py:140
  1512.8 53.4 %collective-permute-start.142 = (bf16[256,1536]{1,0:T(8,128)(2,1)}, bf16[256,1536]{1,0:T(8,128)(2,1)}, u32[]{:S(2)}, u32[]{:S(2)}) collective-permute-start(bf16[256,1536]{1,0:T(8,128)(2,1)} %get-tuple-element.533), channel_id=1, source_target_pairs={{0,1},{1,2},{2,3},{4,5},{5,6},{6,7},{8,9},{9,10},{10,11},{12,13},{... | collective-permute-start | bytes 2359304 | tf_op jit(solution)/shard_map/ppermute | solution.py:82
  1549.8 20.5 %collective-permute-start.143 = (bf16[256,1536]{1,0:T(8,128)(2,1)}, bf16[256,1536]{1,0:T(8,128)(2,1)S(1)}, u32[]{:S(2)}, u32[]{:S(2)}) collective-permute-start(bf16[256,1536]{1,0:T(8,128)(2,1)} %get-tuple-element.534), channel_id=1, source_target_pairs={{1,0},{2,1},{3,2},{5,4},{6,5},{7,6},{9,8},{10,9},{11,10},{13,12},{... | collective-permute-start | bytes 2359304 | tf_op jit(solution)/shard_map/ppermute | solution.py:83
  (382 other events, 6302.2 us)
Sparse Core Ops, SparseCore 0:
  51.2 46.7 all-gather.8
  100.4 29.2 all-gather.10
  166.0 80.9 all-gather.12
  249.3 48.8 all-gather.14
  347.9 60.0 all-gather.16
  471.6 42.3 all-gather.18
  553.0 77.9 all-gather.22
  632.9 48.8 all-gather.20
  799.6 111.7 reduce-scatter.8
  914.7 75.1 reduce-scatter.10
  993.8 53.9 reduce-scatter.12
  1073.2 47.5 reduce-scatter.14
  1229.3 103.5 reduce-scatter.16
  1336.3 77.7 reduce-scatter.18
  1418.4 54.1 reduce-scatter.20
  1486.0 49.9 reduce-scatter.22
